TPU v7x, 32 devices: a whole 2x2x4 slice. The times are simulated.
32 devices in a mesh: gx: 8 (over z, y), gy: 4 (over x, core).
Axes of the slice: x: 2, y: 2, z: 4, core: 2. Of those that a mesh axis runs over, the one named last changes fastest.
Arguments:
- adjoint_in: float32 [57, 4, 64, 512], P(None, None, 'gx', 'gy'), may hold values from -6 to 6
- populations_early: bfloat16 [57, 4, 64, 512], P(None, None, 'gx', 'gy'), may hold values from 0.019897461 to 0.099609375
- populations_late: bfloat16 [57, 4, 64, 512], P(None, None, 'gx', 'gy'), may hold values from 0.019897461 to 0.099609375
- dipoles_early: bfloat16 [3, 4, 64, 512], P(None, None, 'gx', 'gy'), may hold values from -4 to 4
- dipoles_late: bfloat16 [3, 4, 64, 512], P(None, None, 'gx', 'gy'), may hold values from -4 to 4
Outputs:
- adjoint_out: float32 [57, 4, 64, 512], P(None, None, 'gx', 'gy')
All inputs are finite; a program needn't handle non-finite values.
Results may differ from a plain program's by a relative error of at most 0.0003.
Values sent between devices are 32-bit elements; how exact they have to be, the bound alone decides.
No kernel may reach another device: no remote copies, remote signals or barrier semaphores. Data moves between devices by JAX's collectives and lax.ppermute only.
A program may use at most 128 MiB of HBM per device.

v0:
```python
import jax
import jax.numpy as jnp
from jax import lax
from jax.sharding import PartitionSpec as P

VELOCITY = (
    (1, 0, 0),
    (-1, 0, 0),
    (0, 1, 0),
    (0, -1, 0),
    (1, 1, 0),
    (-1, -1, 0),
    (1, -1, 0),
    (-1, 1, 0),
    (1, 0, 1),
    (-1, 0, -1),
    (1, 0, -1),
    (-1, 0, 1),
    (0, 1, 1),
    (0, -1, -1),
    (0, 1, -1),
    (0, -1, 1),
    (0, 0, 0),
    (0, 0, 1),
    (0, 0, -1),
)
WEIGHT = (1.0 / 18.0,) * 4 + (1.0 / 36.0,) * 12 + (1.0 / 3.0, 1.0 / 18.0, 1.0 / 18.0)
RELAXATION = (1.0, 1.0, 1.25)
COUPLING = ((0.0, 1.2, -0.6), (1.2, 0.0, -0.6), (-0.6, -0.6, -0.3))
DIPOLE_COUPLING = 0.5
CHARGE = (1.0, -1.0)
FORWARD_X = (0, 4, 6, 8, 10)
BACKWARD_X = (1, 5, 7, 9, 11)
FORWARD_Y = (2, 4, 7, 12, 14)
BACKWARD_Y = (3, 5, 6, 13, 15)


def passed_along(block, axis, distance):
    devices = range(lax.axis_size(axis))
    route = [((i - distance) % len(devices), i) for i in devices]
    return lax.ppermute(block, axis, route)


def with_halo(x, sides, width):
    for axis, dim in sides:
        size, length = (lax.axis_size(axis), x.shape[dim])
        up = [(i, (i + 1) % size) for i in range(size)]
        down = [(j, i) for i, j in up]
        last = lax.slice_in_dim(x, length - width, length, axis=dim)
        leading = lax.slice_in_dim(x, 0, width, axis=dim)
        before = lax.ppermute(last, axis, up)
        after = lax.ppermute(leading, axis, down)
        x = jnp.concatenate([before, x, after], axis=dim)
    return x


def neighbour(padded, shift_x, shift_y, shift_z):
    row_count = padded.shape[2] - 2
    col_count = padded.shape[3] - 2
    window = padded[
        :, :, 1 + shift_x : 1 + shift_x + row_count, 1 + shift_y : 1 + shift_y + col_count
    ]
    return jnp.roll(window, -shift_z, axis=1)


def stencils(field_pad):
    shape = (field_pad.shape[1], field_pad.shape[2] - 2, field_pad.shape[3] - 2)
    sums = [jnp.zeros(shape, jnp.float32)] * 21
    for q in range(19):
        if q == 16:
            continue
        c = VELOCITY[q]
        weight = WEIGHT[q]
        nearby = neighbour(field_pad, c[0], c[1], c[2])
        projected = c[0] * nearby[3] + c[1] * nearby[4] + c[2] * nearby[5]
        contrast = nearby[0] - nearby[1]
        for d in range(3):
            if c[d] == 0:
                continue
            for s in range(3):
                sums[3 * s + d] = sums[3 * s + d] + weight * c[d] * nearby[s]
            sums[9 + d] = sums[9 + d] + weight * c[d] * projected * nearby[2]
            for j in range(3):
                if c[j] != 0:
                    sums[12 + 3 * d + j] = sums[12 + 3 * d + j] + weight * c[d] * c[j] * contrast
    return jnp.stack(sums)


def forces(potential, dipole, coupled):
    pieces = []
    for s in range(3):
        for d in range(3):
            mixture = (
                COUPLING[s][0] * coupled[d]
                + COUPLING[s][1] * coupled[3 + d]
                + COUPLING[s][2] * coupled[6 + d]
            )
            amount = -potential[s] * mixture
            if s < 2:
                amount = amount - 2.0 * DIPOLE_COUPLING * CHARGE[s] * potential[s] * coupled[9 + d]
            else:
                turned = (
                    coupled[12 + 3 * d] * dipole[0]
                    + coupled[13 + 3 * d] * dipole[1]
                    + coupled[14 + 3 * d] * dipole[2]
                )
                amount = amount + 2.0 * DIPOLE_COUPLING * potential[2] * turned
            pieces.append(amount)
    return jnp.stack(pieces)


def collide(populations, forcing):
    shaped = populations.reshape((3, 19) + populations.shape[1:])
    density = jnp.sum(shaped, axis=1)
    density_sum = jnp.sum(density, axis=0)
    flows = jnp.sum(shaped, axis=0)
    momentum = []
    for d in range(3):
        amount = jnp.zeros_like(density_sum)
        for q in range(19):
            if VELOCITY[q][d] != 0:
                amount = amount + VELOCITY[q][d] * flows[q]
        momentum.append(amount / density_sum)
    collided = []
    for s in range(3):
        drifts = [momentum[d] + RELAXATION[s] * forcing[3 * s + d] / density[s] for d in range(3)]
        square = drifts[0] * drifts[0] + drifts[1] * drifts[1] + drifts[2] * drifts[2]
        for q in range(19):
            c = VELOCITY[q]
            projected = c[0] * drifts[0] + c[1] * drifts[1] + c[2] * drifts[2]
            equilibrium = (
                WEIGHT[q]
                * density[s]
                * (1.0 + 3.0 * projected + 4.5 * projected * projected - 1.5 * square)
            )
            collided.append(shaped[s, q] - (shaped[s, q] - equilibrium) / RELAXATION[s])
    return jnp.stack(collided)


def spread_back(cot_pad, dipole):
    returned = [jnp.zeros(dipole.shape[1:], jnp.float32)] * 3
    for q in range(19):
        if q == 16:
            continue
        c = VELOCITY[q]
        weight = WEIGHT[q]
        nearby = neighbour(cot_pad, -c[0], -c[1], -c[2])
        projected = c[0] * dipole[0] + c[1] * dipole[1] + c[2] * dipole[2]
        tensor = jnp.zeros(dipole.shape[1:], jnp.float32)
        for d in range(3):
            if c[d] == 0:
                continue
            for s in range(3):
                returned[s] = returned[s] + weight * c[d] * nearby[3 * s + d]
            returned[2] = returned[2] + weight * c[d] * projected * nearby[9 + d]
            for j in range(3):
                if c[j] != 0:
                    tensor = tensor + c[d] * c[j] * nearby[12 + 3 * d + j]
        returned[0] = returned[0] + weight * tensor
        returned[1] = returned[1] - weight * tensor
    return jnp.stack(returned)


def saved_field(saved_pops, dipole):
    populations = saved_pops.astype(jnp.float32)
    density = jnp.sum(populations.reshape((3, 19) + populations.shape[1:]), axis=1)
    return jnp.concatenate([1.0 - jnp.exp(-density), dipole.astype(jnp.float32)], axis=0)


def pull_moving(padded, resting):
    pulled = []
    for s in range(3):
        for q in range(19):
            c = VELOCITY[q]
            if q < 16:
                pulled.append(neighbour(padded[s * 16 + q : s * 16 + q + 1], c[0], c[1], c[2])[0])
            else:
                pulled.append(jnp.roll(resting[s * 3 + q - 16], -c[2], axis=0))
    return jnp.stack(pulled)


def place_rims(received, chosen, empty):
    placed = []
    for q in range(16):
        if q in chosen:
            placed.append(received[:, chosen.index(q)])
        else:
            placed.append(empty)
    return jnp.stack(placed, axis=1)


def directional_pad(moving):
    ahead_rows = jnp.stack([moving[:, q, :, :1, :] for q in FORWARD_X], axis=1)
    behind_rows = jnp.stack([moving[:, q, :, -1:, :] for q in BACKWARD_X], axis=1)
    from_next = passed_along(ahead_rows, "gx", -1)
    from_prior = passed_along(behind_rows, "gx", 1)
    row_empty = jnp.zeros_like(moving[:, 0, :, :1, :])
    low_rows = place_rims(from_prior, BACKWARD_X, row_empty)
    high_rows = place_rims(from_next, FORWARD_X, row_empty)
    widened = jnp.concatenate([low_rows, moving, high_rows], axis=3)
    ahead_cols = jnp.stack([widened[:, q, :, :, :1] for q in FORWARD_Y], axis=1)
    behind_cols = jnp.stack([widened[:, q, :, :, -1:] for q in BACKWARD_Y], axis=1)
    col_next = passed_along(ahead_cols, "gy", -1)
    col_prior = passed_along(behind_cols, "gy", 1)
    col_empty = jnp.zeros_like(widened[:, 0, :, :, :1])
    low_cols = place_rims(col_prior, BACKWARD_Y, col_empty)
    high_cols = place_rims(col_next, FORWARD_Y, col_empty)
    padded = jnp.concatenate([low_cols, widened, high_cols], axis=4)
    return padded.reshape((48,) + padded.shape[2:])


def local_adjoint(populations, potential, dipole, coupled, stream):

    def forward(population_arg, potential_arg, coupled_arg):
        return collide(population_arg, forces(potential_arg, dipole, coupled_arg))

    unused, pullback = jax.vjp(forward, populations, potential, coupled)
    return pullback(stream)


def combine(grad_pops, grad_potential, potential):
    grad_density = grad_potential * (1.0 - potential)
    shaped = grad_pops.reshape((3, 19) + grad_pops.shape[1:])
    return (shaped + grad_density[:, None]).reshape(grad_pops.shape)


def reverse_step(adjoint, saved_pops, field_pad):
    populations = saved_pops.astype(jnp.float32)
    shaped = adjoint.reshape((3, 19) + adjoint.shape[1:])
    resting = shaped[:, 16:].reshape((9,) + adjoint.shape[1:])
    padded = directional_pad(shaped[:, :16])
    stream = pull_moving(padded, resting)
    potential = field_pad[:3, :, 1:-1, 1:-1]
    dipole = field_pad[3:, :, 1:-1, 1:-1]
    coupled = stencils(field_pad)
    grad_pops, grad_potential, grad_coupled = local_adjoint(
        populations, potential, dipole, coupled, stream
    )
    cot_pad = with_halo(grad_coupled, (("gx", 2), ("gy", 3)), 1)
    total_potential = grad_potential + spread_back(cot_pad, dipole)
    return combine(grad_pops, total_potential, potential)


def shards(adjoint_in, populations_early, populations_late, dipoles_early, dipoles_late):
    saved_steps = ((populations_late, dipoles_late), (populations_early, dipoles_early))
    adjoint = adjoint_in
    for number in range(2):
        saved_pops, dipole_saved = saved_steps[number]
        field_pad = with_halo(saved_field(saved_pops, dipole_saved), (("gx", 2), ("gy", 3)), 1)
        adjoint = reverse_step(adjoint, saved_pops, field_pad)
    return adjoint


def solution(mesh):
    placed = (
        P(None, None, "gx", "gy"),
        P(None, None, "gx", "gy"),
        P(None, None, "gx", "gy"),
        P(None, None, "gx", "gy"),
        P(None, None, "gx", "gy"),
    )
    return jax.shard_map(
        shards, mesh=mesh, in_specs=placed, out_specs=P(None, None, "gx", "gy"), check_vma=False
    )
```

profile of v0, /device:TPU:0, one launch (start us, length us, event | category | flops | bytes accessed | tf_op | source)
XLA Modules:
  0.0 204.4 jit_solution(11020028722836555230)
XLA Ops:
  4.4 3.0 %collective-permute-start = (f32[3,5,4,1,128]{4,3,2,1,0:T(1,128)S(1)}, f32[3,5,4,1,128]{4,3,2,1,0:T(1,128)S(1)}, u32[]{:S(2)}, u32[]{:S(2)}) collective-permute-start(f32[3,5,4,1,128]{4,3,2,1,0:T(1,128)S(1)} %get-tuple-element.623), channel_id=1, source_target_pairs={{28,0},{0,4},{4,8},{8,12},{12,16},{16,20},{20,24},{24,28},{29,1},{... | collective-permute-start | bytes 92168 | tf_op jit(solution)/shard_map/ppermute | solution.py:41
  7.4 3.1 %collective-permute-start.1 = (f32[3,5,4,1,128]{4,3,2,1,0:T(1,128)S(1)}, f32[3,5,4,1,128]{4,3,2,1,0:T(1,128)S(1)}, u32[]{:S(2)}, u32[]{:S(2)}) collective-permute-start(f32[3,5,4,1,128]{4,3,2,1,0:T(1,128)S(1)} %get-tuple-element.624), channel_id=1, source_target_pairs={{4,0},{8,4},{12,8},{16,12},{20,16},{24,20},{28,24},{0,28},{5,1},{9... | collective-permute-start | bytes 92168 | tf_op jit(solution)/shard_map/ppermute | solution.py:41
  12.5 2.0 collective-permute-start.4
  15.4 4.7 %collective-permute-start.16 = (f32[6,4,1,128]{3,2,1,0:T(1,128)S(1)}, f32[6,4,1,128]{3,2,1,0:T(1,128)S(1)}, u32[]{:S(2)}, u32[]{:S(2)}) collective-permute-start(f32[6,4,1,128]{3,2,1,0:T(1,128)S(1)} %get-tuple-element.953), channel_id=1, source_target_pairs={{4,0},{8,4},{12,8},{16,12},{20,16},{24,20},{28,24},{0,28},{5,1},{9... | collective-permute-start | bytes 36872 | tf_op jit(solution)/shard_map/ppermute | solution.py:52
  28.9 6.2 %collective-permute-done.17 = f32[6,4,1,128]{3,2,1,0:T(1,128)S(1)} collective-permute-done((f32[6,4,1,128]{3,2,1,0:T(1,128)S(1)}, f32[6,4,1,128]{3,2,1,0:T(1,128)S(1)}, u32[]{:S(2)}, u32[]{:S(2)}) %collective-permute-start.17) | collective-permute-done | bytes 12320 | tf_op jit(solution)/shard_map/ppermute | solution.py:51
  39.5 1.7 collective-permute-done.6
  41.1 3.0 %collective-permute-start.19 = (f32[6,4,10,1]{3,2,1,0:T(8,128)S(1)}, f32[6,4,10,1]{3,2,1,0:T(8,128)S(1)}, u32[]{:S(2)}, u32[]{:S(2)}) collective-permute-start(f32[6,4,10,1]{3,2,1,0:T(8,128)S(1)} %get-tuple-element.761), channel_id=1, source_target_pairs={{0,1},{1,2},{2,3},{3,0},{4,5},{5,6},{6,7},{7,4},{8,9},{9,10},{10,1... | collective-permute-start | bytes 2888 | tf_op jit(solution)/shard_map/ppermute | solution.py:51
  44.6 3.7 %collective-permute-done.19 = f32[6,4,10,1]{3,2,1,0:T(8,128)S(1)} collective-permute-done((f32[6,4,10,1]{3,2,1,0:T(8,128)S(1)}, f32[6,4,10,1]{3,2,1,0:T(8,128)S(1)}, u32[]{:S(2)}, u32[]{:S(2)}) %collective-permute-start.19) | collective-permute-done | bytes 992 | tf_op jit(solution)/shard_map/ppermute | solution.py:51
  53.3 1.8 collective-permute-start.3
  55.1 10.2 %collective-permute-done.2 = f32[3,5,4,10,1]{4,3,2,1,0:T(8,128)S(1)} collective-permute-done((f32[3,5,4,10,1]{4,3,2,1,0:T(8,128)S(1)}, f32[3,5,4,10,1]{4,3,2,1,0:T(8,128)S(1)}, u32[]{:S(2)}, u32[]{:S(2)}) %collective-permute-start.2) | collective-permute-done | bytes 2432 | tf_op jit(solution)/shard_map/ppermute | solution.py:41
  65.7 2.1 %pad_maximum_fusion = f32[3,16,4,10,130]{4,3,2,1,0:T(8,128)S(1)} fusion(f32[3,16,4,10,1]{4,3,2,1,0:T(8,128)S(1)} %constant_dynamic-update-slice_fusion.49, f32[3,16,4,1,128]{4,3,2,1,0:T(1,128)S(1)} %constant_dynamic-update-slice_fusion.22, f32[3,16,4,8,128]{4,3,2,1,0:T(8,128)S(1)} %slice.5296, f32[3,16,4,1,128]{4,3,2,1,0:T(1,128)S(1)} %constant_dynamic-update-slice_fusion.5, ...), kind=kLoop, calls=%fused_computation | loop fusion | flops 998400 | bytes 1996800 | tf_op jit(solution)/shard_map/concatenate | solution.py:208
  68.2 2.4 %broadcast_multiply_fusion.58 = (f32[1,4,8,128]{3,2,1,0:T(8,128)S(1)}, f32[1,4,8,128]{3,2,1,0:T(8,128)S(1)}, f32[1,4,8,128]{3,2,1,0:T(8,128)S(1)}, f32[1,4,8,128...) fusion(f32[4,8,128]{2,1,0:T(8,128)S(1)} %convert_reduce_fusion., ...), kind=kLoop, calls=%fused_computation.4019 | loop fusion | flops 6303744 | bytes 5447680 | tf_op jit(solution)/shard_map/transpose(jvp())/mul | solution.py:122
  91.2 4.7 %collective-permute-start.9 = (f32[21,4,1,128]{3,2,1,0:T(1,128)S(1)}, f32[21,4,1,128]{3,2,1,0:T(1,128)S(1)}, u32[]{:S(2)}, u32[]{:S(2)}) collective-permute-start(f32[21,4,1,128]{3,2,1,0:T(1,128)S(1)} %get-tuple-element.678), channel_id=1, source_target_pairs={{4,0},{8,4},{12,8},{16,12},{20,16},{24,20},{28,24},{0,28},{5,1},{9... | collective-permute-start | bytes 129032 | tf_op jit(solution)/shard_map/ppermute | solution.py:52
  105.7 1.6 copy.2773
  107.3 1.8 maximum_maximum_fusion
  113.3 3.0 %add_add_fusion.1 = f32[3,19,4,8,128]{4,3,2,1,0:T(8,128)S(1)} fusion(f32[1,1,4,8,128]{4,3,2,1,0:T(8,128)} %get-tuple-element.501, f32[1,1,4,8,128]{4,3,2,1,0:T(8,128)S(1)} %copy-done.98, f32[1,1,4,8,128]{4,3,2,1,0:T(8,128)} %get-tuple-element.502, f32[1,1,4,8,128]{4,3,2,1,0:T(8,128)S(1)} %copy-done.99, f32[1,1,4,8,128]{4,3,2,1,0:T(8,128)S(1)} %copy-done.79, ...), kind=kLoop, calls=%fused_computation.53 | loop fusion | flops 27082752 | bytes 3211264 | tf_op jit(solution)/shard_map/add | solution.py:224
  117.1 4.7 %collective-permute-start.13 = (f32[3,5,4,1,128]{4,3,2,1,0:T(1,128)S(1)}, f32[3,5,4,1,128]{4,3,2,1,0:T(1,128)S(1)}, u32[]{:S(2)}, u32[]{:S(2)}) collective-permute-start(f32[3,5,4,1,128]{4,3,2,1,0:T(1,128)S(1)} %get-tuple-element.614), channel_id=1, source_target_pairs={{4,0},{8,4},{12,8},{16,12},{20,16},{24,20},{28,24},{0,28},{5,1},{9... | collective-permute-start | bytes 92168 | tf_op jit(solution)/shard_map/ppermute | solution.py:41
  130.4 2.0 collective-permute-start.15
  132.4 9.8 %collective-permute-done.14 = f32[3,5,4,10,1]{4,3,2,1,0:T(8,128)S(1)} collective-permute-done((f32[3,5,4,10,1]{4,3,2,1,0:T(8,128)S(1)}, f32[3,5,4,10,1]{4,3,2,1,0:T(8,128)S(1)}, u32[]{:S(2)}, u32[]{:S(2)}) %collective-permute-start.14) | collective-permute-done | bytes 2432 | tf_op jit(solution)/shard_map/ppermute | solution.py:41
  142.9 2.1 %pad_maximum_fusion.1 = f32[3,16,4,10,130]{4,3,2,1,0:T(8,128)S(1)} fusion(f32[3,16,4,10,1]{4,3,2,1,0:T(8,128)S(1)} %constant_dynamic-update-slice_fusion.109, f32[3,16,4,1,128]{4,3,2,1,0:T(1,128)S(1)} %constant_dynamic-update-slice_fusion.82, f32[3,16,4,8,128]{4,3,2,1,0:T(8,128)S(1)} %slice.5580, ...), kind=kLoop, calls=%fused_computation.1 | loop fusion | flops 998400 | bytes 1996800 | tf_op jit(solution)/shard_map/concatenate | solution.py:208
  145.7 2.5 %broadcast_multiply_fusion.59 = (f32[1,4,8,128]{3,2,1,0:T(8,128)S(1)}, f32[1,4,8,128]{3,2,1,0:T(8,128)S(1)}, f32[1,4,8,128]{3,2,1,0:T(8,128)S(1)}, f32[1,4,8,128...) fusion(f32[4,8,128]{2,1,0:T(8,128)S(1)} %convert_reduce_fusion,, ...), kind=kLoop, calls=%fused_computation.4020 | loop fusion | flops 6303744 | bytes 5447680 | tf_op jit(solution)/shard_map/transpose(jvp())/mul | solution.py:122
  179.4 4.7 %collective-permute-start.21 = (f32[21,4,1,128]{3,2,1,0:T(1,128)S(1)}, f32[21,4,1,128]{3,2,1,0:T(1,128)S(1)}, u32[]{:S(2)}, u32[]{:S(2)}) collective-permute-start(f32[21,4,1,128]{3,2,1,0:T(1,128)S(1)} %get-tuple-element.669), channel_id=1, source_target_pairs={{4,0},{8,4},{12,8},{16,12},{20,16},{24,20},{28,24},{0,28},{5,1},{9... | collective-permute-start | bytes 129032 | tf_op jit(solution)/shard_map/ppermute | solution.py:52
  193.7 1.5 copy.2777
  200.3 3.9 %add_add_fusion = f32[3,19,4,8,128]{4,3,2,1,0:T(8,128)} fusion(f32[1,1,4,8,128]{4,3,2,1,0:T(8,128)} %get-tuple-element.405, f32[1,1,4,8,128]{4,3,2,1,0:T(8,128)S(1)} %copy-done.118, f32[1,1,4,8,128]{4,3,2,1,0:T(8,128)} %get-tuple-element.406, f32[1,1,4,8,128]{4,3,2,1,0:T(8,128)S(1)} %copy-done.119, f32[1,1,4,8,128]{4,3,2,1,0:T(8,128)S(1)} %copy-done.73, ...), kind=kLoop, calls=%fused_computation.52 | loop fusion | flops 27082752 | bytes 3211264 | tf_op jit(solution)/shard_map/add | solution.py:224
  (662 shorter events, 114.4 us)
Async XLA Ops:
  4.4 47.8 %collective-permute-start = (f32[3,5,4,1,128]{4,3,2,1,0:T(1,128)S(1)}, f32[3,5,4,1,128]{4,3,2,1,0:T(1,128)S(1)}, u32[]{:S(2)}, u32[]{:S(2)}) collective-permute-start(f32[3,5,4,1,128]{4,3,2,1,0:T(1,128)S(1)} %get-tuple-element.623), channel_id=1, source_target_pairs={{28,0},{0,4},{4,8},{8,12},{12,16},{16,20},{20,24},{24,28},{29,1},{... | collective-permute-start | bytes 92168 | tf_op jit(solution)/shard_map/ppermute | solution.py:41
  7.4 44.9 %collective-permute-start.1 = (f32[3,5,4,1,128]{4,3,2,1,0:T(1,128)S(1)}, f32[3,5,4,1,128]{4,3,2,1,0:T(1,128)S(1)}, u32[]{:S(2)}, u32[]{:S(2)}) collective-permute-start(f32[3,5,4,1,128]{4,3,2,1,0:T(1,128)S(1)} %get-tuple-element.624), channel_id=1, source_target_pairs={{4,0},{8,4},{12,8},{16,12},{20,16},{24,20},{28,24},{0,28},{5,1},{9... | collective-permute-start | bytes 92168 | tf_op jit(solution)/shard_map/ppermute | solution.py:41
  12.5 16.2 %collective-permute-start.4 = (f32[6,4,1,128]{3,2,1,0:T(1,128)S(1)}, f32[6,4,1,128]{3,2,1,0:T(1,128)S(1)}, u32[]{:S(2)}, u32[]{:S(2)}) collective-permute-start(f32[6,4,1,128]{3,2,1,0:T(1,128)S(1)} %get-tuple-element.960), channel_id=1, source_target_pairs={{4,0},{8,4},{12,8},{16,12},{20,16},{24,20},{28,24},{0,28},{5,1},{9... | collective-permute-start | bytes 36872 | tf_op jit(solution)/shard_map/ppermute | solution.py:52
  14.5 14.3 %collective-permute-start.5 = (f32[6,4,1,128]{3,2,1,0:T(1,128)S(1)}, f32[6,4,1,128]{3,2,1,0:T(1,128)S(1)}, u32[]{:S(2)}, u32[]{:S(2)}) collective-permute-start(f32[6,4,1,128]{3,2,1,0:T(1,128)S(1)} %get-tuple-element.959), channel_id=1, source_target_pairs={{0,4},{4,8},{8,12},{12,16},{16,20},{20,24},{24,28},{28,0},{1,5},{5... | collective-permute-start | bytes 36872 | tf_op jit(solution)/shard_map/ppermute | solution.py:51
  15.4 13.6 %collective-permute-start.16 = (f32[6,4,1,128]{3,2,1,0:T(1,128)S(1)}, f32[6,4,1,128]{3,2,1,0:T(1,128)S(1)}, u32[]{:S(2)}, u32[]{:S(2)}) collective-permute-start(f32[6,4,1,128]{3,2,1,0:T(1,128)S(1)} %get-tuple-element.953), channel_id=1, source_target_pairs={{4,0},{8,4},{12,8},{16,12},{20,16},{24,20},{28,24},{0,28},{5,1},{9... | collective-permute-start | bytes 36872 | tf_op jit(solution)/shard_map/ppermute | solution.py:52
  28.7 6.4 %collective-permute-start.17 = (f32[6,4,1,128]{3,2,1,0:T(1,128)S(1)}, f32[6,4,1,128]{3,2,1,0:T(1,128)S(1)}, u32[]{:S(2)}, u32[]{:S(2)}) collective-permute-start(f32[6,4,1,128]{3,2,1,0:T(1,128)S(1)} %get-tuple-element.952), channel_id=1, source_target_pairs={{0,4},{4,8},{8,12},{12,16},{16,20},{20,24},{24,28},{28,0},{1,5},{5... | collective-permute-start | bytes 36872 | tf_op jit(solution)/shard_map/ppermute | solution.py:51
  36.8 4.4 %collective-permute-start.6 = (f32[6,4,10,1]{3,2,1,0:T(8,128)S(1)}, f32[6,4,10,1]{3,2,1,0:T(8,128)S(1)}, u32[]{:S(2)}, u32[]{:S(2)}) collective-permute-start(f32[6,4,10,1]{3,2,1,0:T(8,128)S(1)} %get-tuple-element.809), channel_id=1, source_target_pairs={{1,0},{2,1},{3,2},{0,3},{5,4},{6,5},{7,6},{4,7},{9,8},{10,9},{11,1... | collective-permute-start | bytes 2888 | tf_op jit(solution)/shard_map/ppermute | solution.py:52
  36.8 7.3 %collective-permute-start.7 = (f32[6,4,10,1]{3,2,1,0:T(8,128)S(1)}, f32[6,4,10,1]{3,2,1,0:T(8,128)S(1)}, u32[]{:S(2)}, u32[]{:S(2)}) collective-permute-start(f32[6,4,10,1]{3,2,1,0:T(8,128)S(1)} %get-tuple-element.810), channel_id=1, source_target_pairs={{0,1},{1,2},{2,3},{3,0},{4,5},{5,6},{6,7},{7,4},{8,9},{9,10},{10,1... | collective-permute-start | bytes 2888 | tf_op jit(solution)/shard_map/ppermute | solution.py:51
  37.5 7.1 %collective-permute-start.18 = (f32[6,4,10,1]{3,2,1,0:T(8,128)S(1)}, f32[6,4,10,1]{3,2,1,0:T(8,128)S(1)}, u32[]{:S(2)}, u32[]{:S(2)}) collective-permute-start(f32[6,4,10,1]{3,2,1,0:T(8,128)S(1)} %get-tuple-element.760), channel_id=1, source_target_pairs={{1,0},{2,1},{3,2},{0,3},{5,4},{6,5},{7,6},{4,7},{9,8},{10,9},{11,1... | collective-permute-start | bytes 2888 | tf_op jit(solution)/shard_map/ppermute | solution.py:52
  41.1 7.1 %collective-permute-start.19 = (f32[6,4,10,1]{3,2,1,0:T(8,128)S(1)}, f32[6,4,10,1]{3,2,1,0:T(8,128)S(1)}, u32[]{:S(2)}, u32[]{:S(2)}) collective-permute-start(f32[6,4,10,1]{3,2,1,0:T(8,128)S(1)} %get-tuple-element.761), channel_id=1, source_target_pairs={{0,1},{1,2},{2,3},{3,0},{4,5},{5,6},{6,7},{7,4},{8,9},{9,10},{10,1... | collective-permute-start | bytes 2888 | tf_op jit(solution)/shard_map/ppermute | solution.py:51
  53.1 12.2 %collective-permute-start.2 = (f32[3,5,4,10,1]{4,3,2,1,0:T(8,128)S(1)}, f32[3,5,4,10,1]{4,3,2,1,0:T(8,128)S(1)}, u32[]{:S(2)}, u32[]{:S(2)}) collective-permute-start(f32[3,5,4,10,1]{4,3,2,1,0:T(8,128)S(1)} %fusion.3), channel_id=1, source_target_pairs={{3,0},{0,1},{1,2},{2,3},{7,4},{4,5},{5,6},{6,7},{11,8},{8,9},{9,10... | collective-permute-start | bytes 7208 | tf_op jit(solution)/shard_map/ppermute | solution.py:41
  53.3 12.2 %collective-permute-start.3 = (f32[3,5,4,10,1]{4,3,2,1,0:T(8,128)S(1)}, f32[3,5,4,10,1]{4,3,2,1,0:T(8,128)S(1)}, u32[]{:S(2)}, u32[]{:S(2)}) collective-permute-start(f32[3,5,4,10,1]{4,3,2,1,0:T(8,128)S(1)} %constant_dynamic-update-slice_fusion.44), channel_id=1, source_target_pairs={{1,0},{2,1},{3,2},{0,3},{5,4},{6,5},{7,6},{4,7},{9,8},{10,9},{11,1... | collective-permute-start | bytes 7208 | tf_op jit(solution)/shard_map/ppermute | solution.py:41
  91.1 9.7 %collective-permute-start.8 = (f32[21,4,1,128]{3,2,1,0:T(1,128)S(1)}, f32[21,4,1,128]{3,2,1,0:T(1,128)S(1)}, u32[]{:S(2)}, u32[]{:S(2)}) collective-permute-start(f32[21,4,1,128]{3,2,1,0:T(1,128)S(1)} %get-tuple-element.677), channel_id=1, source_target_pairs={{0,4},{4,8},{8,12},{12,16},{16,20},{20,24},{24,28},{28,0},{1,5},{5... | collective-permute-start | bytes 129032 | tf_op jit(solution)/shard_map/ppermute | solution.py:51
  91.2 9.6 %collective-permute-start.9 = (f32[21,4,1,128]{3,2,1,0:T(1,128)S(1)}, f32[21,4,1,128]{3,2,1,0:T(1,128)S(1)}, u32[]{:S(2)}, u32[]{:S(2)}) collective-permute-start(f32[21,4,1,128]{3,2,1,0:T(1,128)S(1)} %get-tuple-element.678), channel_id=1, source_target_pairs={{4,0},{8,4},{12,8},{16,12},{20,16},{24,20},{28,24},{0,28},{5,1},{9... | collective-permute-start | bytes 129032 | tf_op jit(solution)/shard_map/ppermute | solution.py:52
  101.6 3.3 %collective-permute-start.10 = (f32[21,4,10,1]{0,1,3,2:T(4,128)S(1)}, f32[21,4,10,1]{0,1,3,2:T(4,128)S(1)}, u32[]{:S(2)}, u32[]{:S(2)}) collective-permute-start(f32[21,4,10,1]{0,1,3,2:T(4,128)S(1)} %copy.2770), channel_id=1, source_target_pairs={{0,1},{1,2},{2,3},{3,0},{4,5},{5,6},{6,7},{7,4},{8,9},{9,10},{10,1... | collective-permute-start | bytes 10088 | tf_op jit(solution)/shard_map/ppermute | solution.py:51
  102.6 3.2 %collective-permute-start.11 = (f32[21,4,10,1]{0,1,3,2:T(4,128)S(1)}, f32[21,4,10,1]{0,1,3,2:T(4,128)}, u32[]{:S(2)}, u32[]{:S(2)}) collective-permute-start(f32[21,4,10,1]{0,1,3,2:T(4,128)S(1)} %copy.2772), channel_id=1, source_target_pairs={{1,0},{2,1},{3,2},{0,3},{5,4},{6,5},{7,6},{4,7},{9,8},{10,9},{11,1... | collective-permute-start | bytes 10088 | tf_op jit(solution)/shard_map/ppermute | solution.py:52
  117.1 12.1 %collective-permute-start.12 = (f32[3,5,4,1,128]{4,3,2,1,0:T(1,128)S(1)}, f32[3,5,4,1,128]{4,3,2,1,0:T(1,128)S(1)}, u32[]{:S(2)}, u32[]{:S(2)}) collective-permute-start(f32[3,5,4,1,128]{4,3,2,1,0:T(1,128)S(1)} %get-tuple-element.613), channel_id=1, source_target_pairs={{28,0},{0,4},{4,8},{8,12},{12,16},{16,20},{20,24},{24,28},{29,1},{... | collective-permute-start | bytes 92168 | tf_op jit(solution)/shard_map/ppermute | solution.py:41
  117.1 12.2 %collective-permute-start.13 = (f32[3,5,4,1,128]{4,3,2,1,0:T(1,128)S(1)}, f32[3,5,4,1,128]{4,3,2,1,0:T(1,128)S(1)}, u32[]{:S(2)}, u32[]{:S(2)}) collective-permute-start(f32[3,5,4,1,128]{4,3,2,1,0:T(1,128)S(1)} %get-tuple-element.614), channel_id=1, source_target_pairs={{4,0},{8,4},{12,8},{16,12},{20,16},{24,20},{28,24},{0,28},{5,1},{9... | collective-permute-start | bytes 92168 | tf_op jit(solution)/shard_map/ppermute | solution.py:41
  130.2 12.1 %collective-permute-start.14 = (f32[3,5,4,10,1]{4,3,2,1,0:T(8,128)S(1)}, f32[3,5,4,10,1]{4,3,2,1,0:T(8,128)S(1)}, u32[]{:S(2)}, u32[]{:S(2)}) collective-permute-start(f32[3,5,4,10,1]{4,3,2,1,0:T(8,128)S(1)} %fusion), channel_id=1, source_target_pairs={{3,0},{0,1},{1,2},{2,3},{7,4},{4,5},{5,6},{6,7},{11,8},{8,9},{9,10... | collective-permute-start | bytes 7208 | tf_op jit(solution)/shard_map/ppermute | solution.py:41
  130.4 12.0 %collective-permute-start.15 = (f32[3,5,4,10,1]{4,3,2,1,0:T(8,128)S(1)}, f32[3,5,4,10,1]{4,3,2,1,0:T(8,128)S(1)}, u32[]{:S(2)}, u32[]{:S(2)}) collective-permute-start(f32[3,5,4,10,1]{4,3,2,1,0:T(8,128)S(1)} %constant_dynamic-update-slice_fusion.104), channel_id=1, source_target_pairs={{1,0},{2,1},{3,2},{0,3},{5,4},{6,5},{7,6},{4,7},{9,8},{10,9},{11,1... | collective-permute-start | bytes 7208 | tf_op jit(solution)/shard_map/ppermute | solution.py:41
  179.3 9.0 %collective-permute-start.20 = (f32[21,4,1,128]{3,2,1,0:T(1,128)S(1)}, f32[21,4,1,128]{3,2,1,0:T(1,128)S(1)}, u32[]{:S(2)}, u32[]{:S(2)}) collective-permute-start(f32[21,4,1,128]{3,2,1,0:T(1,128)S(1)} %get-tuple-element.668), channel_id=1, source_target_pairs={{0,4},{4,8},{8,12},{12,16},{16,20},{20,24},{24,28},{28,0},{1,5},{5... | collective-permute-start | bytes 129032 | tf_op jit(solution)/shard_map/ppermute | solution.py:51
  179.4 9.0 %collective-permute-start.21 = (f32[21,4,1,128]{3,2,1,0:T(1,128)S(1)}, f32[21,4,1,128]{3,2,1,0:T(1,128)S(1)}, u32[]{:S(2)}, u32[]{:S(2)}) collective-permute-start(f32[21,4,1,128]{3,2,1,0:T(1,128)S(1)} %get-tuple-element.669), channel_id=1, source_target_pairs={{4,0},{8,4},{12,8},{16,12},{20,16},{24,20},{28,24},{0,28},{5,1},{9... | collective-permute-start | bytes 129032 | tf_op jit(solution)/shard_map/ppermute | solution.py:52
  189.3 3.6 %collective-permute-start.22 = (f32[21,4,10,1]{0,2,3,1:T(8,128)S(1)}, f32[21,4,10,1]{0,2,3,1:T(8,128)S(1)}, u32[]{:S(2)}, u32[]{:S(2)}) collective-permute-start(f32[21,4,10,1]{0,2,3,1:T(8,128)S(1)} %copy.2774), channel_id=1, source_target_pairs={{0,1},{1,2},{2,3},{3,0},{4,5},{5,6},{6,7},{7,4},{8,9},{9,10},{10,1... | collective-permute-start | bytes 10088 | tf_op jit(solution)/shard_map/ppermute | solution.py:51
  190.5 3.2 %collective-permute-start.23 = (f32[21,4,10,1]{0,2,3,1:T(8,128)S(1)}, f32[21,4,10,1]{0,2,3,1:T(8,128)}, u32[]{:S(2)}, u32[]{:S(2)}) collective-permute-start(f32[21,4,10,1]{0,2,3,1:T(8,128)S(1)} %copy.2776), channel_id=1, source_target_pairs={{1,0},{2,1},{3,2},{0,3},{5,4},{6,5},{7,6},{4,7},{9,8},{10,9},{11,1... | collective-permute-start | bytes 10088 | tf_op jit(solution)/shard_map/ppermute | solution.py:52
  (140 other events, 466.3 us)
where the time goes:
time: 206 us; the launch traced here: 204 us
  other arithmetic  107 us (52%)
  starting transfers between devices  40 us (19%)
  waiting for transfers between devices  31.7 us (15%)
  local copies, waits for them, and re-layouts  22.4 us (11%)
  between operations  3.64 us (2%)
    ppermute x8, starting transfers between devices, with_halo(): after = lax.ppermute(leading, axis, down)  20.3 us
    ppermute x8, waiting for transfers between devices, passed_along(): return lax.ppermute(block, axis, route)  20.1 us
    neg x29, other arithmetic, collide(): collided.append(shaped[s, q] - (shaped[s, q] - equilibrium) / RELAXATION[s])  17.5 us
    ppermute x8, starting transfers between devices, passed_along(): return lax.ppermute(block, axis, route)  14.8 us
    div x21, other arithmetic, collide(): collided.append(shaped[s, q] - (shaped[s, q] - equilibrium) / RELAXATION[s])  13.3 us
    mul x25, other arithmetic, collide(): WEIGHT[q] * density[s]  12.9 us
    another operation x20, other arithmetic, collide(): return jnp.stack(collided)  12.1 us
    ppermute x8, waiting for transfers between devices, with_halo(): before = lax.ppermute(last, axis, up)  9.91 us
  transfers between devices with their start and end apart: 24, of which 5 were waited for; matrix products, arithmetic and copies ran while one was open for 19% of the time, Pallas kernels for 0%

commit v1 on v0

v1 whole, which is shorter than its diff:
```python
import jax
import jax.numpy as jnp
from jax import lax
from jax.experimental import pallas as pl
from jax.experimental.pallas import tpu as pltpu
from jax.sharding import PartitionSpec as P

VELOCITY = (
    (1, 0, 0),
    (-1, 0, 0),
    (0, 1, 0),
    (0, -1, 0),
    (1, 1, 0),
    (-1, -1, 0),
    (1, -1, 0),
    (-1, 1, 0),
    (1, 0, 1),
    (-1, 0, -1),
    (1, 0, -1),
    (-1, 0, 1),
    (0, 1, 1),
    (0, -1, -1),
    (0, 1, -1),
    (0, -1, 1),
    (0, 0, 0),
    (0, 0, 1),
    (0, 0, -1),
)
INDEX = {c: q for q, c in enumerate(VELOCITY)}
W1, W2, W0 = 1.0 / 18.0, 1.0 / 36.0, 1.0 / 3.0
RELAXATION = (1.0, 1.0, 1.25)
COUPLING = ((0.0, 1.2, -0.6), (1.2, 0.0, -0.6), (-0.6, -0.6, -0.3))
CROSS = ((0, 0), (1, 0), (-1, 0), (0, 1), (0, -1))
AHEAD = tuple(INDEX[(1,) + yz] for yz in CROSS)
BEHIND = tuple(INDEX[(-1,) + yz] for yz in CROSS)
SIDE = ((1, 0), (-1, 0), (0, 1), (0, -1), (1, 1), (-1, -1), (1, -1), (-1, 1))
F32 = jnp.float32
VMEM_BYTES = 40 * 1024 * 1024
HALO = 4


class Grid:
    def __init__(self, planes, rows, cols):
        self.planes, self.rows, self.cols = planes, rows, cols
        self.tiles = planes + 1
        self.width = cols // planes
        self.group = 2 * HALO
        self.pack = self.width // self.group
        self.sub = lax.broadcasted_iota(jnp.int32, (rows, cols), 0)
        self.lane = lax.broadcasted_iota(jnp.int32, (rows, cols), 1)

    def roll_rows(self, v, dx):
        return pltpu.roll(v, (-dx) % self.rows, 0)

    def roll_cols(self, v, dy):
        return pltpu.roll(v, (-dy) % self.cols, 1)

    def at_row(self, v, rim, dx):
        edge = self.rows - 1 if dx > 0 else 0
        return jnp.where(self.sub == edge, rim, self.roll_rows(v, dx))

    def in_row(self, v, dx):
        edge = self.rows - 1 if dx > 0 else 0
        return jnp.where(self.sub == edge, 0.0, self.roll_rows(v, dx))

    def sides(self, low, high):
        return jnp.where(self.sub == 0, low, high)

    def over(self, body):
        def step(p, carry):
            body(Tile(self, p, False))
            return carry

        lax.fori_loop(0, self.planes, step, 0)
        body(Tile(self, self.planes, True))


class Tile:
    def __init__(self, grid, index, edge):
        self.grid, self.index, self.edge = grid, index, edge

    def of(self, dz):
        if dz == 0 or self.edge:
            return self.index
        return lax.rem(self.index + (dz + self.grid.planes), self.grid.planes)

    def get(self, ref, c, dz=0):
        v = ref[c, self.of(dz)]
        if self.edge and dz != 0:
            v = self.grid.roll_cols(v, dz * self.grid.width)
        return v

    def split(self, main, edge, c, dz=0):
        if not self.edge:
            return main[c, self.of(dz)]
        v = edge[c]
        return v if dz == 0 else self.grid.roll_cols(v, dz * self.grid.width)


def plus(a, b):
    return b if a is None else a + b


def mixed(coefficients, values):
    total = None
    for k, v in zip(coefficients, values):
        if k == 0:
            continue
        term = v if k == 1 else (-v if k == -1 else k * v)
        total = plus(total, term)
    return total


def axis_pairs():
    for q in (0, 2, 17, 4, 6, 8, 10, 12, 14):
        c = VELOCITY[q]
        yield c, (W1 if sum(abs(i) for i in c) == 1 else W2)


def first_and_second(diff, total):
    first = [None] * 3
    second = {}
    for c, w in axis_pairs():
        for d in range(3):
            if c[d] == 0:
                continue
            if diff is not None:
                first[d] = plus(first[d], (w * c[d]) * diff[c])
            if total is not None:
                for e in range(d, 3):
                    if c[e] != 0:
                        second[d, e] = plus(second.get((d, e)), (w * c[d] * c[e]) * total[c])
    return first, second


def turned(second, v):
    return [sum(second[min(d, e), max(d, e)] * v[e] for e in range(3)) for d in range(3)]


def dot(a, b):
    return a[0] * b[0] + a[1] * b[1] + a[2] * b[2]


def field_forces(grid, tile, fields, rim, rim_psi, rim_dip, dipole):
    memo = {}

    def source(name, dz, edge):
        key = (name, dz, edge)
        if key in memo:
            return memo[key]
        if edge:
            load = lambda c: tile.get(rim, (rim_psi + c) if c < 3 else (rim_dip + c - 3), dz)
        else:
            load = lambda c: tile.get(fields, (9 + c) if c < 3 else (6 + c - 3), dz)
        if isinstance(name, int):
            v = load(name)
        elif name == "chi":
            v = source(0, dz, edge) - source(1, dz, edge)
        elif name[0] == "V":
            v = source(2, dz, edge) * source(3 + name[1], dz, edge)
        else:
            v = mixed(name[1], [source(("V", d), dz, edge) if name[1][d] else None for d in range(3)])
        memo[key] = v
        return v

    def shifted(name, c):
        key = (name, c, "shift")
        if key in memo:
            return memo[key]
        if c[1] != 0:
            v = grid.roll_cols(shifted(name, (c[0], 0, c[2])), c[1])
        elif c[0] != 0:
            v = grid.at_row(source(name, c[2], False), source(name, c[2], True), c[0])
        else:
            v = source(name, c[2], False)
        memo[key] = v
        return v

    def parts(name):
        diff, total = {}, {}
        for c, w in axis_pairs():
            back = tuple(-i for i in c)
            a, b = shifted(name, c), shifted(name, back)
            diff[c], total[c] = a - b, a + b
        return diff, total

    diff, unused = parts(0)
    s0, unused = first_and_second(diff, None)
    diff, unused = parts(2)
    s2, unused = first_and_second(diff, None)
    diff, total = parts("chi")
    schi, second = first_and_second(diff, total)
    s1 = [a - b for a, b in zip(s0, schi)]
    pull = [None] * 3
    for c, w in axis_pairs():
        back = tuple(-i for i in c)
        if sum(abs(i) for i in c) == 1:
            name = ("V", [i for i in range(3) if c[i]][0])
        else:
            name = ("L", c)
        total_c = shifted(name, c) + shifted(name, back)
        for d in range(3):
            if c[d] != 0:
                pull[d] = plus(pull[d], (w * c[d]) * total_c)
    md = turned(second, dipole)
    k0 = [-1.2 * s1[d] + 0.6 * s2[d] - pull[d] for d in range(3)]
    k1 = [-1.2 * s0[d] + 0.6 * s2[d] + pull[d] for d in range(3)]
    k2 = [0.6 * (s0[d] + s1[d]) + 0.3 * s2[d] + md[d] for d in range(3)]
    return k0, k1, k2


def collision_adjoint(grid, tile, load, rim, fields, forces, hold, ab, kept):
    u = [tile.get(fields, 3 + d) for d in range(3)]
    rho = [tile.get(fields, s) for s in range(3)]
    inverse_sum = 1.0 / (rho[0] + rho[1] + rho[2])
    grad_u = [None] * 3
    alphas = []
    t = tile.index
    for s in range(3):
        streamed = []
        for q in range(19):
            c = VELOCITY[q]
            v = load(s * 19 + q, c[2])
            if c[0] != 0:
                j = (AHEAD if c[0] > 0 else BEHIND).index(q)
                v = grid.at_row(v, tile.get(rim, s * 5 + j, c[2]), c[0])
            if c[1] != 0:
                v = grid.roll_cols(v, c[1])
            streamed.append(v)
            if s == 2:
                kept[q, t] = v
        diff, total = {}, {}
        for c, w in axis_pairs():
            a, b = streamed[INDEX[c]], streamed[INDEX[tuple(-i for i in c)]]
            diff[c], total[c] = a - b, a + b
        m1, m2 = first_and_second(diff, total)
        m0 = W0 * streamed[16]
        for c, w in axis_pairs():
            m0 = m0 + w * total[c]
        psi = tile.get(fields, 9 + s)
        inverse = 1.0 / rho[s]
        ratio = psi * inverse
        tau = RELAXATION[s]
        k = forces[s]
        v = [u[d] + (tau * ratio) * k[d] for d in range(3)]
        mv = turned(m2, v)
        g = [3.0 * (m1[d] + 3.0 * mv[d] - m0 * v[d]) for d in range(3)]
        feq = m0 + 3.0 * dot(m1, v) + 4.5 * dot(mv, v) - 1.5 * m0 * dot(v, v)
        alphas.append(feq * (1.0 / tau) + dot(g, k) * (1.0 - psi - ratio))
        scaled = rho[s] * (1.0 / tau)
        for d in range(3):
            grad_u[d] = plus(grad_u[d], scaled * g[d])
            hold[3 * s + d, t] = psi * g[d]
    beta = [grad_u[d] * inverse_sum for d in range(3)]
    along = dot(beta, u)
    for s in range(3):
        ab[s, t] = alphas[s] - along
        ab[3 + s, t] = beta[s]


def spread_plane(grid, get_h, get_d, sign, pairs):
    memo = {}

    def source(dz):
        if dz in memo:
            return memo[dz]
        h = [[get_h(3 * s + d, dz) for d in range(3)] for s in range(3)]
        dip = [get_d(d, dz) for d in range(3)]
        if not isinstance(sign, int):
            for vec in h + [dip]:
                vec[0] = vec[0] * sign
        memo[dz] = (h, dip)
        return memo[dz]

    cx = sign if isinstance(sign, int) else 1
    r = [None] * 3
    w_vec = [None] * 3
    lanes = {}
    for cy, cz in pairs:
        w = W1 if abs(cx) + abs(cy) + abs(cz) == 1 else W2
        h, dip = source(cz)
        c = (cx, cy, cz)
        e = [mixed(c, h[s]) for s in range(3)]
        f = e[2] * mixed(c, dip)
        half = 0.6 * e[2]
        r0 = 1.2 * e[1] - half + f
        r1 = 1.2 * e[0] - half - f
        r2 = -0.6 * (e[0] + e[1]) - 0.3 * e[2]
        qv = e[0] - e[1]
        vals = [w * r0, w * r1, w * r2]
        wq = w * qv
        vals += [wq if cx != 0 else None, wq if cy != 0 else None, wq if cz != 0 else None]
        vals = [vals[0], vals[1], vals[2]] + [
            None if x is None else (x if k == 1 else -x) for x, k in zip(vals[3:], (cx, cy, cz))
        ]
        acc = lanes.setdefault(cy, [None] * 6)
        for i, x in enumerate(vals):
            if x is not None:
                acc[i] = plus(acc[i], x)
    total = [None] * 6
    for cy, acc in lanes.items():
        for i, x in enumerate(acc):
            if x is not None:
                total[i] = plus(total[i], x if cy == 0 else grid.roll_cols(x, cy))
    if not isinstance(sign, int):
        total[3] = total[3] * sign
    return total


def met(total, dipole):
    meet = None
    for d in range(3):
        if total[3 + d] is not None:
            meet = plus(meet, total[3 + d] * dipole[d])
    return [total[0], total[1], total[2] - meet]


def spread_inside(grid, tile, hold, fields):
    get_h = lambda k, dz: tile.get(hold, k, dz)
    get_d = lambda k, dz: tile.get(fields, 6 + k, dz)
    total = spread_plane(grid, get_h, get_d, 0, SIDE)
    for dx in (1, -1):
        part = spread_plane(grid, get_h, get_d, dx, CROSS)
        for i, x in enumerate(part):
            total[i] = plus(total[i], grid.in_row(x, dx))
    return met(total, [tile.get(fields, 6 + d) for d in range(3)])


def rim_sign(grid):
    return jnp.where(
        grid.sub == 0, -1.0, jnp.where(grid.sub == grid.rows - 1, 1.0, 0.0)
    ).astype(F32)


def spread_rim(grid, get_h, get_d, target, sign):
    total = spread_plane(grid, get_h, get_d, sign, CROSS)
    return [x * (sign * sign) for x in met(total, target)]


def unpack_rims(grid, first, second, parity, lines, rims, pairs):
    lines[1 - parity] = first[...]
    lines[parity] = second[...]
    for at, c in enumerate(pairs):
        for t in range(grid.tiles):
            k = c * grid.tiles + t
            rims[at, t] = grid.sides(lines[0, k : k + 1, :], lines[1, k : k + 1, :])


def send_rows(grid, parity, lines, first, second):
    first[...] = lines[0]
    second[...] = lines[1]


def line_count(components, grid):
    lines = components * grid.tiles
    return -(-lines // 8) * 8


def parity_of(axis):
    return lax.rem(lax.axis_index(axis), 2)


def pack_columns_kernel(adj, late, early, dip_late, dip_early, send_c, send_d, own_left, own_right, fl, fe):
    planes, rows, cols = adj.shape[1:]
    grid = Grid(planes, rows, cols)
    for saved, dip, out in ((late, dip_late, fl), (early, dip_early, fe)):
        def step(p, carry):
            flows = [None] * 19
            rho = []
            for s in range(3):
                total = None
                for q in range(19):
                    v = saved[s * 19 + q, p].astype(F32)
                    flows[q] = plus(flows[q], v)
                    total = plus(total, v)
                rho.append(total)
                out[s, p] = total
            inverse = 1.0 / (rho[0] + rho[1] + rho[2])
            for d in range(3):
                momentum = None
                for q in range(19):
                    if VELOCITY[q][d] != 0:
                        momentum = plus(momentum, flows[q] if VELOCITY[q][d] > 0 else -flows[q])
                out[3 + d, p] = momentum * inverse
                out[6 + d, p] = dip[d, p].astype(F32)
            return carry

        lax.fori_loop(0, planes, step, 0)
    pops = adj.shape[0]
    components = pops + 18
    slot = grid.lane // grid.group
    for g in range(own_left.shape[0]):
        left = right = jnp.zeros((rows, cols), F32)
        for j in range(grid.pack):
            c = g * grid.pack + j
            if c >= components:
                continue
            for p in range(planes):
                if c < pops:
                    v = adj[c, p]
                elif c < pops + 9:
                    v = fl[c - pops, p]
                else:
                    v = fe[c - pops - 9, p]
                at = p * grid.pack + j
                rolled = pltpu.roll(v, at * grid.group, 1) if at else v
                left = jnp.where(slot == at, rolled, left)
                right = jnp.where(slot == (at - 1) % (cols // grid.group), rolled, right)
        own_left[g] = left
        own_right[g] = right
    low = lax.rem(grid.lane, grid.group) < HALO
    even = parity_of("gy") == 0
    for h in range(send_c.shape[0]):
        left = jnp.where(low, own_left[2 * h], pltpu.roll(own_left[2 * h + 1], HALO, 1))
        right = jnp.where(low, pltpu.roll(own_right[2 * h + 1], cols - HALO, 1), own_right[2 * h])
        send_c[h] = jnp.where(even, right, left)
        send_d[h] = jnp.where(even, left, right)


def pack_rows_kernel(
    adj, own_left, own_right, recv_c, recv_d, fl_main, fe_main, send_a, send_b, edge, fl, fe, lines
):
    pops, planes, rows, cols = adj.shape
    grid = Grid(planes, rows, cols)
    even = parity_of("gy") == 0
    slot = lax.rem(grid.lane // grid.group, grid.pack)
    left_half = lax.rem(grid.lane, grid.width) < grid.width // 2
    components = pops + 18
    for g in range(own_left.shape[0]):
        first, second = recv_c[g // 2], recv_d[g // 2]
        from_next = jnp.where(even, first, second)
        from_prior = jnp.where(even, second, first)
        if g % 2:
            from_next = pltpu.roll(from_next, cols - HALO, 1)
            from_prior = pltpu.roll(from_prior, HALO, 1)
        for j in range(grid.pack):
            c = g * grid.pack + j
            if c >= components:
                continue
            before = slot == (j - 1) % grid.pack
            low = jnp.where(before, from_prior, own_left[g])
            high = jnp.where(before, own_right[g], from_next)
            v = jnp.where(
                left_half,
                pltpu.roll(low, ((1 - j) * grid.group) % cols, 1),
                pltpu.roll(high, ((3 - j) * grid.group) % cols, 1),
            )
            if c < pops:
                edge[c] = v
            elif c < pops + 9:
                fl[c - pops, planes] = v
            else:
                fe[c - pops - 9, planes] = v
    for main, out in ((fl_main, fl), (fe_main, fe)):
        for c in range(9):
            for p in range(planes):
                out[c, p] = main[c, p]
        for s in range(3):
            for t in range(grid.tiles):
                out[9 + s, t] = 1.0 - jnp.exp(-out[s, t])
    up, down = parity_of("gx"), 1 - parity_of("gx")
    fill = 0

    def put(slot_at, v, row):
        lines[slot_at, fill : fill + 1, :] = v[row : row + 1, :]

    for s in range(3):
        for j in range(5):
            for t in range(grid.tiles):
                ahead, behind = s * 19 + AHEAD[j], s * 19 + BEHIND[j]
                put(up, adj[behind, t] if t < planes else edge[behind], rows - 1)
                put(down, adj[ahead, t] if t < planes else edge[ahead], 0)
                fill += 1
    for out in (fl, fe):
        for c in (9, 10, 11, 6, 7, 8):
            for t in range(grid.tiles):
                put(up, out[c, t], rows - 1)
                put(down, out[c, t], 0)
                fill += 1
    send_rows(grid, up, lines, send_a, send_b)


def late_kernel(
    adj, edge, fl, recv_a, recv_b, send_a, send_b, hold, ab, kept, lines, lines_out, rims
):
    pops, planes, rows, cols = adj.shape
    grid = Grid(planes, rows, cols)
    parity = parity_of("gx")
    unpack_rims(grid, recv_a, recv_b, parity, lines, rims, range(21))

    def collide(tile):
        dipole = [tile.get(fl, 6 + d) for d in range(3)]
        forces = field_forces(grid, tile, fl, rims, 15, 18, dipole)
        load = lambda c, dz: tile.split(adj, edge, c, dz)
        collision_adjoint(grid, tile, load, rims, fl, forces, hold, ab, kept)

    grid.over(collide)

    def finish(tile):
        back = spread_inside(grid, tile, hold, fl)
        for s in range(3):
            ab[s, tile.index] = ab[s, tile.index] + (1.0 - tile.get(fl, 9 + s)) * back[s]

    grid.over(finish)
    up, down = parity, 1 - parity
    fill = 0

    def put(v):
        lines_out[up, fill : fill + 1, :] = v[rows - 1 : rows, :]
        lines_out[down, fill : fill + 1, :] = v[0:1, :]

    for c in range(9):
        for t in range(grid.tiles):
            put(hold[c, t])
            fill += 1
    sign = -rim_sign(grid)
    for kind in range(9):
        for t in range(grid.tiles):
            if kind < 2:
                put(ab[kind, t] + sign * ab[3, t])
            elif kind < 4:
                put(ab[2 + kind, t])
            else:
                cy, cz = CROSS[kind - 4]
                part = ab[2, t] + sign * ab[3, t]
                if cy or cz:
                    part = part + mixed((cy, cz), (ab[4, t], ab[5, t]))
                put((1.0 - 1.0 / RELAXATION[2]) * grid.sides(kept[AHEAD[kind - 4], t], kept[BEHIND[kind - 4], t]) + part)
            fill += 1
    send_rows(grid, up, lines_out, send_a, send_b)


def early_kernel(
    fl, fe, hold1, ab1, kept1, first_a, first_b, recv_a, recv_b, send_a, send_b, hold, ab, kept,
    lines, lines2, lines_out, rims, near, mid, rim_mid,
):
    planes, rows, cols = fl.shape[1] - 1, fl.shape[2], fl.shape[3]
    grid = Grid(planes, rows, cols)
    parity = parity_of("gx")
    unpack_rims(grid, first_a, first_b, parity, lines, rims, range(15, 27))
    unpack_rims(grid, recv_a, recv_b, parity, lines2, near, range(18))
    sign = rim_sign(grid)
    rest = 1.0 - 1.0 / RELAXATION[2]

    def complete(tile):
        t = tile.index
        own_d = lambda k, dz: tile.get(fl, 6 + k, dz)
        rim_d = lambda k, dz: tile.get(rims, 3 + k, dz)
        inward = spread_rim(
            grid, lambda k, dz: tile.get(near, k, dz), rim_d, [own_d(d, 0) for d in range(3)], sign
        )
        outward = spread_rim(
            grid, lambda k, dz: tile.get(hold1, k, dz), own_d, [rim_d(d, 0) for d in range(3)], -sign
        )
        alpha = [tile.get(ab1, s) + (1.0 - tile.get(fl, 9 + s)) * inward[s] for s in range(3)]
        beta = [tile.get(ab1, 3 + d) for d in range(3)]
        for q in range(19):
            c = VELOCITY[q]
            along = mixed(c, beta) if q != 16 else None
            for s in range(3):
                v = alpha[s] if along is None else alpha[s] + along
                if s == 2:
                    v = v + rest * kept1[q, t]
                mid[s * 19 + q, t] = v
        fixes = [(1.0 - tile.get(rims, s)) * outward[s] for s in range(3)]
        sides = [tile.get(near, 11 + d) for d in range(2)]
        for s in range(2):
            base = tile.get(near, 9 + s) + fixes[s]
            for j, (cy, cz) in enumerate(CROSS):
                rim_mid[s * 5 + j, t] = base if j == 0 else base + mixed((cy, cz), sides)
        for j in range(5):
            rim_mid[10 + j, t] = tile.get(near, 13 + j) + fixes[2]

    grid.over(complete)

    def collide(tile):
        dipole = [tile.get(fe, 6 + d) for d in range(3)]
        forces = field_forces(grid, tile, fe, rims, 6, 9, dipole)
        load = lambda c, dz: tile.get(mid, c, dz)
        collision_adjoint(grid, tile, load, rim_mid, fe, forces, hold, ab, kept)

    grid.over(collide)
    up, down = parity, 1 - parity
    fill = 0
    for c in range(9):
        for t in range(grid.tiles):
            v = hold[c, t]
            lines_out[up, fill : fill + 1, :] = v[rows - 1 : rows, :]
            lines_out[down, fill : fill + 1, :] = v[0:1, :]
            fill += 1
    send_rows(grid, up, lines_out, send_a, send_b)


def out_kernel(fe, hold, ab, kept, first_a, first_b, recv_a, recv_b, out, lines, lines2, rims, near, total):
    planes, rows, cols = fe.shape[1] - 1, fe.shape[2], fe.shape[3]
    grid = Grid(planes, rows, cols)
    parity = parity_of("gx")
    unpack_rims(grid, first_a, first_b, parity, lines, rims, range(24, 27))
    unpack_rims(grid, recv_a, recv_b, parity, lines2, near, range(9))
    sign = rim_sign(grid)

    def finish(tile):
        back = spread_inside(grid, tile, hold, fe)
        inward = spread_rim(
            grid,
            lambda k, dz: tile.get(near, k, dz),
            lambda k, dz: tile.get(rims, k, dz),
            [tile.get(fe, 6 + d) for d in range(3)],
            sign,
        )
        for s in range(3):
            total[s, tile.index] = tile.get(ab, s) + (1.0 - tile.get(fe, 9 + s)) * (back[s] + inward[s])

    grid.over(finish)
    is_low, is_high = grid.lane < HALO, grid.lane >= cols - HALO

    def emit(p, carry):
        base = p * grid.width

        def patched(main, edge):
            low = pltpu.roll(edge, lax.rem(2 * cols - base - grid.group, cols), 1)
            high = pltpu.roll(edge, lax.rem(2 * cols - base - 3 * grid.group, cols), 1)
            return jnp.where(is_low, low, jnp.where(is_high, high, main))

        alpha = [patched(total[s, p], total[s, planes]) for s in range(3)]
        beta = [patched(ab[3 + d, p], ab[3 + d, planes]) for d in range(3)]
        for q in range(19):
            along = mixed(VELOCITY[q], beta) if q != 16 else None
            for s in range(3):
                v = alpha[s] if along is None else alpha[s] + along
                if s == 2:
                    v = v + (1.0 - 1.0 / RELAXATION[2]) * patched(kept[q, p], kept[q, planes])
                out[s * 19 + q, p] = v
        return carry

    lax.fori_loop(0, planes, emit, 0)


def call(kernel, outs, scratch, args):
    whole = pl.BlockSpec(memory_space=pltpu.VMEM)
    return pl.pallas_call(
        kernel,
        out_shape=[jax.ShapeDtypeStruct(s, F32) for s in outs],
        in_specs=[whole] * len(args),
        out_specs=[whole] * len(outs),
        scratch_shapes=[pltpu.VMEM(s, F32) for s in scratch],
        compiler_params=pltpu.CompilerParams(vmem_limit_bytes=VMEM_BYTES),
    )(*args)


def swap(block, axis, offset):
    size = lax.axis_size(axis)
    route = []
    for i in range(offset, size + offset, 2):
        a, b = i % size, (i + 1) % size
        route += [(a, b), (b, a)]
    return lax.ppermute(block, axis, route)


def shards(adjoint_in, populations_early, populations_late, dipoles_early, dipoles_late):
    pops, planes, rows, cols = adjoint_in.shape
    tiles = planes + 1
    tile = (rows, cols)
    pack = cols // planes // (2 * HALO)
    groups = -(-(pops + 18) // pack)
    groups += groups % 2

    def lines(n):
        return (-(-n * tiles // 8) * 8, cols)

    def both(n):
        return (2,) + lines(n)

    send_c, send_d, own_left, own_right, fl_main, fe_main = call(
        pack_columns_kernel,
        [(groups // 2,) + tile] * 2 + [(groups,) + tile] * 2 + [(9, planes) + tile] * 2,
        [],
        [adjoint_in, populations_late, populations_early, dipoles_late, dipoles_early],
    )
    recv_c, recv_d = swap(send_c, "gy", 0), swap(send_d, "gy", 1)
    send_a, send_b, edge, fl, fe = call(
        pack_rows_kernel,
        [lines(27)] * 2 + [(pops,) + tile] + [(12, tiles) + tile] * 2,
        [both(27)],
        [adjoint_in, own_left, own_right, recv_c, recv_d, fl_main, fe_main],
    )
    first_a, first_b = swap(send_a, "gx", 0), swap(send_b, "gx", 1)
    saved = [(9, tiles) + tile, (6, tiles) + tile, (19, tiles) + tile]
    send_a, send_b, hold1, ab1, kept1 = call(
        late_kernel,
        [lines(18)] * 2 + saved,
        [both(27), both(18), (21, tiles) + tile],
        [adjoint_in, edge, fl, first_a, first_b],
    )
    recv_a, recv_b = swap(send_a, "gx", 0), swap(send_b, "gx", 1)
    send_a, send_b, hold, ab, kept = call(
        early_kernel,
        [lines(9)] * 2 + saved,
        [
            both(27),
            both(18),
            both(9),
            (12, tiles) + tile,
            (18, tiles) + tile,
            (pops, tiles) + tile,
            (15, tiles) + tile,
        ],
        [fl, fe, hold1, ab1, kept1, first_a, first_b, recv_a, recv_b],
    )
    recv_a, recv_b = swap(send_a, "gx", 0), swap(send_b, "gx", 1)
    (out,) = call(
        out_kernel,
        [(pops, planes) + tile],
        [both(27), both(9), (3, tiles) + tile, (9, tiles) + tile, (3, tiles) + tile],
        [fe, hold, ab, kept, first_a, first_b, recv_a, recv_b],
    )
    return out


def solution(mesh):
    placed = P(None, None, "gx", "gy")
    return jax.shard_map(
        shards, mesh=mesh, in_specs=(placed,) * 5, out_specs=placed, check_vma=False
    )
```

time: 206 us -> 38.9 us (0.19)
  other arithmetic: 107 us -> 0 us
  starting transfers between devices: 40 us -> 15.7 us
  waiting for transfers between devices: 31.7 us -> 11.5 us
  local copies, waits for them, and re-layouts: 22.4 us -> 4.7 us
  Pallas kernels: 0 us -> 6.55 us
  between operations: 3.64 us -> 0.03 us
    ppermute x24 -> x8, starting transfers between devices: 40 us -> 15.7 us  [swap(): return lax.ppermute(block, axis, route)]
    mul x45 -> x0, other arithmetic: 21 us -> none  [the longest x25 12.9 us: collide(): WEIGHT[q] * density[s]]
    neg x38 -> x0, other arithmetic: 20.4 us -> none  [the longest x29 17.5 us: collide(): collided.append(shaped[s, q] - (shaped[s, q] - equilibrium) / RELAXATION[s])]
    ppermute x24 -> x8, waiting for transfers between devices: 31.7 us -> 11.5 us  [swap(): return lax.ppermute(block, axis, route)]
    another operation x33 -> x0, other arithmetic: 18 us -> none  [the longest x20 12.1 us: collide(): return jnp.stack(collided)]
    div x25 -> x0, other arithmetic: 14.6 us -> none  [the longest x21 13.3 us: collide(): collided.append(shaped[s, q] - (shaped[s, q] - equilibrium) / RELAXATION[s])]
    concatenate x26 -> x0, other arithmetic: 13.7 us -> none  [the longest x14 5.74 us: with_halo(): x = jnp.concatenate([before, x, after], axis=dim)]
    add x6 -> x0, other arithmetic: 8.54 us -> none  [the longest x2 6.87 us: combine(): return (shaped + grad_density[:, None]).reshape(grad_pops.shape)]
  transfers between devices with their start and end apart: 24 -> 8, of which waited for: 5 -> 6; matrix products, arithmetic and copies ran while one was open for 19% -> 0% of each run, Pallas kernels for 0% -> 0%
where the time goes in v1:
time: 38.9 us; the launch traced here: 38.5 us
  starting transfers between devices  15.7 us (40%)
  waiting for transfers between devices  11.5 us (30%)
  Pallas kernels  6.55 us (17%)
  local copies, waits for them, and re-layouts  4.7 us (12%)
    ppermute x8, starting transfers between devices, swap(): return lax.ppermute(block, axis, route)  15.7 us
    ppermute x8, waiting for transfers between devices, swap(): return lax.ppermute(block, axis, route)  11.5 us
    pallas_call x5, Pallas kernels, call(): pl.pallas_call(kernel, out_shape=[jax.ShapeDtypeStruct(s, F32) for s in o...  6.55 us
    unnamed x10, local copies, waits for them, and re-layouts  4.7 us
  transfers between devices with their start and end apart: 8, of which 6 were waited for; matrix products, arithmetic and copies ran while one was open for 0% of the time, Pallas kernels for 0%

profile of v1, /device:TPU:0, one launch (start us, length us, event | category | flops | bytes accessed | tf_op | source)
XLA Modules:
  0.0 38.5 jit_solution(909305897124358290)
XLA Ops:
  0.0 1.2 %copy-done = f32[57,4,8,128]{3,2,1,0:T(8,128)S(1)} copy-done((f32[57,4,8,128]{3,2,1,0:T(8,128)S(1)}, f32[57,4,8,128]{3,2,1,0:T(8,128)}, u32[]{:S(2)}) %copy-start) | copy-done | bytes 933912
  1.2 1.0 %copy-done.1 = bf16[57,4,8,128]{3,2,1,0:T(8,128)(2,1)S(1)} copy-done((bf16[57,4,8,128]{3,2,1,0:T(8,128)(2,1)S(1)}, bf16[57,4,8,128]{3,2,1,0:T(8,128)(2,1)}, u32[]{:S(2)}) %copy-start.1) | copy-done | bytes 466968
  2.2 1.0 %copy-done.2 = bf16[57,4,8,128]{3,2,1,0:T(8,128)(2,1)S(1)} copy-done((bf16[57,4,8,128]{3,2,1,0:T(8,128)(2,1)S(1)}, bf16[57,4,8,128]{3,2,1,0:T(8,128)(2,1)}, u32[]{:S(2)}) %copy-start.2) | copy-done | bytes 466968
  3.2 0.7 %copy-done.3 = bf16[3,4,8,128]{3,2,1,0:T(8,128)(2,1)S(1)} copy-done((bf16[3,4,8,128]{3,2,1,0:T(8,128)(2,1)S(1)}, bf16[3,4,8,128]{3,2,1,0:T(8,128)(2,1)}, u32[]{:S(2)}) %copy-start.3) | copy-done | bytes 24600
  4.0 0.7 %copy-done.4 = bf16[3,4,8,128]{3,2,1,0:T(8,128)(2,1)S(1)} copy-done((bf16[3,4,8,128]{3,2,1,0:T(8,128)(2,1)S(1)}, bf16[3,4,8,128]{3,2,1,0:T(8,128)(2,1)}, u32[]{:S(2)}) %copy-start.4) | copy-done | bytes 24600
  4.7 0.7 %shard_map.55 = (f32[10,8,128]{2,1,0:T(8,128)S(1)}, f32[10,8,128]{2,1,0:T(8,128)S(1)}, f32[20,8,128]{2,1,0:T(8,128)S(1)}, f32[20,8,128]{2,1,0:T(8,128)S(1)}, f32...) custom-call(f32[57,4,8,128]{3,2,1,0:T(8,128)S(1)} %copy-done, bf16[57,4,8,128]{3,2,1,0:T(8,128)(2,1)S(1)} %copy-done.1, ...), custom_call_target="tpu_custom_call" | custom-call | tf_op jit(solution)/shard_map/pallas_call | solution.py:641
  5.4 0.5 %collective-permute-start = (f32[10,8,128]{2,1,0:T(8,128)S(1)}, f32[10,8,128]{2,1,0:T(8,128)S(1)}, u32[]{:S(2)}, u32[]{:S(2)}) collective-permute-start(f32[10,8,128]{2,1,0:T(8,128)S(1)} %get-tuple-element.28), channel_id=1, source_target_pairs={{0,1},{1,0},{2,3},{3,2},{4,5},{5,4},{6,7},{7,6},{8,9},{9,8},{10,11... | collective-permute-start | bytes 122888 | tf_op jit(solution)/shard_map/ppermute | solution.py:657
  5.9 2.6 %collective-permute-start.1 = (f32[10,8,128]{2,1,0:T(8,128)S(1)}, f32[10,8,128]{2,1,0:T(8,128)S(1)}, u32[]{:S(2)}, u32[]{:S(2)}) collective-permute-start(f32[10,8,128]{2,1,0:T(8,128)S(1)} %get-tuple-element.29), channel_id=1, source_target_pairs={{1,2},{2,1},{3,0},{0,3},{5,6},{6,5},{7,4},{4,7},{9,10},{10,9},{11,... | collective-permute-start | bytes 122888 | tf_op jit(solution)/shard_map/ppermute | solution.py:657
  8.6 1.8 %collective-permute-done.1.recv_d = f32[10,8,128]{2,1,0:T(8,128)S(1)} collective-permute-done((f32[10,8,128]{2,1,0:T(8,128)S(1)}, f32[10,8,128]{2,1,0:T(8,128)S(1)}, u32[]{:S(2)}, u32[]{:S(2)}) %collective-permute-start.1) | collective-permute-done | bytes 40992 | tf_op jit(solution)/shard_map/ppermute | solution.py:657
  10.4 0.3 shard_map.56
  10.7 1.6 %collective-permute-start.2 = (f32[136,128]{1,0:T(8,128)S(1)}, f32[136,128]{1,0:T(8,128)S(1)}, u32[]{:S(2)}, u32[]{:S(2)}) collective-permute-start(f32[136,128]{1,0:T(8,128)S(1)} %get-tuple-element.35), channel_id=1, source_target_pairs={{0,4},{4,0},{8,12},{12,8},{16,20},{20,16},{24,28},{28,24},{1,5},{5... | collective-permute-start | bytes 208904 | tf_op jit(solution)/shard_map/ppermute | solution.py:657
  12.3 3.5 %collective-permute-start.3 = (f32[136,128]{1,0:T(8,128)S(1)}, f32[136,128]{1,0:T(8,128)S(1)}, u32[]{:S(2)}, u32[]{:S(2)}) collective-permute-start(f32[136,128]{1,0:T(8,128)S(1)} %get-tuple-element.36), channel_id=1, source_target_pairs={{4,8},{8,4},{12,16},{16,12},{20,24},{24,20},{28,0},{0,28},{5,9},{9... | collective-permute-start | bytes 208904 | tf_op jit(solution)/shard_map/ppermute | solution.py:657
  15.9 3.4 %collective-permute-done.3.recv_b.first_b = f32[136,128]{1,0:T(8,128)S(1)} collective-permute-done((f32[136,128]{1,0:T(8,128)S(1)}, f32[136,128]{1,0:T(8,128)S(1)}, u32[]{:S(2)}, u32[]{:S(2)}) %collective-permute-start.3) | collective-permute-done | bytes 69664 | tf_op jit(solution)/shard_map/ppermute | solution.py:657
  19.3 1.7 %shard_map.57 = (f32[96,128]{1,0:T(8,128)S(1)}, f32[96,128]{1,0:T(8,128)S(1)}, f32[9,5,8,128]{3,2,1,0:T(8,128)S(1)}, f32[6,5,8,128]{3,2,1,0:T(8,128)S(1)}, f32[19,5,8,128]{3,2,1,0:T(8,128)S(1)}) custom-call(f32[57,4,8,128]{3,2,1,0:T(8,128)S(1)} %copy-done, f32[57,8,128]{2,1,0:T(8,128)S(1)} %get-tuple-element.34.edge, ...), custom_call_target="tpu_custom_call" | custom-call | tf_op jit(solution)/shard_map/pallas_call | solution.py:641
  21.0 0.1 collective-permute-start.4
  21.1 3.6 %collective-permute-start.5 = (f32[96,128]{1,0:T(8,128)S(1)}, f32[96,128]{1,0:T(8,128)S(1)}, u32[]{:S(2)}, u32[]{:S(2)}) collective-permute-start(f32[96,128]{1,0:T(8,128)S(1)} %get-tuple-element.41), channel_id=1, source_target_pairs={{4,8},{8,4},{12,16},{16,12},{20,24},{24,20},{28,0},{0,28},{5,9},{9... | collective-permute-start | bytes 147464 | tf_op jit(solution)/shard_map/ppermute | solution.py:657
  24.7 0.5 %collective-permute-done.4.recv_a = f32[96,128]{1,0:T(8,128)S(1)} collective-permute-done((f32[96,128]{1,0:T(8,128)S(1)}, f32[96,128]{1,0:T(8,128)S(1)}, u32[]{:S(2)}, u32[]{:S(2)}) %collective-permute-start.4) | collective-permute-done | bytes 49184 | tf_op jit(solution)/shard_map/ppermute | solution.py:657
  25.2 2.8 %collective-permute-done.5.recv_b = f32[96,128]{1,0:T(8,128)S(1)} collective-permute-done((f32[96,128]{1,0:T(8,128)S(1)}, f32[96,128]{1,0:T(8,128)S(1)}, u32[]{:S(2)}, u32[]{:S(2)}) %collective-permute-start.5) | collective-permute-done | bytes 49184 | tf_op jit(solution)/shard_map/ppermute | solution.py:657
  28.0 1.7 %shard_map.58 = (f32[48,128]{1,0:T(8,128)S(1)}, f32[48,128]{1,0:T(8,128)S(1)}, f32[9,5,8,128]{3,2,1,0:T(8,128)S(1)}, f32[6,5,8,128]{3,2,1,0:T(8,128)S(1)}, f32[19,5,8,128]{3,2,1,0:T(8,128)S(1)}) custom-call(f32[12,5,8,128]{3,2,1,0:T(8,128)S(1)} %get-tuple-element.33.fl, f32[12,5,8,128]{3,2,1,0:T(8,128)S(1)} %get-tuple-element.32.fe, ...), custom_call_target="tpu_custom_call" | custom-call | tf_op jit(solution)/shard_map/pallas_call | solution.py:641
  29.6 0.2 collective-permute-start.6
  29.8 3.5 %collective-permute-start.7 = (f32[48,128]{1,0:T(8,128)S(1)}, f32[48,128]{1,0:T(8,128)S(1)}, u32[]{:S(2)}, u32[]{:S(2)}) collective-permute-start(f32[48,128]{1,0:T(8,128)S(1)} %get-tuple-element.46), channel_id=1, source_target_pairs={{4,8},{8,4},{12,16},{16,12},{20,24},{24,20},{28,0},{0,28},{5,9},{9... | collective-permute-start | bytes 73736 | tf_op jit(solution)/shard_map/ppermute | solution.py:657
  33.4 0.1 collective-permute-done.6.recv_a
  33.5 2.8 %collective-permute-done.7.recv_b = f32[48,128]{1,0:T(8,128)S(1)} collective-permute-done((f32[48,128]{1,0:T(8,128)S(1)}, f32[48,128]{1,0:T(8,128)S(1)}, u32[]{:S(2)}, u32[]{:S(2)}) %collective-permute-start.7) | collective-permute-done | bytes 24608 | tf_op jit(solution)/shard_map/ppermute | solution.py:657
  36.4 2.2 %shard_map.59 = f32[57,4,8,128]{3,2,1,0:T(8,128)} custom-call(f32[12,5,8,128]{3,2,1,0:T(8,128)S(1)} %get-tuple-element.32.fe, f32[9,5,8,128]{3,2,1,0:T(8,128)S(1)} %get-tuple-element.42.hold, f32[6,5,8,128]{3,2,1,0:T(8,128)S(1)} %get-tuple-element.43.ab, f32[19,5,8,128]{3,2,1,0:T(8,128)S(1)} %get-tuple-element.44.kept, ...), custom_call_target="tpu_custom_call" | custom-call | tf_op jit(solution)/shard_map/pallas_call | solution.py:641
  (7 shorter events, 0.0 us)
Async XLA Ops:
  0.0 1.2 %copy-start = (f32[57,4,8,128]{3,2,1,0:T(8,128)S(1)}, f32[57,4,8,128]{3,2,1,0:T(8,128)}, u32[]{:S(2)}) copy-start(f32[57,4,8,128]{3,2,1,0:T(8,128)} %adj.5) | copy-start | bytes 2801668
  1.2 1.0 %copy-start.1 = (bf16[57,4,8,128]{3,2,1,0:T(8,128)(2,1)S(1)}, bf16[57,4,8,128]{3,2,1,0:T(8,128)(2,1)}, u32[]{:S(2)}) copy-start(bf16[57,4,8,128]{3,2,1,0:T(8,128)(2,1)} %late.1) | copy-start | bytes 1400836
  2.2 1.0 %copy-start.2 = (bf16[57,4,8,128]{3,2,1,0:T(8,128)(2,1)S(1)}, bf16[57,4,8,128]{3,2,1,0:T(8,128)(2,1)}, u32[]{:S(2)}) copy-start(bf16[57,4,8,128]{3,2,1,0:T(8,128)(2,1)} %early.1) | copy-start | bytes 1400836
  3.2 0.7 %copy-start.3 = (bf16[3,4,8,128]{3,2,1,0:T(8,128)(2,1)S(1)}, bf16[3,4,8,128]{3,2,1,0:T(8,128)(2,1)}, u32[]{:S(2)}) copy-start(bf16[3,4,8,128]{3,2,1,0:T(8,128)(2,1)} %dip_late.1) | copy-start | bytes 73732
  4.0 0.7 %copy-start.4 = (bf16[3,4,8,128]{3,2,1,0:T(8,128)(2,1)S(1)}, bf16[3,4,8,128]{3,2,1,0:T(8,128)(2,1)}, u32[]{:S(2)}) copy-start(bf16[3,4,8,128]{3,2,1,0:T(8,128)(2,1)} %dip_early.1) | copy-start | bytes 73732
  5.4 3.1 %collective-permute-start = (f32[10,8,128]{2,1,0:T(8,128)S(1)}, f32[10,8,128]{2,1,0:T(8,128)S(1)}, u32[]{:S(2)}, u32[]{:S(2)}) collective-permute-start(f32[10,8,128]{2,1,0:T(8,128)S(1)} %get-tuple-element.28), channel_id=1, source_target_pairs={{0,1},{1,0},{2,3},{3,2},{4,5},{5,4},{6,7},{7,6},{8,9},{9,8},{10,11... | collective-permute-start | bytes 122888 | tf_op jit(solution)/shard_map/ppermute | solution.py:657
  5.9 4.5 %collective-permute-start.1 = (f32[10,8,128]{2,1,0:T(8,128)S(1)}, f32[10,8,128]{2,1,0:T(8,128)S(1)}, u32[]{:S(2)}, u32[]{:S(2)}) collective-permute-start(f32[10,8,128]{2,1,0:T(8,128)S(1)} %get-tuple-element.29), channel_id=1, source_target_pairs={{1,2},{2,1},{3,0},{0,3},{5,6},{6,5},{7,4},{4,7},{9,10},{10,9},{11,... | collective-permute-start | bytes 122888 | tf_op jit(solution)/shard_map/ppermute | solution.py:657
  10.7 5.2 %collective-permute-start.2 = (f32[136,128]{1,0:T(8,128)S(1)}, f32[136,128]{1,0:T(8,128)S(1)}, u32[]{:S(2)}, u32[]{:S(2)}) collective-permute-start(f32[136,128]{1,0:T(8,128)S(1)} %get-tuple-element.35), channel_id=1, source_target_pairs={{0,4},{4,0},{8,12},{12,8},{16,20},{20,16},{24,28},{28,24},{1,5},{5... | collective-permute-start | bytes 208904 | tf_op jit(solution)/shard_map/ppermute | solution.py:657
  12.3 7.0 %collective-permute-start.3 = (f32[136,128]{1,0:T(8,128)S(1)}, f32[136,128]{1,0:T(8,128)S(1)}, u32[]{:S(2)}, u32[]{:S(2)}) collective-permute-start(f32[136,128]{1,0:T(8,128)S(1)} %get-tuple-element.36), channel_id=1, source_target_pairs={{4,8},{8,4},{12,16},{16,12},{20,24},{24,20},{28,0},{0,28},{5,9},{9... | collective-permute-start | bytes 208904 | tf_op jit(solution)/shard_map/ppermute | solution.py:657
  21.0 4.2 %collective-permute-start.4 = (f32[96,128]{1,0:T(8,128)S(1)}, f32[96,128]{1,0:T(8,128)S(1)}, u32[]{:S(2)}, u32[]{:S(2)}) collective-permute-start(f32[96,128]{1,0:T(8,128)S(1)} %get-tuple-element.40), channel_id=1, source_target_pairs={{0,4},{4,0},{8,12},{12,8},{16,20},{20,16},{24,28},{28,24},{1,5},{5... | collective-permute-start | bytes 147464 | tf_op jit(solution)/shard_map/ppermute | solution.py:657
  21.1 6.9 %collective-permute-start.5 = (f32[96,128]{1,0:T(8,128)S(1)}, f32[96,128]{1,0:T(8,128)S(1)}, u32[]{:S(2)}, u32[]{:S(2)}) collective-permute-start(f32[96,128]{1,0:T(8,128)S(1)} %get-tuple-element.41), channel_id=1, source_target_pairs={{4,8},{8,4},{12,16},{16,12},{20,24},{24,20},{28,0},{0,28},{5,9},{9... | collective-permute-start | bytes 147464 | tf_op jit(solution)/shard_map/ppermute | solution.py:657
  29.6 3.9 %collective-permute-start.6 = (f32[48,128]{1,0:T(8,128)S(1)}, f32[48,128]{1,0:T(8,128)S(1)}, u32[]{:S(2)}, u32[]{:S(2)}) collective-permute-start(f32[48,128]{1,0:T(8,128)S(1)} %get-tuple-element.45), channel_id=1, source_target_pairs={{0,4},{4,0},{8,12},{12,8},{16,20},{20,16},{24,28},{28,24},{1,5},{5... | collective-permute-start | bytes 73736 | tf_op jit(solution)/shard_map/ppermute | solution.py:657
  29.8 6.5 %collective-permute-start.7 = (f32[48,128]{1,0:T(8,128)S(1)}, f32[48,128]{1,0:T(8,128)S(1)}, u32[]{:S(2)}, u32[]{:S(2)}) collective-permute-start(f32[48,128]{1,0:T(8,128)S(1)} %get-tuple-element.46), channel_id=1, source_target_pairs={{4,8},{8,4},{12,16},{16,12},{20,24},{24,20},{28,0},{0,28},{5,9},{9... | collective-permute-start | bytes 73736 | tf_op jit(solution)/shard_map/ppermute | solution.py:657

commit v2 on v1

--- a/solution.py
+++ b/solution.py
@@ -332,9 +332,16 @@
     ).astype(F32)
 
 
-def spread_rim(grid, get_h, get_d, target, sign):
-    total = spread_plane(grid, get_h, get_d, sign, CROSS)
-    return [x * (sign * sign) for x in met(total, target)]
+def hand_over(grid, tile, hold, fields, rim, rim_dip, given):
+    total = spread_plane(
+        grid,
+        lambda k, dz: tile.get(hold, k, dz),
+        lambda k, dz: tile.get(fields, 6 + k, dz),
+        -rim_sign(grid),
+        CROSS,
+    )
+    for s, x in enumerate(met(total, [tile.get(rim, rim_dip + d) for d in range(3)])):
+        given[s, tile.index] = x
 
 
 def unpack_rims(grid, first, second, parity, lines, rims, pairs):
@@ -351,19 +358,35 @@
     second[...] = lines[1]
 
 
-def line_count(components, grid):
-    lines = components * grid.tiles
-    return -(-lines // 8) * 8
-
-
 def parity_of(axis):
     return lax.rem(lax.axis_index(axis), 2)
 
 
-def pack_columns_kernel(adj, late, early, dip_late, dip_early, send_c, send_d, own_left, own_right, fl, fe):
+def pack_columns_kernel(
+    adj_in, late_in, early_in, dip_late_in, dip_early_in,
+    send_c, send_d, own_left, own_right, fl, fe, adj,
+    late, early, dip_late, dip_early, sems,
+):
     planes, rows, cols = adj.shape[1:]
     grid = Grid(planes, rows, cols)
-    for saved, dip, out in ((late, dip_late, fl), (early, dip_early, fe)):
+    copies = [
+        pltpu.make_async_copy(a, b, sems.at[i])
+        for i, (a, b) in enumerate(
+            (
+                (dip_late_in, dip_late),
+                (late_in, late),
+                (dip_early_in, dip_early),
+                (early_in, early),
+                (adj_in, adj),
+            )
+        )
+    ]
+    for copy in copies:
+        copy.start()
+    for which, (saved, dip, out) in enumerate(((late, dip_late, fl), (early, dip_early, fe))):
+        copies[2 * which].wait()
+        copies[2 * which + 1].wait()
+
         def step(p, carry):
             flows = [None] * 19
             rho = []
@@ -386,6 +409,7 @@
             return carry
 
         lax.fori_loop(0, planes, step, 0)
+    copies[4].wait()
     pops = adj.shape[0]
     components = pops + 18
     slot = grid.lane // grid.group
@@ -481,7 +505,7 @@
 
 
 def late_kernel(
-    adj, edge, fl, recv_a, recv_b, send_a, send_b, hold, ab, kept, lines, lines_out, rims
+    adj, edge, fl, recv_a, recv_b, send_a, send_b, ab, kept, given, lines, lines_out, rims, hold
 ):
     pops, planes, rows, cols = adj.shape
     grid = Grid(planes, rows, cols)
@@ -495,11 +519,13 @@
         collision_adjoint(grid, tile, load, rims, fl, forces, hold, ab, kept)
 
     grid.over(collide)
+    sign = -rim_sign(grid)
 
     def finish(tile):
         back = spread_inside(grid, tile, hold, fl)
         for s in range(3):
             ab[s, tile.index] = ab[s, tile.index] + (1.0 - tile.get(fl, 9 + s)) * back[s]
+        hand_over(grid, tile, hold, fl, rims, 18, given)
 
     grid.over(finish)
     up, down = parity, 1 - parity
@@ -509,11 +535,10 @@
         lines_out[up, fill : fill + 1, :] = v[rows - 1 : rows, :]
         lines_out[down, fill : fill + 1, :] = v[0:1, :]
 
-    for c in range(9):
+    for c in range(3):
         for t in range(grid.tiles):
-            put(hold[c, t])
+            put(given[c, t])
             fill += 1
-    sign = -rim_sign(grid)
     for kind in range(9):
         for t in range(grid.tiles):
             if kind < 2:
@@ -531,27 +556,20 @@
 
 
 def early_kernel(
-    fl, fe, hold1, ab1, kept1, first_a, first_b, recv_a, recv_b, send_a, send_b, hold, ab, kept,
-    lines, lines2, lines_out, rims, near, mid, rim_mid,
+    fl, fe, ab1, kept1, given1, first_a, first_b, recv_a, recv_b, send_a, send_b, hold, ab, kept,
+    lines, lines2, lines_out, rims, near, mid, rim_mid, given,
 ):
     planes, rows, cols = fl.shape[1] - 1, fl.shape[2], fl.shape[3]
     grid = Grid(planes, rows, cols)
     parity = parity_of("gx")
-    unpack_rims(grid, first_a, first_b, parity, lines, rims, range(15, 27))
-    unpack_rims(grid, recv_a, recv_b, parity, lines2, near, range(18))
-    sign = rim_sign(grid)
+    unpack_rims(grid, first_a, first_b, parity, lines, rims, (15, 16, 17) + tuple(range(21, 27)))
+    unpack_rims(grid, recv_a, recv_b, parity, lines2, near, range(12))
     rest = 1.0 - 1.0 / RELAXATION[2]
+    at_rim = (grid.sub == 0) | (grid.sub == rows - 1)
 
     def complete(tile):
         t = tile.index
-        own_d = lambda k, dz: tile.get(fl, 6 + k, dz)
-        rim_d = lambda k, dz: tile.get(rims, 3 + k, dz)
-        inward = spread_rim(
-            grid, lambda k, dz: tile.get(near, k, dz), rim_d, [own_d(d, 0) for d in range(3)], sign
-        )
-        outward = spread_rim(
-            grid, lambda k, dz: tile.get(hold1, k, dz), own_d, [rim_d(d, 0) for d in range(3)], -sign
-        )
+        inward = [jnp.where(at_rim, tile.get(near, s), 0.0) for s in range(3)]
         alpha = [tile.get(ab1, s) + (1.0 - tile.get(fl, 9 + s)) * inward[s] for s in range(3)]
         beta = [tile.get(ab1, 3 + d) for d in range(3)]
         for q in range(19):
@@ -562,57 +580,53 @@
                 if s == 2:
                     v = v + rest * kept1[q, t]
                 mid[s * 19 + q, t] = v
-        fixes = [(1.0 - tile.get(rims, s)) * outward[s] for s in range(3)]
-        sides = [tile.get(near, 11 + d) for d in range(2)]
+        fixes = [(1.0 - tile.get(rims, s)) * tile.get(given1, s) for s in range(3)]
+        sides = [tile.get(near, 5 + d) for d in range(2)]
         for s in range(2):
-            base = tile.get(near, 9 + s) + fixes[s]
+            base = tile.get(near, 3 + s) + fixes[s]
             for j, (cy, cz) in enumerate(CROSS):
                 rim_mid[s * 5 + j, t] = base if j == 0 else base + mixed((cy, cz), sides)
         for j in range(5):
-            rim_mid[10 + j, t] = tile.get(near, 13 + j) + fixes[2]
+            rim_mid[10 + j, t] = tile.get(near, 7 + j) + fixes[2]
 
     grid.over(complete)
 
     def collide(tile):
         dipole = [tile.get(fe, 6 + d) for d in range(3)]
-        forces = field_forces(grid, tile, fe, rims, 6, 9, dipole)
+        forces = field_forces(grid, tile, fe, rims, 3, 6, dipole)
         load = lambda c, dz: tile.get(mid, c, dz)
         collision_adjoint(grid, tile, load, rim_mid, fe, forces, hold, ab, kept)
 
     grid.over(collide)
+    grid.over(lambda tile: hand_over(grid, tile, hold, fe, rims, 6, given))
     up, down = parity, 1 - parity
     fill = 0
-    for c in range(9):
+    for c in range(3):
         for t in range(grid.tiles):
-            v = hold[c, t]
+            v = given[c, t]
             lines_out[up, fill : fill + 1, :] = v[rows - 1 : rows, :]
             lines_out[down, fill : fill + 1, :] = v[0:1, :]
             fill += 1
     send_rows(grid, up, lines_out, send_a, send_b)
 
 
-def out_kernel(fe, hold, ab, kept, first_a, first_b, recv_a, recv_b, out, lines, lines2, rims, near, total):
+def out_kernel(fe, hold, ab, kept, recv_a, recv_b, out, lines, near, total, staged, sems):
     planes, rows, cols = fe.shape[1] - 1, fe.shape[2], fe.shape[3]
     grid = Grid(planes, rows, cols)
-    parity = parity_of("gx")
-    unpack_rims(grid, first_a, first_b, parity, lines, rims, range(24, 27))
-    unpack_rims(grid, recv_a, recv_b, parity, lines2, near, range(9))
-    sign = rim_sign(grid)
+    unpack_rims(grid, recv_a, recv_b, parity_of("gx"), lines, near, range(3))
+    at_rim = (grid.sub == 0) | (grid.sub == rows - 1)
 
     def finish(tile):
         back = spread_inside(grid, tile, hold, fe)
-        inward = spread_rim(
-            grid,
-            lambda k, dz: tile.get(near, k, dz),
-            lambda k, dz: tile.get(rims, k, dz),
-            [tile.get(fe, 6 + d) for d in range(3)],
-            sign,
-        )
         for s in range(3):
-            total[s, tile.index] = tile.get(ab, s) + (1.0 - tile.get(fe, 9 + s)) * (back[s] + inward[s])
+            back[s] = back[s] + jnp.where(at_rim, tile.get(near, s), 0.0)
+            total[s, tile.index] = tile.get(ab, s) + (1.0 - tile.get(fe, 9 + s)) * back[s]
 
     grid.over(finish)
     is_low, is_high = grid.lane < HALO, grid.lane >= cols - HALO
+
+    def to_out(p):
+        return pltpu.make_async_copy(staged.at[:, p], out.at[:, p], sems.at[p])
 
     def emit(p, carry):
         base = p * grid.width
@@ -630,20 +644,24 @@
                 v = alpha[s] if along is None else alpha[s] + along
                 if s == 2:
                     v = v + (1.0 - 1.0 / RELAXATION[2]) * patched(kept[q, p], kept[q, planes])
-                out[s * 19 + q, p] = v
+                staged[s * 19 + q, p] = v
+        to_out(p).start()
         return carry
 
     lax.fori_loop(0, planes, emit, 0)
-
-
-def call(kernel, outs, scratch, args):
-    whole = pl.BlockSpec(memory_space=pltpu.VMEM)
+    for p in range(planes):
+        to_out(p).wait()
+
+
+def call(kernel, outs, scratch, args, in_hbm=False, out_hbm=False):
+    vmem = pl.BlockSpec(memory_space=pltpu.VMEM)
+    hbm = pl.BlockSpec(memory_space=pltpu.HBM)
     return pl.pallas_call(
         kernel,
         out_shape=[jax.ShapeDtypeStruct(s, F32) for s in outs],
-        in_specs=[whole] * len(args),
-        out_specs=[whole] * len(outs),
-        scratch_shapes=[pltpu.VMEM(s, F32) for s in scratch],
+        in_specs=[hbm if in_hbm else vmem] * len(args),
+        out_specs=[hbm if out_hbm else vmem] * len(outs),
+        scratch_shapes=[pltpu.VMEM(s, F32) if isinstance(s, tuple) else s for s in scratch],
         compiler_params=pltpu.CompilerParams(vmem_limit_bytes=VMEM_BYTES),
     )(*args)
 
@@ -671,48 +689,57 @@
     def both(n):
         return (2,) + lines(n)
 
-    send_c, send_d, own_left, own_right, fl_main, fe_main = call(
+    send_c, send_d, own_left, own_right, fl_main, fe_main, adj = call(
         pack_columns_kernel,
-        [(groups // 2,) + tile] * 2 + [(groups,) + tile] * 2 + [(9, planes) + tile] * 2,
-        [],
+        [(groups // 2,) + tile] * 2
+        + [(groups,) + tile] * 2
+        + [(9, planes) + tile] * 2
+        + [(pops, planes) + tile],
+        [pltpu.VMEM(x.shape, x.dtype) for x in (populations_late, populations_early)]
+        + [pltpu.VMEM(x.shape, x.dtype) for x in (dipoles_late, dipoles_early)]
+        + [pltpu.SemaphoreType.DMA((5,))],
         [adjoint_in, populations_late, populations_early, dipoles_late, dipoles_early],
+        in_hbm=True,
     )
     recv_c, recv_d = swap(send_c, "gy", 0), swap(send_d, "gy", 1)
     send_a, send_b, edge, fl, fe = call(
         pack_rows_kernel,
         [lines(27)] * 2 + [(pops,) + tile] + [(12, tiles) + tile] * 2,
         [both(27)],
-        [adjoint_in, own_left, own_right, recv_c, recv_d, fl_main, fe_main],
+        [adj, own_left, own_right, recv_c, recv_d, fl_main, fe_main],
     )
     first_a, first_b = swap(send_a, "gx", 0), swap(send_b, "gx", 1)
-    saved = [(9, tiles) + tile, (6, tiles) + tile, (19, tiles) + tile]
-    send_a, send_b, hold1, ab1, kept1 = call(
+    hold_shape, ab_shape, kept_shape = [(n, tiles) + tile for n in (9, 6, 19)]
+    three = (3, tiles) + tile
+    send_a, send_b, ab1, kept1, given1 = call(
         late_kernel,
-        [lines(18)] * 2 + saved,
-        [both(27), both(18), (21, tiles) + tile],
-        [adjoint_in, edge, fl, first_a, first_b],
+        [lines(12)] * 2 + [ab_shape, kept_shape, three],
+        [both(27), both(12), (21, tiles) + tile, hold_shape],
+        [adj, edge, fl, first_a, first_b],
     )
     recv_a, recv_b = swap(send_a, "gx", 0), swap(send_b, "gx", 1)
     send_a, send_b, hold, ab, kept = call(
         early_kernel,
-        [lines(9)] * 2 + saved,
+        [lines(3)] * 2 + [hold_shape, ab_shape, kept_shape],
         [
             both(27),
-            both(18),
-            both(9),
+            both(12),
+            both(3),
+            (9, tiles) + tile,
             (12, tiles) + tile,
-            (18, tiles) + tile,
             (pops, tiles) + tile,
             (15, tiles) + tile,
+            three,
         ],
-        [fl, fe, hold1, ab1, kept1, first_a, first_b, recv_a, recv_b],
+        [fl, fe, ab1, kept1, given1, first_a, first_b, recv_a, recv_b],
     )
     recv_a, recv_b = swap(send_a, "gx", 0), swap(send_b, "gx", 1)
     (out,) = call(
         out_kernel,
         [(pops, planes) + tile],
-        [both(27), both(9), (3, tiles) + tile, (9, tiles) + tile, (3, tiles) + tile],
-        [fe, hold, ab, kept, first_a, first_b, recv_a, recv_b],
+        [both(3), three, three, (pops, planes) + tile, pltpu.SemaphoreType.DMA((planes,))],
+        [fe, hold, ab, kept, recv_a, recv_b],
+        out_hbm=True,
     )
     return out
 

time: 38.9 us -> 39.1 us (level)
  Pallas kernels: 6.55 us -> 7.1 us
    pallas_call x5, Pallas kernels: 6.55 us -> 7.1 us  [call(): pl.pallas_call(kernel, out_shape=[jax.ShapeDtypeStruct(s, F32) for s in o...]
  transfers between devices with their start and end apart: 8 -> 8, of which waited for: 6 -> 5; matrix products, arithmetic and copies ran while one was open for 0% -> 0% of each run, Pallas kernels for 0% -> 0%
where the time goes in v2:
time: 39.1 us; the launch traced here: 38.8 us
  starting transfers between devices  15.7 us (40%)
  waiting for transfers between devices  11.2 us (29%)
  Pallas kernels  7.1 us (18%)
  local copies, waits for them, and re-layouts  4.7 us (12%)
    ppermute x8, starting transfers between devices, swap(): return lax.ppermute(block, axis, route)  15.7 us
    ppermute x8, waiting for transfers between devices, swap(): return lax.ppermute(block, axis, route)  11.2 us
    pallas_call x5, Pallas kernels, call(): pl.pallas_call(kernel, out_shape=[jax.ShapeDtypeStruct(s, F32) for s in o...  7.1 us
    unnamed x10, local copies, waits for them, and re-layouts  4.7 us
  transfers between devices with their start and end apart: 8, of which 5 were waited for; matrix products, arithmetic and copies ran while one was open for 0% of the time, Pallas kernels for 0%

profile of v2, /device:TPU:0, one launch (start us, length us, event | category | flops | bytes accessed | tf_op | source)
XLA Modules:
  0.0 38.8 jit_solution(674721628411955256)
XLA Ops:
  0.0 1.2 %copy-done = f32[57,4,8,128]{3,2,1,0:T(8,128)S(1)} copy-done((f32[57,4,8,128]{3,2,1,0:T(8,128)S(1)}, f32[57,4,8,128]{3,2,1,0:T(8,128)}, u32[]{:S(2)}) %copy-start) | copy-done | bytes 933912
  1.2 1.0 %copy-done.1 = bf16[57,4,8,128]{3,2,1,0:T(8,128)(2,1)S(1)} copy-done((bf16[57,4,8,128]{3,2,1,0:T(8,128)(2,1)S(1)}, bf16[57,4,8,128]{3,2,1,0:T(8,128)(2,1)}, u32[]{:S(2)}) %copy-start.1) | copy-done | bytes 466968
  2.2 1.0 %copy-done.2 = bf16[57,4,8,128]{3,2,1,0:T(8,128)(2,1)S(1)} copy-done((bf16[57,4,8,128]{3,2,1,0:T(8,128)(2,1)S(1)}, bf16[57,4,8,128]{3,2,1,0:T(8,128)(2,1)}, u32[]{:S(2)}) %copy-start.2) | copy-done | bytes 466968
  3.2 0.7 %copy-done.3 = bf16[3,4,8,128]{3,2,1,0:T(8,128)(2,1)S(1)} copy-done((bf16[3,4,8,128]{3,2,1,0:T(8,128)(2,1)S(1)}, bf16[3,4,8,128]{3,2,1,0:T(8,128)(2,1)}, u32[]{:S(2)}) %copy-start.3) | copy-done | bytes 24600
  4.0 0.7 %copy-done.4 = bf16[3,4,8,128]{3,2,1,0:T(8,128)(2,1)S(1)} copy-done((bf16[3,4,8,128]{3,2,1,0:T(8,128)(2,1)S(1)}, bf16[3,4,8,128]{3,2,1,0:T(8,128)(2,1)}, u32[]{:S(2)}) %copy-start.4) | copy-done | bytes 24600
  4.7 1.6 %shard_map.55 = (f32[10,8,128]{2,1,0:T(8,128)S(1)}, f32[10,8,128]{2,1,0:T(8,128)S(1)}, f32[20,8,128]{2,1,0:T(8,128)S(1)}, f32[20,8,128]{2,1,0:T(8,128)S(1)}, f32...) custom-call(f32[57,4,8,128]{3,2,1,0:T(8,128)S(1)} %copy-done, ...), custom_call_target="tpu_custom_call" | custom-call | tf_op jit(solution)/shard_map/pallas_call | solution.py:659
  6.3 0.5 %collective-permute-start = (f32[10,8,128]{2,1,0:T(8,128)S(1)}, f32[10,8,128]{2,1,0:T(8,128)S(1)}, u32[]{:S(2)}, u32[]{:S(2)}) collective-permute-start(f32[10,8,128]{2,1,0:T(8,128)S(1)} %get-tuple-element.30), channel_id=1, source_target_pairs={{0,1},{1,0},{2,3},{3,2},{4,5},{5,4},{6,7},{7,6},{8,9},{9,8},{10,11... | collective-permute-start | bytes 122888 | tf_op jit(solution)/shard_map/ppermute | solution.py:675
  6.8 2.6 %collective-permute-start.1 = (f32[10,8,128]{2,1,0:T(8,128)S(1)}, f32[10,8,128]{2,1,0:T(8,128)S(1)}, u32[]{:S(2)}, u32[]{:S(2)}) collective-permute-start(f32[10,8,128]{2,1,0:T(8,128)S(1)} %get-tuple-element.31), channel_id=1, source_target_pairs={{1,2},{2,1},{3,0},{0,3},{5,6},{6,5},{7,4},{4,7},{9,10},{10,9},{11,... | collective-permute-start | bytes 122888 | tf_op jit(solution)/shard_map/ppermute | solution.py:675
  9.5 1.8 %collective-permute-done.1.recv_d = f32[10,8,128]{2,1,0:T(8,128)S(1)} collective-permute-done((f32[10,8,128]{2,1,0:T(8,128)S(1)}, f32[10,8,128]{2,1,0:T(8,128)S(1)}, u32[]{:S(2)}, u32[]{:S(2)}) %collective-permute-start.1) | collective-permute-done | bytes 40992 | tf_op jit(solution)/shard_map/ppermute | solution.py:675
  11.3 0.3 shard_map.56
  11.6 1.6 %collective-permute-start.2 = (f32[136,128]{1,0:T(8,128)S(1)}, f32[136,128]{1,0:T(8,128)S(1)}, u32[]{:S(2)}, u32[]{:S(2)}) collective-permute-start(f32[136,128]{1,0:T(8,128)S(1)} %get-tuple-element.37), channel_id=1, source_target_pairs={{0,4},{4,0},{8,12},{12,8},{16,20},{20,16},{24,28},{28,24},{1,5},{5... | collective-permute-start | bytes 208904 | tf_op jit(solution)/shard_map/ppermute | solution.py:675
  13.2 3.5 %collective-permute-start.3 = (f32[136,128]{1,0:T(8,128)S(1)}, f32[136,128]{1,0:T(8,128)S(1)}, u32[]{:S(2)}, u32[]{:S(2)}) collective-permute-start(f32[136,128]{1,0:T(8,128)S(1)} %get-tuple-element.38), channel_id=1, source_target_pairs={{4,8},{8,4},{12,16},{16,12},{20,24},{24,20},{28,0},{0,28},{5,9},{9... | collective-permute-start | bytes 208904 | tf_op jit(solution)/shard_map/ppermute | solution.py:675
  16.8 0.0 collective-permute-done.2.recv_a.first_a
  16.8 3.4 %collective-permute-done.3.recv_b.first_b = f32[136,128]{1,0:T(8,128)S(1)} collective-permute-done((f32[136,128]{1,0:T(8,128)S(1)}, f32[136,128]{1,0:T(8,128)S(1)}, u32[]{:S(2)}, u32[]{:S(2)}) %collective-permute-start.3) | collective-permute-done | bytes 69664 | tf_op jit(solution)/shard_map/ppermute | solution.py:675
  20.2 1.7 %shard_map.57 = (f32[64,128]{1,0:T(8,128)S(1)}, f32[64,128]{1,0:T(8,128)S(1)}, f32[6,5,8,128]{3,2,1,0:T(8,128)S(1)}, f32[19,5,8,128]{3,2,1,0:T(8,128)S(1)}, f32[3,5,8,128]{3,2,1,0:T(8,128)S(1)}) custom-call(f32[57,4,8,128]{3,2,1,0:T(8,128)S(1)} %get-tuple-element.27.adj, f32[57,8,128]{2,1,0:T(8,128)S(1)} %get-tuple-element.36.edge, ...), custom_call_target="tpu_custom_call" | custom-call | tf_op jit(solution)/shard_map/pallas_call | solution.py:659
  21.9 0.1 collective-permute-start.4
  22.0 3.6 %collective-permute-start.5 = (f32[64,128]{1,0:T(8,128)S(1)}, f32[64,128]{1,0:T(8,128)S(1)}, u32[]{:S(2)}, u32[]{:S(2)}) collective-permute-start(f32[64,128]{1,0:T(8,128)S(1)} %get-tuple-element.43), channel_id=1, source_target_pairs={{4,8},{8,4},{12,16},{16,12},{20,24},{24,20},{28,0},{0,28},{5,9},{9... | collective-permute-start | bytes 98312 | tf_op jit(solution)/shard_map/ppermute | solution.py:675
  25.6 0.3 collective-permute-done.4.recv_a
  25.9 2.8 %collective-permute-done.5.recv_b = f32[64,128]{1,0:T(8,128)S(1)} collective-permute-done((f32[64,128]{1,0:T(8,128)S(1)}, f32[64,128]{1,0:T(8,128)S(1)}, u32[]{:S(2)}, u32[]{:S(2)}) %collective-permute-start.5) | collective-permute-done | bytes 32800 | tf_op jit(solution)/shard_map/ppermute | solution.py:675
  28.7 1.6 %shard_map.58 = (f32[16,128]{1,0:T(8,128)S(1)}, f32[16,128]{1,0:T(8,128)S(1)}, f32[9,5,8,128]{3,2,1,0:T(8,128)S(1)}, f32[6,5,8,128]{3,2,1,0:T(8,128)S(1)}, f32[19,5,8,128]{3,2,1,0:T(8,128)S(1)}) custom-call(f32[12,5,8,128]{3,2,1,0:T(8,128)S(1)} %get-tuple-element.35.fl, f32[12,5,8,128]{3,2,1,0:T(8,128)S(1)} %get-tuple-element.34.fe, ...), custom_call_target="tpu_custom_call" | custom-call | tf_op jit(solution)/shard_map/pallas_call | solution.py:659
  30.3 0.2 collective-permute-start.6
  30.5 3.5 %collective-permute-start.7 = (f32[16,128]{1,0:T(8,128)S(1)}, f32[16,128]{1,0:T(8,128)S(1)}, u32[]{:S(2)}, u32[]{:S(2)}) collective-permute-start(f32[16,128]{1,0:T(8,128)S(1)} %get-tuple-element.48), channel_id=1, source_target_pairs={{4,8},{8,4},{12,16},{16,12},{20,24},{24,20},{28,0},{0,28},{5,9},{9... | collective-permute-start | bytes 24584 | tf_op jit(solution)/shard_map/ppermute | solution.py:675
  34.1 2.8 %collective-permute-done.7.recv_b = f32[16,128]{1,0:T(8,128)S(1)} collective-permute-done((f32[16,128]{1,0:T(8,128)S(1)}, f32[16,128]{1,0:T(8,128)S(1)}, u32[]{:S(2)}, u32[]{:S(2)}) %collective-permute-start.7) | collective-permute-done | bytes 8224 | tf_op jit(solution)/shard_map/ppermute | solution.py:675
  36.9 1.9 %shard_map.59 = f32[57,4,8,128]{3,2,1,0:T(8,128)} custom-call(f32[12,5,8,128]{3,2,1,0:T(8,128)S(1)} %get-tuple-element.34.fe, f32[9,5,8,128]{3,2,1,0:T(8,128)S(1)} %get-tuple-element.44.hold, f32[6,5,8,128]{3,2,1,0:T(8,128)S(1)} %get-tuple-element.45.ab, f32[19,5,8,128]{3,2,1,0:T(8,128)S(1)} %get-tuple-element.46.kept, ...), custom_call_target="tpu_custom_call" | custom-call | tf_op jit(solution)/shard_map/pallas_call | solution.py:659
  (7 shorter events, 0.0 us)
Async XLA Ops:
  0.0 1.2 %copy-start = (f32[57,4,8,128]{3,2,1,0:T(8,128)S(1)}, f32[57,4,8,128]{3,2,1,0:T(8,128)}, u32[]{:S(2)}) copy-start(f32[57,4,8,128]{3,2,1,0:T(8,128)} %adj_in.1) | copy-start | bytes 2801668
  1.2 1.0 %copy-start.1 = (bf16[57,4,8,128]{3,2,1,0:T(8,128)(2,1)S(1)}, bf16[57,4,8,128]{3,2,1,0:T(8,128)(2,1)}, u32[]{:S(2)}) copy-start(bf16[57,4,8,128]{3,2,1,0:T(8,128)(2,1)} %late_in.1) | copy-start | bytes 1400836
  2.2 1.0 %copy-start.2 = (bf16[57,4,8,128]{3,2,1,0:T(8,128)(2,1)S(1)}, bf16[57,4,8,128]{3,2,1,0:T(8,128)(2,1)}, u32[]{:S(2)}) copy-start(bf16[57,4,8,128]{3,2,1,0:T(8,128)(2,1)} %early_in.1) | copy-start | bytes 1400836
  3.2 0.7 %copy-start.3 = (bf16[3,4,8,128]{3,2,1,0:T(8,128)(2,1)S(1)}, bf16[3,4,8,128]{3,2,1,0:T(8,128)(2,1)}, u32[]{:S(2)}) copy-start(bf16[3,4,8,128]{3,2,1,0:T(8,128)(2,1)} %dip_late_in.1) | copy-start | bytes 73732
  4.0 0.7 %copy-start.4 = (bf16[3,4,8,128]{3,2,1,0:T(8,128)(2,1)S(1)}, bf16[3,4,8,128]{3,2,1,0:T(8,128)(2,1)}, u32[]{:S(2)}) copy-start(bf16[3,4,8,128]{3,2,1,0:T(8,128)(2,1)} %dip_early_in.1) | copy-start | bytes 73732
  6.3 3.1 %collective-permute-start = (f32[10,8,128]{2,1,0:T(8,128)S(1)}, f32[10,8,128]{2,1,0:T(8,128)S(1)}, u32[]{:S(2)}, u32[]{:S(2)}) collective-permute-start(f32[10,8,128]{2,1,0:T(8,128)S(1)} %get-tuple-element.30), channel_id=1, source_target_pairs={{0,1},{1,0},{2,3},{3,2},{4,5},{5,4},{6,7},{7,6},{8,9},{9,8},{10,11... | collective-permute-start | bytes 122888 | tf_op jit(solution)/shard_map/ppermute | solution.py:675
  6.8 4.5 %collective-permute-start.1 = (f32[10,8,128]{2,1,0:T(8,128)S(1)}, f32[10,8,128]{2,1,0:T(8,128)S(1)}, u32[]{:S(2)}, u32[]{:S(2)}) collective-permute-start(f32[10,8,128]{2,1,0:T(8,128)S(1)} %get-tuple-element.31), channel_id=1, source_target_pairs={{1,2},{2,1},{3,0},{0,3},{5,6},{6,5},{7,4},{4,7},{9,10},{10,9},{11,... | collective-permute-start | bytes 122888 | tf_op jit(solution)/shard_map/ppermute | solution.py:675
  11.6 5.2 %collective-permute-start.2 = (f32[136,128]{1,0:T(8,128)S(1)}, f32[136,128]{1,0:T(8,128)S(1)}, u32[]{:S(2)}, u32[]{:S(2)}) collective-permute-start(f32[136,128]{1,0:T(8,128)S(1)} %get-tuple-element.37), channel_id=1, source_target_pairs={{0,4},{4,0},{8,12},{12,8},{16,20},{20,16},{24,28},{28,24},{1,5},{5... | collective-permute-start | bytes 208904 | tf_op jit(solution)/shard_map/ppermute | solution.py:675
  13.2 7.0 %collective-permute-start.3 = (f32[136,128]{1,0:T(8,128)S(1)}, f32[136,128]{1,0:T(8,128)S(1)}, u32[]{:S(2)}, u32[]{:S(2)}) collective-permute-start(f32[136,128]{1,0:T(8,128)S(1)} %get-tuple-element.38), channel_id=1, source_target_pairs={{4,8},{8,4},{12,16},{16,12},{20,24},{24,20},{28,0},{0,28},{5,9},{9... | collective-permute-start | bytes 208904 | tf_op jit(solution)/shard_map/ppermute | solution.py:675
  21.9 4.0 %collective-permute-start.4 = (f32[64,128]{1,0:T(8,128)S(1)}, f32[64,128]{1,0:T(8,128)S(1)}, u32[]{:S(2)}, u32[]{:S(2)}) collective-permute-start(f32[64,128]{1,0:T(8,128)S(1)} %get-tuple-element.42), channel_id=1, source_target_pairs={{0,4},{4,0},{8,12},{12,8},{16,20},{20,16},{24,28},{28,24},{1,5},{5... | collective-permute-start | bytes 98312 | tf_op jit(solution)/shard_map/ppermute | solution.py:675
  22.0 6.7 %collective-permute-start.5 = (f32[64,128]{1,0:T(8,128)S(1)}, f32[64,128]{1,0:T(8,128)S(1)}, u32[]{:S(2)}, u32[]{:S(2)}) collective-permute-start(f32[64,128]{1,0:T(8,128)S(1)} %get-tuple-element.43), channel_id=1, source_target_pairs={{4,8},{8,4},{12,16},{16,12},{20,24},{24,20},{28,0},{0,28},{5,9},{9... | collective-permute-start | bytes 98312 | tf_op jit(solution)/shard_map/ppermute | solution.py:675
  30.3 3.8 %collective-permute-start.6 = (f32[16,128]{1,0:T(8,128)S(1)}, f32[16,128]{1,0:T(8,128)S(1)}, u32[]{:S(2)}, u32[]{:S(2)}) collective-permute-start(f32[16,128]{1,0:T(8,128)S(1)} %get-tuple-element.47), channel_id=1, source_target_pairs={{0,4},{4,0},{8,12},{12,8},{16,20},{20,16},{24,28},{28,24},{1,5},{5... | collective-permute-start | bytes 24584 | tf_op jit(solution)/shard_map/ppermute | solution.py:675
  30.5 6.3 %collective-permute-start.7 = (f32[16,128]{1,0:T(8,128)S(1)}, f32[16,128]{1,0:T(8,128)S(1)}, u32[]{:S(2)}, u32[]{:S(2)}) collective-permute-start(f32[16,128]{1,0:T(8,128)S(1)} %get-tuple-element.48), channel_id=1, source_target_pairs={{4,8},{8,4},{12,16},{16,12},{20,24},{24,20},{28,0},{0,28},{5,9},{9... | collective-permute-start | bytes 24584 | tf_op jit(solution)/shard_map/ppermute | solution.py:675

commit v3 on v2

--- a/solution.py
+++ b/solution.py
@@ -663,7 +663,7 @@
         out_specs=[hbm if out_hbm else vmem] * len(outs),
         scratch_shapes=[pltpu.VMEM(s, F32) if isinstance(s, tuple) else s for s in scratch],
         compiler_params=pltpu.CompilerParams(vmem_limit_bytes=VMEM_BYTES),
-    )(*args)
+    )(*[pltpu.with_memory_space_constraint(x, pltpu.HBM) if in_hbm else x for x in args])
 
 
 def swap(block, axis, offset):

time: 39.1 us -> 34.5 us (0.88)
  local copies, waits for them, and re-layouts: 4.7 us -> 0 us
    unnamed x10 -> x0, local copies, waits for them, and re-layouts: 4.7 us -> none
where the time goes in v3:
time: 34.5 us; the launch traced here: 34.4 us
  starting transfers between devices  15.7 us (46%)
  waiting for transfers between devices  11.2 us (32%)
  Pallas kernels  7.45 us (22%)
    ppermute x8, starting transfers between devices, swap(): return lax.ppermute(block, axis, route)  15.7 us
    ppermute x8, waiting for transfers between devices, swap(): return lax.ppermute(block, axis, route)  11.2 us
    pallas_call x5, Pallas kernels, call(): pl.pallas_call(kernel, out_shape=[jax.ShapeDtypeStruct(s, F32) for s in o...  7.45 us
  transfers between devices with their start and end apart: 8, of which 5 were waited for; matrix products, arithmetic and copies ran while one was open for 0% of the time, Pallas kernels for 0%

profile of v3, /device:TPU:0, one launch (start us, length us, event | category | flops | bytes accessed | tf_op | source)
XLA Modules:
  0.0 34.4 jit_solution(8863480502493461468)
XLA Ops:
  0.0 2.0 %shard_map.55 = (f32[10,8,128]{2,1,0:T(8,128)S(1)}, f32[10,8,128]{2,1,0:T(8,128)S(1)}, f32[20,8,128]{2,1,0:T(8,128)S(1)}, f32[20,8,128]{2,1,0:T(8,128)S(1)}, f32...) custom-call(f32[57,4,8,128]{3,2,1,0:T(8,128)} %adj_in.1, ...), custom_call_target="tpu_custom_call" | custom-call | tf_op jit(solution)/shard_map/pallas_call | solution.py:659
  2.0 0.5 %collective-permute-start = (f32[10,8,128]{2,1,0:T(8,128)S(1)}, f32[10,8,128]{2,1,0:T(8,128)S(1)}, u32[]{:S(2)}, u32[]{:S(2)}) collective-permute-start(f32[10,8,128]{2,1,0:T(8,128)S(1)} %get-tuple-element.30), channel_id=1, source_target_pairs={{0,1},{1,0},{2,3},{3,2},{4,5},{5,4},{6,7},{7,6},{8,9},{9,8},{10,11... | collective-permute-start | bytes 122888 | tf_op jit(solution)/shard_map/ppermute | solution.py:675
  2.5 2.6 %collective-permute-start.1 = (f32[10,8,128]{2,1,0:T(8,128)S(1)}, f32[10,8,128]{2,1,0:T(8,128)S(1)}, u32[]{:S(2)}, u32[]{:S(2)}) collective-permute-start(f32[10,8,128]{2,1,0:T(8,128)S(1)} %get-tuple-element.31), channel_id=1, source_target_pairs={{1,2},{2,1},{3,0},{0,3},{5,6},{6,5},{7,4},{4,7},{9,10},{10,9},{11,... | collective-permute-start | bytes 122888 | tf_op jit(solution)/shard_map/ppermute | solution.py:675
  5.1 0.0 collective-permute-done.recv_c
  5.1 1.8 %collective-permute-done.1.recv_d = f32[10,8,128]{2,1,0:T(8,128)S(1)} collective-permute-done((f32[10,8,128]{2,1,0:T(8,128)S(1)}, f32[10,8,128]{2,1,0:T(8,128)S(1)}, u32[]{:S(2)}, u32[]{:S(2)}) %collective-permute-start.1) | collective-permute-done | bytes 40992 | tf_op jit(solution)/shard_map/ppermute | solution.py:675
  6.9 0.3 shard_map.56
  7.2 1.6 %collective-permute-start.2 = (f32[136,128]{1,0:T(8,128)S(1)}, f32[136,128]{1,0:T(8,128)S(1)}, u32[]{:S(2)}, u32[]{:S(2)}) collective-permute-start(f32[136,128]{1,0:T(8,128)S(1)} %get-tuple-element.37), channel_id=1, source_target_pairs={{0,4},{4,0},{8,12},{12,8},{16,20},{20,16},{24,28},{28,24},{1,5},{5... | collective-permute-start | bytes 208904 | tf_op jit(solution)/shard_map/ppermute | solution.py:675
  8.9 3.5 %collective-permute-start.3 = (f32[136,128]{1,0:T(8,128)S(1)}, f32[136,128]{1,0:T(8,128)S(1)}, u32[]{:S(2)}, u32[]{:S(2)}) collective-permute-start(f32[136,128]{1,0:T(8,128)S(1)} %get-tuple-element.38), channel_id=1, source_target_pairs={{4,8},{8,4},{12,16},{16,12},{20,24},{24,20},{28,0},{0,28},{5,9},{9... | collective-permute-start | bytes 208904 | tf_op jit(solution)/shard_map/ppermute | solution.py:675
  12.4 0.0 collective-permute-done.2.recv_a.first_a
  12.4 3.4 %collective-permute-done.3.recv_b.first_b = f32[136,128]{1,0:T(8,128)S(1)} collective-permute-done((f32[136,128]{1,0:T(8,128)S(1)}, f32[136,128]{1,0:T(8,128)S(1)}, u32[]{:S(2)}, u32[]{:S(2)}) %collective-permute-start.3) | collective-permute-done | bytes 69664 | tf_op jit(solution)/shard_map/ppermute | solution.py:675
  15.9 1.7 %shard_map.57 = (f32[64,128]{1,0:T(8,128)S(1)}, f32[64,128]{1,0:T(8,128)S(1)}, f32[6,5,8,128]{3,2,1,0:T(8,128)S(1)}, f32[19,5,8,128]{3,2,1,0:T(8,128)S(1)}, f32[3,5,8,128]{3,2,1,0:T(8,128)S(1)}) custom-call(f32[57,4,8,128]{3,2,1,0:T(8,128)S(1)} %get-tuple-element.27.adj, f32[57,8,128]{2,1,0:T(8,128)S(1)} %get-tuple-element.36.edge, ...), custom_call_target="tpu_custom_call" | custom-call | tf_op jit(solution)/shard_map/pallas_call | solution.py:659
  17.6 0.1 collective-permute-start.4
  17.7 3.6 %collective-permute-start.5 = (f32[64,128]{1,0:T(8,128)S(1)}, f32[64,128]{1,0:T(8,128)S(1)}, u32[]{:S(2)}, u32[]{:S(2)}) collective-permute-start(f32[64,128]{1,0:T(8,128)S(1)} %get-tuple-element.43), channel_id=1, source_target_pairs={{4,8},{8,4},{12,16},{16,12},{20,24},{24,20},{28,0},{0,28},{5,9},{9... | collective-permute-start | bytes 98312 | tf_op jit(solution)/shard_map/ppermute | solution.py:675
  21.3 0.3 collective-permute-done.4.recv_a
  21.6 2.8 %collective-permute-done.5.recv_b = f32[64,128]{1,0:T(8,128)S(1)} collective-permute-done((f32[64,128]{1,0:T(8,128)S(1)}, f32[64,128]{1,0:T(8,128)S(1)}, u32[]{:S(2)}, u32[]{:S(2)}) %collective-permute-start.5) | collective-permute-done | bytes 32800 | tf_op jit(solution)/shard_map/ppermute | solution.py:675
  24.3 1.6 %shard_map.58 = (f32[16,128]{1,0:T(8,128)S(1)}, f32[16,128]{1,0:T(8,128)S(1)}, f32[9,5,8,128]{3,2,1,0:T(8,128)S(1)}, f32[6,5,8,128]{3,2,1,0:T(8,128)S(1)}, f32[19,5,8,128]{3,2,1,0:T(8,128)S(1)}) custom-call(f32[12,5,8,128]{3,2,1,0:T(8,128)S(1)} %get-tuple-element.35.fl, f32[12,5,8,128]{3,2,1,0:T(8,128)S(1)} %get-tuple-element.34.fe, ...), custom_call_target="tpu_custom_call" | custom-call | tf_op jit(solution)/shard_map/pallas_call | solution.py:659
  25.9 0.2 collective-permute-start.6
  26.2 3.5 %collective-permute-start.7 = (f32[16,128]{1,0:T(8,128)S(1)}, f32[16,128]{1,0:T(8,128)S(1)}, u32[]{:S(2)}, u32[]{:S(2)}) collective-permute-start(f32[16,128]{1,0:T(8,128)S(1)} %get-tuple-element.48), channel_id=1, source_target_pairs={{4,8},{8,4},{12,16},{16,12},{20,24},{24,20},{28,0},{0,28},{5,9},{9... | collective-permute-start | bytes 24584 | tf_op jit(solution)/shard_map/ppermute | solution.py:675
  29.7 0.0 collective-permute-done.6.recv_a
  29.7 2.8 %collective-permute-done.7.recv_b = f32[16,128]{1,0:T(8,128)S(1)} collective-permute-done((f32[16,128]{1,0:T(8,128)S(1)}, f32[16,128]{1,0:T(8,128)S(1)}, u32[]{:S(2)}, u32[]{:S(2)}) %collective-permute-start.7) | collective-permute-done | bytes 8224 | tf_op jit(solution)/shard_map/ppermute | solution.py:675
  32.5 1.9 %shard_map.59 = f32[57,4,8,128]{3,2,1,0:T(8,128)} custom-call(f32[12,5,8,128]{3,2,1,0:T(8,128)S(1)} %get-tuple-element.34.fe, f32[9,5,8,128]{3,2,1,0:T(8,128)S(1)} %get-tuple-element.44.hold, f32[6,5,8,128]{3,2,1,0:T(8,128)S(1)} %get-tuple-element.45.ab, f32[19,5,8,128]{3,2,1,0:T(8,128)S(1)} %get-tuple-element.46.kept, ...), custom_call_target="tpu_custom_call" | custom-call | tf_op jit(solution)/shard_map/pallas_call | solution.py:659
Async XLA Ops:
  2.0 3.1 %collective-permute-start = (f32[10,8,128]{2,1,0:T(8,128)S(1)}, f32[10,8,128]{2,1,0:T(8,128)S(1)}, u32[]{:S(2)}, u32[]{:S(2)}) collective-permute-start(f32[10,8,128]{2,1,0:T(8,128)S(1)} %get-tuple-element.30), channel_id=1, source_target_pairs={{0,1},{1,0},{2,3},{3,2},{4,5},{5,4},{6,7},{7,6},{8,9},{9,8},{10,11... | collective-permute-start | bytes 122888 | tf_op jit(solution)/shard_map/ppermute | solution.py:675
  2.5 4.5 %collective-permute-start.1 = (f32[10,8,128]{2,1,0:T(8,128)S(1)}, f32[10,8,128]{2,1,0:T(8,128)S(1)}, u32[]{:S(2)}, u32[]{:S(2)}) collective-permute-start(f32[10,8,128]{2,1,0:T(8,128)S(1)} %get-tuple-element.31), channel_id=1, source_target_pairs={{1,2},{2,1},{3,0},{0,3},{5,6},{6,5},{7,4},{4,7},{9,10},{10,9},{11,... | collective-permute-start | bytes 122888 | tf_op jit(solution)/shard_map/ppermute | solution.py:675
  7.2 5.2 %collective-permute-start.2 = (f32[136,128]{1,0:T(8,128)S(1)}, f32[136,128]{1,0:T(8,128)S(1)}, u32[]{:S(2)}, u32[]{:S(2)}) collective-permute-start(f32[136,128]{1,0:T(8,128)S(1)} %get-tuple-element.37), channel_id=1, source_target_pairs={{0,4},{4,0},{8,12},{12,8},{16,20},{20,16},{24,28},{28,24},{1,5},{5... | collective-permute-start | bytes 208904 | tf_op jit(solution)/shard_map/ppermute | solution.py:675
  8.9 7.0 %collective-permute-start.3 = (f32[136,128]{1,0:T(8,128)S(1)}, f32[136,128]{1,0:T(8,128)S(1)}, u32[]{:S(2)}, u32[]{:S(2)}) collective-permute-start(f32[136,128]{1,0:T(8,128)S(1)} %get-tuple-element.38), channel_id=1, source_target_pairs={{4,8},{8,4},{12,16},{16,12},{20,24},{24,20},{28,0},{0,28},{5,9},{9... | collective-permute-start | bytes 208904 | tf_op jit(solution)/shard_map/ppermute | solution.py:675
  17.6 4.0 %collective-permute-start.4 = (f32[64,128]{1,0:T(8,128)S(1)}, f32[64,128]{1,0:T(8,128)S(1)}, u32[]{:S(2)}, u32[]{:S(2)}) collective-permute-start(f32[64,128]{1,0:T(8,128)S(1)} %get-tuple-element.42), channel_id=1, source_target_pairs={{0,4},{4,0},{8,12},{12,8},{16,20},{20,16},{24,28},{28,24},{1,5},{5... | collective-permute-start | bytes 98312 | tf_op jit(solution)/shard_map/ppermute | solution.py:675
  17.7 6.7 %collective-permute-start.5 = (f32[64,128]{1,0:T(8,128)S(1)}, f32[64,128]{1,0:T(8,128)S(1)}, u32[]{:S(2)}, u32[]{:S(2)}) collective-permute-start(f32[64,128]{1,0:T(8,128)S(1)} %get-tuple-element.43), channel_id=1, source_target_pairs={{4,8},{8,4},{12,16},{16,12},{20,24},{24,20},{28,0},{0,28},{5,9},{9... | collective-permute-start | bytes 98312 | tf_op jit(solution)/shard_map/ppermute | solution.py:675
  25.9 3.8 %collective-permute-start.6 = (f32[16,128]{1,0:T(8,128)S(1)}, f32[16,128]{1,0:T(8,128)S(1)}, u32[]{:S(2)}, u32[]{:S(2)}) collective-permute-start(f32[16,128]{1,0:T(8,128)S(1)} %get-tuple-element.47), channel_id=1, source_target_pairs={{0,4},{4,0},{8,12},{12,8},{16,20},{20,16},{24,28},{28,24},{1,5},{5... | collective-permute-start | bytes 24584 | tf_op jit(solution)/shard_map/ppermute | solution.py:675
  26.2 6.3 %collective-permute-start.7 = (f32[16,128]{1,0:T(8,128)S(1)}, f32[16,128]{1,0:T(8,128)S(1)}, u32[]{:S(2)}, u32[]{:S(2)}) collective-permute-start(f32[16,128]{1,0:T(8,128)S(1)} %get-tuple-element.48), channel_id=1, source_target_pairs={{4,8},{8,4},{12,16},{16,12},{20,24},{24,20},{28,0},{0,28},{5,9},{9... | collective-permute-start | bytes 24584 | tf_op jit(solution)/shard_map/ppermute | solution.py:675

commit v4 on v3

--- a/solution.py
+++ b/solution.py
@@ -34,6 +34,12 @@
 AHEAD = tuple(INDEX[(1,) + yz] for yz in CROSS)
 BEHIND = tuple(INDEX[(-1,) + yz] for yz in CROSS)
 SIDE = ((1, 0), (-1, 0), (0, 1), (0, -1), (1, 1), (-1, -1), (1, -1), (-1, 1))
+PSI_DIP = (9, 10, 11, 6, 7, 8)
+FIRST_LINES = 15 + 6 + 12 + 6
+KEPT_LINES = tuple(range(15, 18)) + tuple(range(21, 39))
+RIM_EARLY, RIM_FAR = 3, 15
+LEVEL = tuple(q for q in range(19) if VELOCITY[q][0] == 0)
+SECOND_LINES = 3 + 5 + 4 + 5 + 5 + 9
 F32 = jnp.float32
 VMEM_BYTES = 40 * 1024 * 1024
 HALO = 4
@@ -141,25 +147,22 @@
     return a[0] * b[0] + a[1] * b[1] + a[2] * b[2]
 
 
-def field_forces(grid, tile, fields, rim, rim_psi, rim_dip, dipole):
+def field_forces(grid, loads, across, dipole):
     memo = {}
 
-    def source(name, dz, edge):
-        key = (name, dz, edge)
+    def source(name, dz, place):
+        key = (name, dz, place)
         if key in memo:
             return memo[key]
-        if edge:
-            load = lambda c: tile.get(rim, (rim_psi + c) if c < 3 else (rim_dip + c - 3), dz)
+        if isinstance(name, int):
+            v = loads[place](name, dz)
+        elif name == "chi":
+            v = source(0, dz, place) - source(1, dz, place)
+        elif name[0] == "V":
+            v = source(2, dz, place) * source(3 + name[1], dz, place)
         else:
-            load = lambda c: tile.get(fields, (9 + c) if c < 3 else (6 + c - 3), dz)
-        if isinstance(name, int):
-            v = load(name)
-        elif name == "chi":
-            v = source(0, dz, edge) - source(1, dz, edge)
-        elif name[0] == "V":
-            v = source(2, dz, edge) * source(3 + name[1], dz, edge)
-        else:
-            v = mixed(name[1], [source(("V", d), dz, edge) if name[1][d] else None for d in range(3)])
+            c = name[1]
+            v = mixed(c, [source(("V", d), dz, place) if c[d] else None for d in range(3)])
         memo[key] = v
         return v
 
@@ -170,9 +173,9 @@
         if c[1] != 0:
             v = grid.roll_cols(shifted(name, (c[0], 0, c[2])), c[1])
         elif c[0] != 0:
-            v = grid.at_row(source(name, c[2], False), source(name, c[2], True), c[0])
+            v = across(lambda place, dz: source(name, dz, place), c[0], c[2])
         else:
-            v = source(name, c[2], False)
+            v = source(name, c[2], 0)
         memo[key] = v
         return v
 
@@ -209,14 +212,70 @@
     return k0, k1, k2
 
 
-def collision_adjoint(grid, tile, load, rim, fields, forces, hold, ab, kept):
-    u = [tile.get(fields, 3 + d) for d in range(3)]
-    rho = [tile.get(fields, s) for s in range(3)]
+def brick_forces(grid, tile, fields, rim, rim_psi, rim_dip):
+    def own(c, dz):
+        return tile.get(fields, (9 + c) if c < 3 else (3 + c), dz)
+
+    def beyond(c, dz):
+        return tile.get(rim, (rim_psi + c) if c < 3 else (rim_dip + c - 3), dz)
+
+    def across(get, cx, dz):
+        return grid.at_row(get(0, dz), get(1, dz), cx)
+
+    return field_forces(grid, (own, beyond), across, [own(3 + d, 0) for d in range(3)])
+
+
+def rim_forces(grid, tile, fields, rim, psi1, dip1, psi2, dip2):
+    outward = jnp.where(grid.sub < grid.rows // 2, -1.0, 1.0).astype(F32)
+
+    def loader(ref, psi, dip):
+        def load(c, dz):
+            v = tile.get(ref, (psi + c) if c < 3 else (dip + c - 3), dz)
+            return v * outward if c == 3 else v
+
+        return load
+
+    loads = {0: loader(rim, psi1, dip1), 1: loader(rim, psi2, dip2), -1: loader(fields, 9, 6)}
+    dipole = [loads[0](3 + d, 0) for d in range(3)]
+    return field_forces(grid, loads, lambda get, cx, dz: get(cx, dz), dipole)
+
+
+def collision_adjoint(streamed_of, rho, u, psi, forces):
     inverse_sum = 1.0 / (rho[0] + rho[1] + rho[2])
     grad_u = [None] * 3
-    alphas = []
+    alphas, held = [], []
+    for s in range(3):
+        streamed = streamed_of(s)
+        diff, total = {}, {}
+        for c, w in axis_pairs():
+            a, b = streamed[INDEX[c]], streamed[INDEX[tuple(-i for i in c)]]
+            diff[c], total[c] = a - b, a + b
+        m1, m2 = first_and_second(diff, total)
+        m0 = W0 * streamed[16]
+        for c, w in axis_pairs():
+            m0 = m0 + w * total[c]
+        inverse = 1.0 / rho[s]
+        ratio = psi[s] * inverse
+        tau = RELAXATION[s]
+        k = forces[s]
+        v = [u[d] + (tau * ratio) * k[d] for d in range(3)]
+        mv = turned(m2, v)
+        g = [3.0 * (m1[d] + 3.0 * mv[d] - m0 * v[d]) for d in range(3)]
+        feq = m0 + 3.0 * dot(m1, v) + 4.5 * dot(mv, v) - 1.5 * m0 * dot(v, v)
+        alphas.append(feq * (1.0 / tau) + dot(g, k) * (1.0 - psi[s] - ratio))
+        scaled = rho[s] * (1.0 / tau)
+        for d in range(3):
+            grad_u[d] = plus(grad_u[d], scaled * g[d])
+            held.append(psi[s] * g[d])
+    beta = [grad_u[d] * inverse_sum for d in range(3)]
+    along = dot(beta, u)
+    return held, [a - along for a in alphas], beta
+
+
+def brick_collision(grid, tile, load, rim, fields, forces, hold, ab, kept):
     t = tile.index
-    for s in range(3):
+
+    def streamed_of(s):
         streamed = []
         for q in range(19):
             c = VELOCITY[q]
@@ -229,32 +288,14 @@
             streamed.append(v)
             if s == 2:
                 kept[q, t] = v
-        diff, total = {}, {}
-        for c, w in axis_pairs():
-            a, b = streamed[INDEX[c]], streamed[INDEX[tuple(-i for i in c)]]
-            diff[c], total[c] = a - b, a + b
-        m1, m2 = first_and_second(diff, total)
-        m0 = W0 * streamed[16]
-        for c, w in axis_pairs():
-            m0 = m0 + w * total[c]
-        psi = tile.get(fields, 9 + s)
-        inverse = 1.0 / rho[s]
-        ratio = psi * inverse
-        tau = RELAXATION[s]
-        k = forces[s]
-        v = [u[d] + (tau * ratio) * k[d] for d in range(3)]
-        mv = turned(m2, v)
-        g = [3.0 * (m1[d] + 3.0 * mv[d] - m0 * v[d]) for d in range(3)]
-        feq = m0 + 3.0 * dot(m1, v) + 4.5 * dot(mv, v) - 1.5 * m0 * dot(v, v)
-        alphas.append(feq * (1.0 / tau) + dot(g, k) * (1.0 - psi - ratio))
-        scaled = rho[s] * (1.0 / tau)
-        for d in range(3):
-            grad_u[d] = plus(grad_u[d], scaled * g[d])
-            hold[3 * s + d, t] = psi * g[d]
-    beta = [grad_u[d] * inverse_sum for d in range(3)]
-    along = dot(beta, u)
+        return streamed
+
+    rho, u, psi = [[tile.get(fields, at + d) for d in range(3)] for at in (0, 3, 9)]
+    held, alpha, beta = collision_adjoint(streamed_of, rho, u, psi, forces)
+    for k in range(9):
+        hold[k, t] = held[k]
     for s in range(3):
-        ab[s, t] = alphas[s] - along
+        ab[s, t] = alpha[s]
         ab[3 + s, t] = beta[s]
 
 
@@ -488,6 +529,13 @@
     def put(slot_at, v, row):
         lines[slot_at, fill : fill + 1, :] = v[row : row + 1, :]
 
+    def put_both(out, c, depth):
+        nonlocal fill
+        for t in range(grid.tiles):
+            put(up, out[c, t], rows - 1 - depth)
+            put(down, out[c, t], depth)
+            fill += 1
+
     for s in range(3):
         for j in range(5):
             for t in range(grid.tiles):
@@ -495,12 +543,12 @@
                 put(up, adj[behind, t] if t < planes else edge[behind], rows - 1)
                 put(down, adj[ahead, t] if t < planes else edge[ahead], 0)
                 fill += 1
-    for out in (fl, fe):
-        for c in (9, 10, 11, 6, 7, 8):
-            for t in range(grid.tiles):
-                put(up, out[c, t], rows - 1)
-                put(down, out[c, t], 0)
-                fill += 1
+    for c in PSI_DIP:
+        put_both(fl, c, 0)
+    for c in range(12):
+        put_both(fe, c, 0)
+    for c in PSI_DIP:
+        put_both(fe, c, 1)
     send_rows(grid, up, lines, send_a, send_b)
 
 
@@ -513,13 +561,11 @@
     unpack_rims(grid, recv_a, recv_b, parity, lines, rims, range(21))
 
     def collide(tile):
-        dipole = [tile.get(fl, 6 + d) for d in range(3)]
-        forces = field_forces(grid, tile, fl, rims, 15, 18, dipole)
+        forces = brick_forces(grid, tile, fl, rims, 15, 18)
         load = lambda c, dz: tile.split(adj, edge, c, dz)
-        collision_adjoint(grid, tile, load, rims, fl, forces, hold, ab, kept)
+        brick_collision(grid, tile, load, rims, fl, forces, hold, ab, kept)
 
     grid.over(collide)
-    sign = -rim_sign(grid)
 
     def finish(tile):
         back = spread_inside(grid, tile, hold, fl)
@@ -531,41 +577,78 @@
     up, down = parity, 1 - parity
     fill = 0
 
-    def put(v):
-        lines_out[up, fill : fill + 1, :] = v[rows - 1 : rows, :]
-        lines_out[down, fill : fill + 1, :] = v[0:1, :]
+    def put(make, depth=0):
+        nonlocal fill
+        for t in range(grid.tiles):
+            v = make(t)
+            lines_out[up, fill : fill + 1, :] = v[rows - 1 - depth : rows - depth, :]
+            lines_out[down, fill : fill + 1, :] = v[depth : depth + 1, :]
+            fill += 1
+
+    low = grid.sub < rows // 2
+    inward = jnp.where(low, 1.0, -1.0).astype(F32)
+    rest = 1.0 - 1.0 / RELAXATION[2]
+
+    def crossing(j):
+        cy, cz = CROSS[j]
+
+        def make(t):
+            v = rest * jnp.where(low, kept[AHEAD[j], t], kept[BEHIND[j], t])
+            v = v + (ab[2, t] + inward * ab[3, t])
+            return v + mixed((cy, cz), (ab[4, t], ab[5, t])) if j else v
+
+        return make
+
+    def level(q):
+        def make(t):
+            v = rest * kept[q, t] + ab[2, t]
+            return v + mixed(VELOCITY[q], [ab[3 + d, t] for d in range(3)]) if q != 16 else v
+
+        return make
 
     for c in range(3):
-        for t in range(grid.tiles):
-            put(given[c, t])
-            fill += 1
-    for kind in range(9):
-        for t in range(grid.tiles):
-            if kind < 2:
-                put(ab[kind, t] + sign * ab[3, t])
-            elif kind < 4:
-                put(ab[2 + kind, t])
-            else:
-                cy, cz = CROSS[kind - 4]
-                part = ab[2, t] + sign * ab[3, t]
-                if cy or cz:
-                    part = part + mixed((cy, cz), (ab[4, t], ab[5, t]))
-                put((1.0 - 1.0 / RELAXATION[2]) * grid.sides(kept[AHEAD[kind - 4], t], kept[BEHIND[kind - 4], t]) + part)
-            fill += 1
+        put(lambda t: given[c, t])
+    for c in (0, 1, 3, 4, 5):
+        put(lambda t: ab[c, t])
+    for c in range(2):
+        put(lambda t: ab[c, t] + inward * ab[3, t], 1)
+    for c in (4, 5):
+        put(lambda t: ab[c, t], 1)
+    for depth in range(2):
+        for j in range(5):
+            put(crossing(j), depth)
+    for q in LEVEL:
+        put(level(q))
     send_rows(grid, up, lines_out, send_a, send_b)
 
 
+def forces_kernel(fe, recv_a, recv_b, after, forces, forces_rim, rims, lines):
+    planes, rows, cols = fe.shape[1] - 1, fe.shape[2], fe.shape[3]
+    grid = Grid(planes, rows, cols)
+    unpack_rims(grid, recv_a, recv_b, parity_of("gx"), lines, rims, KEPT_LINES)
+    psi, dip = RIM_EARLY + 9, RIM_EARLY + 6
+
+    def both(tile):
+        brick = brick_forces(grid, tile, fe, rims, psi, dip)
+        beyond = rim_forces(grid, tile, fe, rims, psi, dip, RIM_FAR, RIM_FAR + 3)
+        for s in range(3):
+            for d in range(3):
+                forces[3 * s + d, tile.index] = brick[s][d]
+                forces_rim[3 * s + d, tile.index] = beyond[s][d]
+
+    grid.over(both)
+
+
 def early_kernel(
-    fl, fe, ab1, kept1, given1, first_a, first_b, recv_a, recv_b, send_a, send_b, hold, ab, kept,
-    lines, lines2, lines_out, rims, near, mid, rim_mid, given,
+    fl, fe, ab1, kept1, given1, forces, forces_rim, rims, recv_a, recv_b, out,
+    lines, near, mid, rim_mid, rim_level, rim_far, hold, hold_rim, ab, kept, total, staged, sems,
 ):
     planes, rows, cols = fl.shape[1] - 1, fl.shape[2], fl.shape[3]
     grid = Grid(planes, rows, cols)
-    parity = parity_of("gx")
-    unpack_rims(grid, first_a, first_b, parity, lines, rims, (15, 16, 17) + tuple(range(21, 27)))
-    unpack_rims(grid, recv_a, recv_b, parity, lines2, near, range(12))
+    unpack_rims(grid, recv_a, recv_b, parity_of("gx"), lines, near, range(SECOND_LINES))
     rest = 1.0 - 1.0 / RELAXATION[2]
     at_rim = (grid.sub == 0) | (grid.sub == rows - 1)
+    outward = jnp.where(grid.sub < rows // 2, -1.0, 1.0).astype(F32)
 
     def complete(tile):
         t = tile.index
@@ -573,54 +656,87 @@
         alpha = [tile.get(ab1, s) + (1.0 - tile.get(fl, 9 + s)) * inward[s] for s in range(3)]
         beta = [tile.get(ab1, 3 + d) for d in range(3)]
         for q in range(19):
-            c = VELOCITY[q]
-            along = mixed(c, beta) if q != 16 else None
+            along = mixed(VELOCITY[q], beta) if q != 16 else None
             for s in range(3):
                 v = alpha[s] if along is None else alpha[s] + along
                 if s == 2:
                     v = v + rest * kept1[q, t]
                 mid[s * 19 + q, t] = v
         fixes = [(1.0 - tile.get(rims, s)) * tile.get(given1, s) for s in range(3)]
-        sides = [tile.get(near, 5 + d) for d in range(2)]
-        for s in range(2):
-            base = tile.get(near, 3 + s) + fixes[s]
-            for j, (cy, cz) in enumerate(CROSS):
-                rim_mid[s * 5 + j, t] = base if j == 0 else base + mixed((cy, cz), sides)
-        for j in range(5):
-            rim_mid[10 + j, t] = tile.get(near, 7 + j) + fixes[2]
+        alpha = [tile.get(near, 3 + s) + fixes[s] for s in range(2)]
+        beta = [tile.get(near, 5 + d) for d in range(3)]
+        far = [tile.get(near, 8 + s) for s in range(4)]
+        ahead = outward * beta[0]
+        for j, yz in enumerate(CROSS):
+            side = mixed(yz, beta[1:]) if j else None
+            side_far = mixed(yz, far[2:]) if j else None
+            for s in range(2):
+                rim_mid[s * 5 + j, t] = plus(side, alpha[s] + ahead)
+                rim_far[s * 5 + j, t] = plus(side_far, far[s])
+            rim_mid[10 + j, t] = tile.get(near, 12 + j) + fixes[2]
+            rim_far[10 + j, t] = tile.get(near, 17 + j)
+        for i, q in enumerate(LEVEL):
+            side = mixed(VELOCITY[q][1:], beta[1:]) if q != 16 else None
+            for s in range(2):
+                rim_level[s * 9 + i, t] = plus(side, alpha[s])
+            rim_level[18 + i, t] = tile.get(near, 22 + i) + fixes[2]
 
     grid.over(complete)
 
     def collide(tile):
-        dipole = [tile.get(fe, 6 + d) for d in range(3)]
-        forces = field_forces(grid, tile, fe, rims, 3, 6, dipole)
+        t = tile.index
         load = lambda c, dz: tile.get(mid, c, dz)
-        collision_adjoint(grid, tile, load, rim_mid, fe, forces, hold, ab, kept)
+        known = [[forces[3 * s + d, t] for d in range(3)] for s in range(3)]
+        brick_collision(grid, tile, load, rim_mid, fe, known, hold, ab, kept)
 
     grid.over(collide)
-    grid.over(lambda tile: hand_over(grid, tile, hold, fe, rims, 6, given))
-    up, down = parity, 1 - parity
-    fill = 0
-    for c in range(3):
-        for t in range(grid.tiles):
-            v = given[c, t]
-            lines_out[up, fill : fill + 1, :] = v[rows - 1 : rows, :]
-            lines_out[down, fill : fill + 1, :] = v[0:1, :]
-            fill += 1
-    send_rows(grid, up, lines_out, send_a, send_b)
-
-
-def out_kernel(fe, hold, ab, kept, recv_a, recv_b, out, lines, near, total, staged, sems):
-    planes, rows, cols = fe.shape[1] - 1, fe.shape[2], fe.shape[3]
-    grid = Grid(planes, rows, cols)
-    unpack_rims(grid, recv_a, recv_b, parity_of("gx"), lines, near, range(3))
-    at_rim = (grid.sub == 0) | (grid.sub == rows - 1)
+    low = grid.sub < rows // 2
+
+    def collide_rim(tile):
+        t = tile.index
+
+        def streamed_of(s):
+            streamed = []
+            for q in range(19):
+                c = VELOCITY[q]
+                if c[0] == 0:
+                    v = tile.get(rim_level, s * 9 + LEVEL.index(q), c[2])
+                elif c[0] > 0:
+                    v = tile.get(rim_far, s * 5 + AHEAD.index(q), c[2])
+                else:
+                    j = BEHIND.index(q)
+                    v = jnp.where(
+                        low,
+                        tile.get(mid, s * 19 + AHEAD[j], c[2]),
+                        tile.get(mid, s * 19 + BEHIND[j], c[2]),
+                    )
+                if c[1] != 0:
+                    v = grid.roll_cols(v, c[1])
+                streamed.append(v)
+            return streamed
+
+        known = [[forces_rim[3 * s + d, t] for d in range(3)] for s in range(3)]
+        rho, u, psi = [[rims[RIM_EARLY + at + d, t] for d in range(3)] for at in (0, 3, 9)]
+        u[0] = u[0] * outward
+        held, unused, unused = collision_adjoint(streamed_of, rho, u, psi, known)
+        for k in range(9):
+            hold_rim[k, t] = held[k] * outward if k % 3 == 0 else held[k]
+
+    grid.over(collide_rim)
 
     def finish(tile):
         back = spread_inside(grid, tile, hold, fe)
-        for s in range(3):
-            back[s] = back[s] + jnp.where(at_rim, tile.get(near, s), 0.0)
-            total[s, tile.index] = tile.get(ab, s) + (1.0 - tile.get(fe, 9 + s)) * back[s]
+        dipole = [tile.get(fe, 6 + d) for d in range(3)]
+        part = spread_plane(
+            grid,
+            lambda k, dz: tile.get(hold_rim, k, dz),
+            lambda k, dz: tile.get(rims, RIM_EARLY + 6 + k, dz),
+            rim_sign(grid),
+            CROSS,
+        )
+        for s, x in enumerate(met(part, dipole)):
+            x = back[s] + jnp.where(at_rim, x, 0.0)
+            total[s, tile.index] = tile.get(ab, s) + (1.0 - tile.get(fe, 9 + s)) * x
 
     grid.over(finish)
     is_low, is_high = grid.lane < HALO, grid.lane >= cols - HALO
@@ -643,7 +759,7 @@
             for s in range(3):
                 v = alpha[s] if along is None else alpha[s] + along
                 if s == 2:
-                    v = v + (1.0 - 1.0 / RELAXATION[2]) * patched(kept[q, p], kept[q, planes])
+                    v = v + rest * patched(kept[q, p], kept[q, planes])
                 staged[s * 19 + q, p] = v
         to_out(p).start()
         return carry
@@ -704,41 +820,35 @@
     recv_c, recv_d = swap(send_c, "gy", 0), swap(send_d, "gy", 1)
     send_a, send_b, edge, fl, fe = call(
         pack_rows_kernel,
-        [lines(27)] * 2 + [(pops,) + tile] + [(12, tiles) + tile] * 2,
-        [both(27)],
+        [lines(FIRST_LINES)] * 2 + [(pops,) + tile] + [(12, tiles) + tile] * 2,
+        [both(FIRST_LINES)],
         [adj, own_left, own_right, recv_c, recv_d, fl_main, fe_main],
     )
     first_a, first_b = swap(send_a, "gx", 0), swap(send_b, "gx", 1)
-    hold_shape, ab_shape, kept_shape = [(n, tiles) + tile for n in (9, 6, 19)]
-    three = (3, tiles) + tile
+
+    def tiled(*counts):
+        return [(n, tiles) + tile for n in counts]
+
     send_a, send_b, ab1, kept1, given1 = call(
         late_kernel,
-        [lines(12)] * 2 + [ab_shape, kept_shape, three],
-        [both(27), both(12), (21, tiles) + tile, hold_shape],
+        [lines(SECOND_LINES)] * 2 + tiled(6, 19, 3),
+        [both(FIRST_LINES), both(SECOND_LINES)] + tiled(21, 9),
         [adj, edge, fl, first_a, first_b],
     )
     recv_a, recv_b = swap(send_a, "gx", 0), swap(send_b, "gx", 1)
-    send_a, send_b, hold, ab, kept = call(
+    forces, forces_rim, rims = call(
+        forces_kernel,
+        tiled(9, 9, len(KEPT_LINES)),
+        [both(FIRST_LINES)],
+        [fe, first_a, first_b, given1],
+    )
+    (out,) = call(
         early_kernel,
-        [lines(3)] * 2 + [hold_shape, ab_shape, kept_shape],
-        [
-            both(27),
-            both(12),
-            both(3),
-            (9, tiles) + tile,
-            (12, tiles) + tile,
-            (pops, tiles) + tile,
-            (15, tiles) + tile,
-            three,
-        ],
-        [fl, fe, ab1, kept1, given1, first_a, first_b, recv_a, recv_b],
-    )
-    recv_a, recv_b = swap(send_a, "gx", 0), swap(send_b, "gx", 1)
-    (out,) = call(
-        out_kernel,
         [(pops, planes) + tile],
-        [both(3), three, three, (pops, planes) + tile, pltpu.SemaphoreType.DMA((planes,))],
-        [fe, hold, ab, kept, recv_a, recv_b],
+        [both(SECOND_LINES)]
+        + tiled(SECOND_LINES, pops, 15, 27, 15, 9, 9, 6, 19, 3)
+        + [(pops, planes) + tile, pltpu.SemaphoreType.DMA((planes,))],
+        [fl, fe, ab1, kept1, given1, forces, forces_rim, rims, recv_a, recv_b],
         out_hbm=True,
     )
     return out

time: 34.5 us -> 29.3 us (0.85)
  starting transfers between devices: 15.7 us -> 12 us
  waiting for transfers between devices: 11.2 us -> 8.62 us
  Pallas kernels: 7.45 us -> 8.55 us
    ppermute x8 -> x6, starting transfers between devices: 15.7 us -> 12 us  [swap(): return lax.ppermute(block, axis, route)]
    ppermute x8 -> x6, waiting for transfers between devices: 11.2 us -> 8.62 us  [swap(): return lax.ppermute(block, axis, route)]
    pallas_call x5, Pallas kernels: 7.45 us -> 8.55 us  [call(): pl.pallas_call(kernel, out_shape=[jax.ShapeDtypeStruct(s, F32) for s in o...]
  transfers between devices with their start and end apart: 8 -> 6, of which waited for: 5 -> 4; matrix products, arithmetic and copies ran while one was open for 0% -> 0% of each run, Pallas kernels for 0% -> 3%
where the time goes in v4:
time: 29.3 us; the launch traced here: 29.2 us
  starting transfers between devices  12 us (41%)
  waiting for transfers between devices  8.62 us (29%)
  Pallas kernels  8.55 us (29%)
    ppermute x6, starting transfers between devices, swap(): return lax.ppermute(block, axis, route)  12 us
    ppermute x6, waiting for transfers between devices, swap(): return lax.ppermute(block, axis, route)  8.62 us
    pallas_call x5, Pallas kernels, call(): pl.pallas_call(kernel, out_shape=[jax.ShapeDtypeStruct(s, F32) for s in o...  8.55 us
  transfers between devices with their start and end apart: 6, of which 4 were waited for; matrix products, arithmetic and copies ran while one was open for 0% of the time, Pallas kernels for 3%

profile of v4, /device:TPU:0, one launch (start us, length us, event | category | flops | bytes accessed | tf_op | source)
XLA Modules:
  0.0 29.2 jit_solution(7135614013485213986)
XLA Ops:
  0.0 2.0 %shard_map.55 = (f32[10,8,128]{2,1,0:T(8,128)S(1)}, f32[10,8,128]{2,1,0:T(8,128)S(1)}, f32[20,8,128]{2,1,0:T(8,128)S(1)}, f32[20,8,128]{2,1,0:T(8,128)S(1)}, f32...) custom-call(f32[57,4,8,128]{3,2,1,0:T(8,128)} %adj_in.1, ...), custom_call_target="tpu_custom_call" | custom-call | tf_op jit(solution)/shard_map/pallas_call | solution.py:775
  2.0 0.5 %collective-permute-start = (f32[10,8,128]{2,1,0:T(8,128)S(1)}, f32[10,8,128]{2,1,0:T(8,128)S(1)}, u32[]{:S(2)}, u32[]{:S(2)}) collective-permute-start(f32[10,8,128]{2,1,0:T(8,128)S(1)} %get-tuple-element.28), channel_id=1, source_target_pairs={{0,1},{1,0},{2,3},{3,2},{4,5},{5,4},{6,7},{7,6},{8,9},{9,8},{10,11... | collective-permute-start | bytes 122888 | tf_op jit(solution)/shard_map/ppermute | solution.py:791
  2.5 2.6 %collective-permute-start.1 = (f32[10,8,128]{2,1,0:T(8,128)S(1)}, f32[10,8,128]{2,1,0:T(8,128)S(1)}, u32[]{:S(2)}, u32[]{:S(2)}) collective-permute-start(f32[10,8,128]{2,1,0:T(8,128)S(1)} %get-tuple-element.29), channel_id=1, source_target_pairs={{1,2},{2,1},{3,0},{0,3},{5,6},{6,5},{7,4},{4,7},{9,10},{10,9},{11,... | collective-permute-start | bytes 122888 | tf_op jit(solution)/shard_map/ppermute | solution.py:791
  5.1 0.0 collective-permute-done.recv_c
  5.1 1.8 %collective-permute-done.1.recv_d = f32[10,8,128]{2,1,0:T(8,128)S(1)} collective-permute-done((f32[10,8,128]{2,1,0:T(8,128)S(1)}, f32[10,8,128]{2,1,0:T(8,128)S(1)}, u32[]{:S(2)}, u32[]{:S(2)}) %collective-permute-start.1) | collective-permute-done | bytes 40992 | tf_op jit(solution)/shard_map/ppermute | solution.py:791
  6.9 0.3 %shard_map.56 = (f32[200,128]{1,0:T(8,128)S(1)}, f32[200,128]{1,0:T(8,128)S(1)}, f32[57,8,128]{2,1,0:T(8,128)S(1)}, f32[12,5,8,128]{3,2,1,0:T(8,128)S(1)}, f32[12,5,8,128]{3,2,1,0:T(8,128)S(1)}) custom-call(f32[57,4,8,128]{3,2,1,0:T(8,128)S(1)} %get-tuple-element.25.adj, f32[20,8,128]{2,1,0:T(8,128)S(1)} %get-tuple-element.26.own_left, ...), custom_call_target="tpu_custom_call" | custom-call | tf_op jit(solution)/shard_map/pallas_call | solution.py:775
  7.3 1.6 %collective-permute-start.2 = (f32[200,128]{1,0:T(8,128)S(1)}, f32[200,128]{1,0:T(8,128)S(1)}, u32[]{:S(2)}, u32[]{:S(2)}) collective-permute-start(f32[200,128]{1,0:T(8,128)S(1)} %get-tuple-element.35), channel_id=1, source_target_pairs={{0,4},{4,0},{8,12},{12,8},{16,20},{20,16},{24,28},{28,24},{1,5},{5... | collective-permute-start | bytes 307208 | tf_op jit(solution)/shard_map/ppermute | solution.py:791
  8.9 3.5 %collective-permute-start.3 = (f32[200,128]{1,0:T(8,128)S(1)}, f32[200,128]{1,0:T(8,128)S(1)}, u32[]{:S(2)}, u32[]{:S(2)}) collective-permute-start(f32[200,128]{1,0:T(8,128)S(1)} %get-tuple-element.36), channel_id=1, source_target_pairs={{4,8},{8,4},{12,16},{16,12},{20,24},{24,20},{28,0},{0,28},{5,9},{9... | collective-permute-start | bytes 307208 | tf_op jit(solution)/shard_map/ppermute | solution.py:791
  12.4 1.4 %collective-permute-done.2.recv_a = f32[200,128]{1,0:T(8,128)S(1)} collective-permute-done((f32[200,128]{1,0:T(8,128)S(1)}, f32[200,128]{1,0:T(8,128)S(1)}, u32[]{:S(2)}, u32[]{:S(2)}) %collective-permute-start.2) | collective-permute-done | bytes 102432 | tf_op jit(solution)/shard_map/ppermute | solution.py:791
  13.8 2.7 %collective-permute-done.3.recv_b = f32[200,128]{1,0:T(8,128)S(1)} collective-permute-done((f32[200,128]{1,0:T(8,128)S(1)}, f32[200,128]{1,0:T(8,128)S(1)}, u32[]{:S(2)}, u32[]{:S(2)}) %collective-permute-start.3) | collective-permute-done | bytes 102432 | tf_op jit(solution)/shard_map/ppermute | solution.py:791
  16.5 1.8 %shard_map.57 = (f32[160,128]{1,0:T(8,128)S(1)}, f32[160,128]{1,0:T(8,128)S(1)}, f32[6,5,8,128]{3,2,1,0:T(8,128)S(1)}, f32[19,5,8,128]{3,2,1,0:T(8,128)S(1)}, f32[3,5,8,128]{3,2,1,0:T(8,128)S(1)}) custom-call(f32[57,4,8,128]{3,2,1,0:T(8,128)S(1)} %get-tuple-element.25.adj, f32[57,8,128]{2,1,0:T(8,128)S(1)} %get-tuple-element.34.edge, ...), custom_call_target="tpu_custom_call" | custom-call | tf_op jit(solution)/shard_map/pallas_call | solution.py:775
  18.3 0.1 collective-permute-start.4
  18.4 3.6 %collective-permute-start.5 = (f32[160,128]{1,0:T(8,128)S(1)}, f32[160,128]{1,0:T(8,128)S(1)}, u32[]{:S(2)}, u32[]{:S(2)}) collective-permute-start(f32[160,128]{1,0:T(8,128)S(1)} %get-tuple-element.44), channel_id=1, source_target_pairs={{4,8},{8,4},{12,16},{16,12},{20,24},{24,20},{28,0},{0,28},{5,9},{9... | collective-permute-start | bytes 245768 | tf_op jit(solution)/shard_map/ppermute | solution.py:791
  22.0 0.9 %shard_map.58 = (f32[9,5,8,128]{3,2,1,0:T(8,128)S(1)}, f32[9,5,8,128]{3,2,1,0:T(8,128)S(1)}, f32[21,5,8,128]{3,2,1,0:T(8,128)S(1)}) custom-call(f32[12,5,8,128]{3,2,1,0:T(8,128)S(1)} %get-tuple-element.33.fe, f32[200,128]{1,0:T(8,128)S(1)} %collective-permute-done.2.recv_a, f32[200,128]{1,0:T(8,128)S(1)} %collective-permute-done.3.recv_b, ...), custom_call_target="tpu_custom_call" | custom-call | tf_op jit(solution)/shard_map/pallas_call | solution.py:775
  22.9 0.0 collective-permute-done.4.recv_a
  23.0 2.7 %collective-permute-done.5.recv_b = f32[160,128]{1,0:T(8,128)S(1)} collective-permute-done((f32[160,128]{1,0:T(8,128)S(1)}, f32[160,128]{1,0:T(8,128)S(1)}, u32[]{:S(2)}, u32[]{:S(2)}) %collective-permute-start.5) | collective-permute-done | bytes 81952 | tf_op jit(solution)/shard_map/ppermute | solution.py:791
  25.6 3.6 %shard_map.59 = f32[57,4,8,128]{3,2,1,0:T(8,128)} custom-call(f32[12,5,8,128]{3,2,1,0:T(8,128)S(1)} %get-tuple-element.32.fl, f32[12,5,8,128]{3,2,1,0:T(8,128)S(1)} %get-tuple-element.33.fe, f32[6,5,8,128]{3,2,1,0:T(8,128)S(1)} %get-tuple-element.37.ab1, f32[19,5,8,128]{3,2,1,0:T(8,128)S(1)} %get-tuple-element.38.kept1, ...), custom_call_target="tpu_custom_call" | custom-call | tf_op jit(solution)/shard_map/pallas_call | solution.py:775
Async XLA Ops:
  2.0 3.1 %collective-permute-start = (f32[10,8,128]{2,1,0:T(8,128)S(1)}, f32[10,8,128]{2,1,0:T(8,128)S(1)}, u32[]{:S(2)}, u32[]{:S(2)}) collective-permute-start(f32[10,8,128]{2,1,0:T(8,128)S(1)} %get-tuple-element.28), channel_id=1, source_target_pairs={{0,1},{1,0},{2,3},{3,2},{4,5},{5,4},{6,7},{7,6},{8,9},{9,8},{10,11... | collective-permute-start | bytes 122888 | tf_op jit(solution)/shard_map/ppermute | solution.py:791
  2.5 4.5 %collective-permute-start.1 = (f32[10,8,128]{2,1,0:T(8,128)S(1)}, f32[10,8,128]{2,1,0:T(8,128)S(1)}, u32[]{:S(2)}, u32[]{:S(2)}) collective-permute-start(f32[10,8,128]{2,1,0:T(8,128)S(1)} %get-tuple-element.29), channel_id=1, source_target_pairs={{1,2},{2,1},{3,0},{0,3},{5,6},{6,5},{7,4},{4,7},{9,10},{10,9},{11,... | collective-permute-start | bytes 122888 | tf_op jit(solution)/shard_map/ppermute | solution.py:791
  7.3 6.6 %collective-permute-start.2 = (f32[200,128]{1,0:T(8,128)S(1)}, f32[200,128]{1,0:T(8,128)S(1)}, u32[]{:S(2)}, u32[]{:S(2)}) collective-permute-start(f32[200,128]{1,0:T(8,128)S(1)} %get-tuple-element.35), channel_id=1, source_target_pairs={{0,4},{4,0},{8,12},{12,8},{16,20},{20,16},{24,28},{28,24},{1,5},{5... | collective-permute-start | bytes 307208 | tf_op jit(solution)/shard_map/ppermute | solution.py:791
  8.9 7.7 %collective-permute-start.3 = (f32[200,128]{1,0:T(8,128)S(1)}, f32[200,128]{1,0:T(8,128)S(1)}, u32[]{:S(2)}, u32[]{:S(2)}) collective-permute-start(f32[200,128]{1,0:T(8,128)S(1)} %get-tuple-element.36), channel_id=1, source_target_pairs={{4,8},{8,4},{12,16},{16,12},{20,24},{24,20},{28,0},{0,28},{5,9},{9... | collective-permute-start | bytes 307208 | tf_op jit(solution)/shard_map/ppermute | solution.py:791
  18.3 4.6 %collective-permute-start.4 = (f32[160,128]{1,0:T(8,128)S(1)}, f32[160,128]{1,0:T(8,128)S(1)}, u32[]{:S(2)}, u32[]{:S(2)}) collective-permute-start(f32[160,128]{1,0:T(8,128)S(1)} %get-tuple-element.43), channel_id=1, source_target_pairs={{0,4},{4,0},{8,12},{12,8},{16,20},{20,16},{24,28},{28,24},{1,5},{5... | collective-permute-start | bytes 245768 | tf_op jit(solution)/shard_map/ppermute | solution.py:791
  18.4 7.2 %collective-permute-start.5 = (f32[160,128]{1,0:T(8,128)S(1)}, f32[160,128]{1,0:T(8,128)S(1)}, u32[]{:S(2)}, u32[]{:S(2)}) collective-permute-start(f32[160,128]{1,0:T(8,128)S(1)} %get-tuple-element.44), channel_id=1, source_target_pairs={{4,8},{8,4},{12,16},{16,12},{20,24},{24,20},{28,0},{0,28},{5,9},{9... | collective-permute-start | bytes 245768 | tf_op jit(solution)/shard_map/ppermute | solution.py:791

commit v5 on v4

--- a/solution.py
+++ b/solution.py
@@ -34,13 +34,15 @@
 AHEAD = tuple(INDEX[(1,) + yz] for yz in CROSS)
 BEHIND = tuple(INDEX[(-1,) + yz] for yz in CROSS)
 SIDE = ((1, 0), (-1, 0), (0, 1), (0, -1), (1, 1), (-1, -1), (1, -1), (-1, 1))
-PSI_DIP = (9, 10, 11, 6, 7, 8)
-FIRST_LINES = 15 + 6 + 12 + 6
-KEPT_LINES = tuple(range(15, 18)) + tuple(range(21, 39))
-RIM_EARLY, RIM_FAR = 3, 15
 LEVEL = tuple(q for q in range(19) if VELOCITY[q][0] == 0)
-SECOND_LINES = 3 + 5 + 4 + 5 + 5 + 9
+ALONG, AFTER, LATE, EARLY = 15, 42, 57, 72
+STATIC = 87
+FAR = 9
+LATE_PSI, EARLY_PSI = STATIC, STATIC + 3
+RIMS = STATIC + 6
+DYNAMIC = 12
 F32 = jnp.float32
+CHUNKS = 4
 VMEM_BYTES = 40 * 1024 * 1024
 HALO = 4
 
@@ -72,13 +74,28 @@
     def sides(self, low, high):
         return jnp.where(self.sub == 0, low, high)
 
-    def over(self, body):
+    def over_main(self, body):
         def step(p, carry):
             body(Tile(self, p, False))
             return carry
 
         lax.fori_loop(0, self.planes, step, 0)
+
+    def over_edge(self, body):
         body(Tile(self, self.planes, True))
+
+    def over(self, body):
+        self.over_main(body)
+        self.over_edge(body)
+
+    def at_rim(self):
+        return (self.sub == 0) | (self.sub == self.rows - 1)
+
+    def low(self):
+        return self.sub < self.rows // 2
+
+    def outward(self):
+        return jnp.where(self.low(), -1.0, 1.0).astype(F32)
 
 
 class Tile:
@@ -91,16 +108,29 @@
         return lax.rem(self.index + (dz + self.grid.planes), self.grid.planes)
 
     def get(self, ref, c, dz=0):
-        v = ref[c, self.of(dz)]
+        if isinstance(ref, Pair):
+            v = ref.edge[c] if self.edge else ref.main[c, self.of(dz)]
+        else:
+            v = ref[c, self.of(dz)]
         if self.edge and dz != 0:
             v = self.grid.roll_cols(v, dz * self.grid.width)
         return v
 
-    def split(self, main, edge, c, dz=0):
-        if not self.edge:
-            return main[c, self.of(dz)]
-        v = edge[c]
-        return v if dz == 0 else self.grid.roll_cols(v, dz * self.grid.width)
+    def put(self, ref, c, v):
+        if not isinstance(ref, Pair):
+            ref[c, self.index] = v
+        elif self.edge:
+            ref.edge[c] = v
+        else:
+            ref.main[c, self.index] = v
+
+
+class Pair:
+    def __init__(self, main, edge):
+        self.main, self.edge = main, edge
+
+    def at(self, c, t):
+        return self.edge[c] if t == self.main.shape[1] else self.main[c, t]
 
 
 def plus(a, b):
@@ -220,22 +250,28 @@
         return tile.get(rim, (rim_psi + c) if c < 3 else (rim_dip + c - 3), dz)
 
     def across(get, cx, dz):
+        if rim is None:
+            return grid.in_row(get(0, dz), cx)
         return grid.at_row(get(0, dz), get(1, dz), cx)
 
     return field_forces(grid, (own, beyond), across, [own(3 + d, 0) for d in range(3)])
 
 
-def rim_forces(grid, tile, fields, rim, psi1, dip1, psi2, dip2):
-    outward = jnp.where(grid.sub < grid.rows // 2, -1.0, 1.0).astype(F32)
-
-    def loader(ref, psi, dip):
+def rim_forces(grid, tile, fields, rims, psi, base):
+    outward = grid.outward()
+
+    def loader(ref, psi_at, dip_at):
         def load(c, dz):
-            v = tile.get(ref, (psi + c) if c < 3 else (dip + c - 3), dz)
+            v = tile.get(ref, (psi_at + c) if c < 3 else (dip_at + c - 3), dz)
             return v * outward if c == 3 else v
 
         return load
 
-    loads = {0: loader(rim, psi1, dip1), 1: loader(rim, psi2, dip2), -1: loader(fields, 9, 6)}
+    loads = {
+        0: loader(rims, psi, base + 6),
+        1: loader(rims, base + FAR, base + FAR + 3),
+        -1: loader(fields, 9, 6),
+    }
     dipole = [loads[0](3 + d, 0) for d in range(3)]
     return field_forces(grid, loads, lambda get, cx, dz: get(cx, dz), dipole)
 
@@ -273,8 +309,6 @@
 
 
 def brick_collision(grid, tile, load, rim, fields, forces, hold, ab, kept):
-    t = tile.index
-
     def streamed_of(s):
         streamed = []
         for q in range(19):
@@ -282,21 +316,55 @@
             v = load(s * 19 + q, c[2])
             if c[0] != 0:
                 j = (AHEAD if c[0] > 0 else BEHIND).index(q)
-                v = grid.at_row(v, tile.get(rim, s * 5 + j, c[2]), c[0])
+                if rim is None:
+                    v = grid.in_row(v, c[0])
+                else:
+                    v = grid.at_row(v, tile.get(rim, s * 5 + j, c[2]), c[0])
             if c[1] != 0:
                 v = grid.roll_cols(v, c[1])
             streamed.append(v)
             if s == 2:
-                kept[q, t] = v
+                tile.put(kept, q, v)
         return streamed
 
     rho, u, psi = [[tile.get(fields, at + d) for d in range(3)] for at in (0, 3, 9)]
     held, alpha, beta = collision_adjoint(streamed_of, rho, u, psi, forces)
     for k in range(9):
-        hold[k, t] = held[k]
+        tile.put(hold, k, held[k])
     for s in range(3):
-        ab[s, t] = alpha[s]
-        ab[3 + s, t] = beta[s]
+        tile.put(ab, s, alpha[s])
+        tile.put(ab, 3 + s, beta[s])
+
+
+def rim_collision(grid, tile, level, after, inner, rho, u, psi, forces, hold, ab, kept):
+    outward, low = grid.outward(), grid.low()
+
+    def streamed_of(s):
+        streamed = []
+        for q in range(19):
+            c = VELOCITY[q]
+            if c[0] == 0:
+                v = level(s, LEVEL.index(q), c[2])
+            elif c[0] > 0:
+                v = after(s, AHEAD.index(q), c[2])
+            else:
+                j = BEHIND.index(q)
+                v = jnp.where(low, inner(s * 19 + AHEAD[j], c[2]), inner(s * 19 + BEHIND[j], c[2]))
+            if c[1] != 0:
+                v = grid.roll_cols(v, c[1])
+            streamed.append(v)
+            if s == 2 and kept is not None and c[0] >= 0:
+                tile.put(kept, LEVEL.index(q) if c[0] == 0 else 9 + AHEAD.index(q), v)
+        return streamed
+
+    u = [u[0] * outward, u[1], u[2]]
+    held, alpha, beta = collision_adjoint(streamed_of, rho, u, psi, forces)
+    for k in range(9):
+        tile.put(hold, k, held[k] * outward if k % 3 == 0 else held[k])
+    if ab is not None:
+        for s in range(3):
+            tile.put(ab, s, alpha[s])
+            tile.put(ab, 3 + s, beta[s] * outward if s == 0 else beta[s])
 
 
 def spread_plane(grid, get_h, get_d, sign, pairs):
@@ -373,34 +441,75 @@
     ).astype(F32)
 
 
-def hand_over(grid, tile, hold, fields, rim, rim_dip, given):
+def hand_over(grid, tile, hold, hold_dip, target, sign):
+    dip, at = hold_dip
     total = spread_plane(
         grid,
         lambda k, dz: tile.get(hold, k, dz),
-        lambda k, dz: tile.get(fields, 6 + k, dz),
-        -rim_sign(grid),
+        lambda k, dz: tile.get(dip, at + k, dz),
+        sign,
         CROSS,
     )
-    for s, x in enumerate(met(total, [tile.get(rim, rim_dip + d) for d in range(3)])):
-        given[s, tile.index] = x
-
-
-def unpack_rims(grid, first, second, parity, lines, rims, pairs):
+    return met(total, target)
+
+
+def spread_level(grid, tile, hold, dip, at):
+    total = spread_plane(
+        grid,
+        lambda k, dz: tile.get(hold, k, dz),
+        lambda k, dz: tile.get(dip, at + k, dz),
+        0,
+        SIDE,
+    )
+    return met(total, [tile.get(dip, at + d) for d in range(3)])
+
+
+def parity_of(axis):
+    return lax.rem(lax.axis_index(axis), 2)
+
+
+def lines_from(first, second, parity, lines):
     lines[1 - parity] = first[...]
     lines[parity] = second[...]
-    for at, c in enumerate(pairs):
-        for t in range(grid.tiles):
-            k = c * grid.tiles + t
-            rims[at, t] = grid.sides(lines[0, k : k + 1, :], lines[1, k : k + 1, :])
-
-
-def send_rows(grid, parity, lines, first, second):
+
+
+def lines_to(first, second, lines):
     first[...] = lines[0]
     second[...] = lines[1]
 
 
-def parity_of(axis):
-    return lax.rem(lax.axis_index(axis), 2)
+def psi_of(rho):
+    return 1.0 - jnp.exp(-rho)
+
+
+def pack_static(get, tiles, rows, lines, parity):
+    up, down = parity, 1 - parity
+    fill = 0
+
+    def put(kind, above, below, depth):
+        nonlocal fill
+        for t in tiles:
+            v = get(kind, above, t)
+            lines[up, fill : fill + 1, :] = v[rows - 1 - depth : rows - depth, :]
+            v = get(kind, below, t)
+            lines[down, fill : fill + 1, :] = v[depth : depth + 1, :]
+            fill += 1
+
+    for s in range(3):
+        for j in range(5):
+            put(0, s * 19 + BEHIND[j], s * 19 + AHEAD[j], 0)
+    for s in range(3):
+        for q in LEVEL:
+            put(0, s * 19 + q, s * 19 + q, 0)
+    for s in range(3):
+        for j in range(5):
+            put(0, s * 19 + BEHIND[j], s * 19 + AHEAD[j], 1)
+    for kind in (1, 2):
+        for c in range(9):
+            put(kind, c, c, 0)
+        for c in (9, 10, 11, 6, 7, 8):
+            put(kind, c, c, 1)
+    return fill
 
 
 def pack_columns_kernel(
@@ -418,10 +527,13 @@
                 (late_in, late),
                 (dip_early_in, dip_early),
                 (early_in, early),
-                (adj_in, adj),
             )
         )
     ]
+    per_chunk = -(-adj.shape[0] // (CHUNKS * grid.pack)) * grid.pack
+    for i in range(CHUNKS):
+        part = pl.ds(i * per_chunk, min(per_chunk, adj.shape[0] - i * per_chunk))
+        copies.append(pltpu.make_async_copy(adj_in.at[part], adj.at[part], sems.at[4 + i]))
     for copy in copies:
         copy.start()
     for which, (saved, dip, out) in enumerate(((late, dip_late, fl), (early, dip_early, fe))):
@@ -439,6 +551,7 @@
                     total = plus(total, v)
                 rho.append(total)
                 out[s, p] = total
+                out[9 + s, p] = psi_of(total)
             inverse = 1.0 / (rho[0] + rho[1] + rho[2])
             for d in range(3):
                 momentum = None
@@ -450,11 +563,12 @@
             return carry
 
         lax.fori_loop(0, planes, step, 0)
-    copies[4].wait()
     pops = adj.shape[0]
     components = pops + 18
     slot = grid.lane // grid.group
     for g in range(own_left.shape[0]):
+        if g * grid.pack % per_chunk == 0 and g * grid.pack < pops:
+            copies[4 + g * grid.pack // per_chunk].wait()
         left = right = jnp.zeros((rows, cols), F32)
         for j in range(grid.pack):
             c = g * grid.pack + j
@@ -482,10 +596,36 @@
         send_d[h] = jnp.where(even, left, right)
 
 
-def pack_rows_kernel(
-    adj, own_left, own_right, recv_c, recv_d, fl_main, fe_main, send_a, send_b, edge, fl, fe, lines
+def static_kernel(adj, fl, fe, send_a, send_b, lines):
+    planes, rows, cols = adj.shape[1:]
+    kinds = (adj, fl, fe)
+    pack_static(lambda kind, c, t: kinds[kind][c, t], range(planes), rows, lines, parity_of("gx"))
+    lines_to(send_a, send_b, lines)
+
+
+def inside_collision(grid, tile, load, fields, hold, ab, kept):
+    forces = brick_forces(grid, tile, fields, None, 0, 0)
+    brick_collision(grid, tile, load, None, fields, forces, hold, ab, kept)
+    at_rim = grid.at_rim()
+    for k in range(9):
+        tile.put(hold, k, jnp.where(at_rim, 0.0, tile.get(hold, k)))
+
+
+def inside_kernel(adj, fl, hold, ab, kept):
+    grid = Grid(*adj.shape[1:])
+    grid.over_main(
+        lambda tile: inside_collision(
+            grid, tile, lambda c, dz: tile.get(adj, c, dz), fl, hold, ab, kept
+        )
+    )
+
+
+def edge_kernel(
+    own_left, own_right, recv_c, recv_d, fl_main, hold_main, ab_main, kept_main,
+    send_a, send_b, edge, fl, fe, lines, hold, ab, kept, sides,
 ):
-    pops, planes, rows, cols = adj.shape
+    planes, rows, cols = fl_main.shape[1:]
+    pops = edge.shape[0]
     grid = Grid(planes, rows, cols)
     even = parity_of("gy") == 0
     slot = lax.rem(grid.lane // grid.group, grid.pack)
@@ -512,231 +652,230 @@
             )
             if c < pops:
                 edge[c] = v
-            elif c < pops + 9:
-                fl[c - pops, planes] = v
             else:
-                fe[c - pops - 9, planes] = v
-    for main, out in ((fl_main, fl), (fe_main, fe)):
-        for c in range(9):
-            for p in range(planes):
-                out[c, p] = main[c, p]
+                field, k = (fl, c - pops) if c < pops + 9 else (fe, c - pops - 9)
+                field[k] = v
+                if k < 3:
+                    field[9 + k] = psi_of(v)
+    fields = Pair(fl_main, fl)
+    hold, ab, kept = Pair(hold_main, hold), Pair(ab_main, ab), Pair(kept_main, kept)
+    adj = Pair(None, edge)
+    grid.over_edge(
+        lambda tile: inside_collision(
+            grid, tile, lambda c, dz: tile.get(adj, c, dz), fields, hold, ab, kept
+        )
+    )
+    low = grid.low()
+    inward = -grid.outward()
+    rest = 1.0 - 1.0 / RELAXATION[2]
+
+    def second_row(tile):
+        back = spread_inside(grid, tile, hold, fields)
+        alpha = [tile.get(ab, s) + (1.0 - tile.get(fields, 9 + s)) * back[s] for s in range(3)]
+        beta = [tile.get(ab, 3 + d) for d in range(3)]
+        ahead = inward * beta[0]
         for s in range(3):
-            for t in range(grid.tiles):
-                out[9 + s, t] = 1.0 - jnp.exp(-out[s, t])
-    up, down = parity_of("gx"), 1 - parity_of("gx")
-    fill = 0
-
-    def put(slot_at, v, row):
-        lines[slot_at, fill : fill + 1, :] = v[row : row + 1, :]
-
-    def put_both(out, c, depth):
-        nonlocal fill
+            tile.put(sides, s, back[s])
+        for s in range(2):
+            tile.put(sides, 3 + s, alpha[s] + ahead)
+            tile.put(sides, 5 + s, beta[1 + s])
+        for j, yz in enumerate(CROSS):
+            v = rest * jnp.where(low, tile.get(kept, AHEAD[j]), tile.get(kept, BEHIND[j]))
+            v = v + (alpha[2] + ahead)
+            tile.put(sides, 7 + j, v + mixed(yz, beta[1:]) if j else v)
+
+    grid.over(second_row)
+    parity = parity_of("gx")
+    kinds = (edge, fl, fe)
+    fill = pack_static(lambda kind, c, t: kinds[kind][c], (0,), rows, lines, parity)
+    for c in range(DYNAMIC):
+        depth = 0 if c < 3 else 1
         for t in range(grid.tiles):
-            put(up, out[c, t], rows - 1 - depth)
-            put(down, out[c, t], depth)
+            lines[parity, fill : fill + 1, :] = sides[c, t, rows - 1 - depth : rows - depth, :]
+            lines[1 - parity, fill : fill + 1, :] = sides[c, t, depth : depth + 1, :]
             fill += 1
-
+    lines_to(send_a, send_b, lines)
+
+
+def first_step(grid, tile, adj, fl, rims, hold, ab, kept, hold_rim, ab_rim, kept_rim):
+    forces = brick_forces(grid, tile, fl, rims, LATE_PSI, LATE + 6)
+    load = lambda c, dz: tile.get(adj, c, dz)
+    brick_collision(grid, tile, load, rims, fl, forces, hold, ab, kept)
+    forces = rim_forces(grid, tile, fl, rims, LATE_PSI, LATE)
+    rho, u = [[tile.get(rims, LATE + at + d) for d in range(3)] for at in (0, 3)]
+    psi = [tile.get(rims, LATE_PSI + s) for s in range(3)]
+    rim_collision(
+        grid,
+        tile,
+        lambda s, i, dz: tile.get(rims, ALONG + s * 9 + i, dz),
+        lambda s, j, dz: tile.get(rims, AFTER + s * 5 + j, dz),
+        load,
+        rho,
+        u,
+        psi,
+        forces,
+        hold_rim,
+        ab_rim,
+        kept_rim,
+    )
+
+
+def early_forces(grid, tile, fe, rims, forces, forces_rim):
+    brick = brick_forces(grid, tile, fe, rims, EARLY_PSI, EARLY + 6)
+    beyond = rim_forces(grid, tile, fe, rims, EARLY_PSI, EARLY)
     for s in range(3):
-        for j in range(5):
-            for t in range(grid.tiles):
-                ahead, behind = s * 19 + AHEAD[j], s * 19 + BEHIND[j]
-                put(up, adj[behind, t] if t < planes else edge[behind], rows - 1)
-                put(down, adj[ahead, t] if t < planes else edge[ahead], 0)
-                fill += 1
-    for c in PSI_DIP:
-        put_both(fl, c, 0)
-    for c in range(12):
-        put_both(fe, c, 0)
-    for c in PSI_DIP:
-        put_both(fe, c, 1)
-    send_rows(grid, up, lines, send_a, send_b)
-
-
-def late_kernel(
-    adj, edge, fl, recv_a, recv_b, send_a, send_b, ab, kept, given, lines, lines_out, rims, hold
+        for d in range(3):
+            tile.put(forces, 3 * s + d, brick[s][d])
+            tile.put(forces_rim, 3 * s + d, beyond[s][d])
+
+
+def rim_psis(grid, tile, rims):
+    for s in range(3):
+        tile.put(rims, LATE_PSI + s, psi_of(tile.get(rims, LATE + s)))
+        tile.put(rims, EARLY_PSI + s, psi_of(tile.get(rims, EARLY + s)))
+
+
+def main_kernel(
+    adj, fl, fe, recv_a, recv_b, after,
+    rims, hold, ab, kept, hold_rim, ab_rim, kept_rim, forces, forces_rim, lines,
 ):
-    pops, planes, rows, cols = adj.shape
+    planes, rows, cols = adj.shape[1:]
     grid = Grid(planes, rows, cols)
-    parity = parity_of("gx")
-    unpack_rims(grid, recv_a, recv_b, parity, lines, rims, range(21))
-
-    def collide(tile):
-        forces = brick_forces(grid, tile, fl, rims, 15, 18)
-        load = lambda c, dz: tile.split(adj, edge, c, dz)
-        brick_collision(grid, tile, load, rims, fl, forces, hold, ab, kept)
-
-    grid.over(collide)
-
-    def finish(tile):
-        back = spread_inside(grid, tile, hold, fl)
-        for s in range(3):
-            ab[s, tile.index] = ab[s, tile.index] + (1.0 - tile.get(fl, 9 + s)) * back[s]
-        hand_over(grid, tile, hold, fl, rims, 18, given)
-
-    grid.over(finish)
-    up, down = parity, 1 - parity
-    fill = 0
-
-    def put(make, depth=0):
-        nonlocal fill
+    lines_from(recv_a, recv_b, parity_of("gx"), lines)
+    for c in range(STATIC):
+        for p in range(planes):
+            k = c * planes + p
+            rims[c, p] = grid.sides(lines[0, k : k + 1, :], lines[1, k : k + 1, :])
+    grid.over_main(lambda tile: rim_psis(grid, tile, rims))
+
+    def step(tile):
+        first_step(grid, tile, adj, fl, rims, hold, ab, kept, hold_rim, ab_rim, kept_rim)
+        early_forces(grid, tile, fe, rims, forces, forces_rim)
+
+    grid.over_main(step)
+
+
+def last_kernel(
+    fl_m, fe_m, edge, fl_e, fe_e, rims_m, hold_m, ab_m, kept_m, hold_rim_m, ab_rim_m, kept_rim_m,
+    forces_m, forces_rim_m, recv_a, recv_b, out,
+    rims_e, hold_e, ab_e, kept_e, hold_rim_e, ab_rim_e, kept_rim_e, forces_e, forces_rim_e,
+    lines, near, mid, rim_mid, rim_level, rim_far, hold2, hold_rim2, ab2, kept2, total, staged,
+    sems,
+):
+    planes, rows, cols = fl_m.shape[1:]
+    grid = Grid(planes, rows, cols)
+    lines_from(recv_a, recv_b, parity_of("gx"), lines)
+    for c in range(STATIC):
+        rims_e[c] = grid.sides(lines[0, c : c + 1, :], lines[1, c : c + 1, :])
+    for c in range(DYNAMIC):
         for t in range(grid.tiles):
-            v = make(t)
-            lines_out[up, fill : fill + 1, :] = v[rows - 1 - depth : rows - depth, :]
-            lines_out[down, fill : fill + 1, :] = v[depth : depth + 1, :]
-            fill += 1
-
-    low = grid.sub < rows // 2
-    inward = jnp.where(low, 1.0, -1.0).astype(F32)
+            k = STATIC + c * grid.tiles + t
+            near[c, t] = grid.sides(lines[0, k : k + 1, :], lines[1, k : k + 1, :])
+    fl, fe, rims = Pair(fl_m, fl_e), Pair(fe_m, fe_e), Pair(rims_m, rims_e)
+    hold, ab, kept = Pair(hold_m, hold_e), Pair(ab_m, ab_e), Pair(kept_m, kept_e)
+    hold_rim, ab_rim = Pair(hold_rim_m, hold_rim_e), Pair(ab_rim_m, ab_rim_e)
+    kept_rim = Pair(kept_rim_m, kept_rim_e)
+    forces, forces_rim = Pair(forces_m, forces_e), Pair(forces_rim_m, forces_rim_e)
     rest = 1.0 - 1.0 / RELAXATION[2]
-
-    def crossing(j):
-        cy, cz = CROSS[j]
-
-        def make(t):
-            v = rest * jnp.where(low, kept[AHEAD[j], t], kept[BEHIND[j], t])
-            v = v + (ab[2, t] + inward * ab[3, t])
-            return v + mixed((cy, cz), (ab[4, t], ab[5, t])) if j else v
-
-        return make
-
-    def level(q):
-        def make(t):
-            v = rest * kept[q, t] + ab[2, t]
-            return v + mixed(VELOCITY[q], [ab[3 + d, t] for d in range(3)]) if q != 16 else v
-
-        return make
-
-    for c in range(3):
-        put(lambda t: given[c, t])
-    for c in (0, 1, 3, 4, 5):
-        put(lambda t: ab[c, t])
-    for c in range(2):
-        put(lambda t: ab[c, t] + inward * ab[3, t], 1)
-    for c in (4, 5):
-        put(lambda t: ab[c, t], 1)
-    for depth in range(2):
-        for j in range(5):
-            put(crossing(j), depth)
-    for q in LEVEL:
-        put(level(q))
-    send_rows(grid, up, lines_out, send_a, send_b)
-
-
-def forces_kernel(fe, recv_a, recv_b, after, forces, forces_rim, rims, lines):
-    planes, rows, cols = fe.shape[1] - 1, fe.shape[2], fe.shape[3]
-    grid = Grid(planes, rows, cols)
-    unpack_rims(grid, recv_a, recv_b, parity_of("gx"), lines, rims, KEPT_LINES)
-    psi, dip = RIM_EARLY + 9, RIM_EARLY + 6
-
-    def both(tile):
-        brick = brick_forces(grid, tile, fe, rims, psi, dip)
-        beyond = rim_forces(grid, tile, fe, rims, psi, dip, RIM_FAR, RIM_FAR + 3)
-        for s in range(3):
-            for d in range(3):
-                forces[3 * s + d, tile.index] = brick[s][d]
-                forces_rim[3 * s + d, tile.index] = beyond[s][d]
-
-    grid.over(both)
-
-
-def early_kernel(
-    fl, fe, ab1, kept1, given1, forces, forces_rim, rims, recv_a, recv_b, out,
-    lines, near, mid, rim_mid, rim_level, rim_far, hold, hold_rim, ab, kept, total, staged, sems,
-):
-    planes, rows, cols = fl.shape[1] - 1, fl.shape[2], fl.shape[3]
-    grid = Grid(planes, rows, cols)
-    unpack_rims(grid, recv_a, recv_b, parity_of("gx"), lines, near, range(SECOND_LINES))
-    rest = 1.0 - 1.0 / RELAXATION[2]
-    at_rim = (grid.sub == 0) | (grid.sub == rows - 1)
-    outward = jnp.where(grid.sub < rows // 2, -1.0, 1.0).astype(F32)
+    at_rim = grid.at_rim()
+    sign = rim_sign(grid)
+    outward = grid.outward()
+
+    def edge_steps(tile):
+        rim_psis(grid, tile, rims)
+        first_step(
+            grid, tile, Pair(None, edge), fl, rims, hold, ab, kept, hold_rim, ab_rim, kept_rim
+        )
+        early_forces(grid, tile, fe, rims, forces, forces_rim)
+
+    grid.over_edge(edge_steps)
 
     def complete(tile):
         t = tile.index
-        inward = [jnp.where(at_rim, tile.get(near, s), 0.0) for s in range(3)]
-        alpha = [tile.get(ab1, s) + (1.0 - tile.get(fl, 9 + s)) * inward[s] for s in range(3)]
-        beta = [tile.get(ab1, 3 + d) for d in range(3)]
+        own_dip, rim_dip = (fl, 6), (rims, LATE + 6)
+        dip = [tile.get(fl, 6 + d) for d in range(3)]
+        dip_rim = [tile.get(rims, LATE + 6 + d) for d in range(3)]
+        dip_far = [tile.get(rims, LATE + FAR + 3 + d) for d in range(3)]
+        back = spread_inside(grid, tile, hold, fl)
+        inward = hand_over(grid, tile, hold_rim, rim_dip, dip, sign)
+        alpha = [
+            tile.get(ab, s)
+            + (1.0 - tile.get(fl, 9 + s)) * (back[s] + jnp.where(at_rim, inward[s], 0.0))
+            for s in range(3)
+        ]
+        beta = [tile.get(ab, 3 + d) for d in range(3)]
         for q in range(19):
             along = mixed(VELOCITY[q], beta) if q != 16 else None
             for s in range(3):
                 v = alpha[s] if along is None else alpha[s] + along
                 if s == 2:
-                    v = v + rest * kept1[q, t]
+                    v = v + rest * tile.get(kept, q)
                 mid[s * 19 + q, t] = v
-        fixes = [(1.0 - tile.get(rims, s)) * tile.get(given1, s) for s in range(3)]
-        alpha = [tile.get(near, 3 + s) + fixes[s] for s in range(2)]
-        beta = [tile.get(near, 5 + d) for d in range(3)]
-        far = [tile.get(near, 8 + s) for s in range(4)]
+        given = hand_over(grid, tile, hold, own_dip, dip_rim, -sign)
+        level = spread_level(grid, tile, hold_rim, *rim_dip)
+        alpha = [
+            tile.get(ab_rim, s)
+            + (1.0 - tile.get(rims, LATE_PSI + s)) * (given[s] + level[s] + near[s, t])
+            for s in range(3)
+        ]
+        beta = [tile.get(ab_rim, 3 + d) for d in range(3)]
+        given = hand_over(grid, tile, hold_rim, rim_dip, dip_far, -sign)
+        fixes = [(1.0 - tile.get(rims, LATE + FAR + s)) * given[s] for s in range(3)]
+        far = [near[3 + s, t] + fixes[s] for s in range(2)]
+        far_beta = [near[5 + d, t] for d in range(2)]
         ahead = outward * beta[0]
         for j, yz in enumerate(CROSS):
             side = mixed(yz, beta[1:]) if j else None
-            side_far = mixed(yz, far[2:]) if j else None
-            for s in range(2):
-                rim_mid[s * 5 + j, t] = plus(side, alpha[s] + ahead)
-                rim_far[s * 5 + j, t] = plus(side_far, far[s])
-            rim_mid[10 + j, t] = tile.get(near, 12 + j) + fixes[2]
-            rim_far[10 + j, t] = tile.get(near, 17 + j)
+            side_far = mixed(yz, far_beta) if j else None
+            for s in range(3):
+                v = plus(side, alpha[s] + ahead)
+                if s == 2:
+                    v = v + rest * tile.get(kept_rim, 9 + j)
+                    rim_far[10 + j, t] = near[7 + j, t] + fixes[2]
+                else:
+                    rim_far[s * 5 + j, t] = plus(side_far, far[s])
+                rim_mid[s * 5 + j, t] = v
         for i, q in enumerate(LEVEL):
             side = mixed(VELOCITY[q][1:], beta[1:]) if q != 16 else None
-            for s in range(2):
-                rim_level[s * 9 + i, t] = plus(side, alpha[s])
-            rim_level[18 + i, t] = tile.get(near, 22 + i) + fixes[2]
+            for s in range(3):
+                v = plus(side, alpha[s])
+                if s == 2:
+                    v = v + rest * tile.get(kept_rim, i)
+                rim_level[s * 9 + i, t] = v
 
     grid.over(complete)
 
     def collide(tile):
-        t = tile.index
         load = lambda c, dz: tile.get(mid, c, dz)
-        known = [[forces[3 * s + d, t] for d in range(3)] for s in range(3)]
-        brick_collision(grid, tile, load, rim_mid, fe, known, hold, ab, kept)
+        known = [[tile.get(forces, 3 * s + d) for d in range(3)] for s in range(3)]
+        brick_collision(grid, tile, load, rim_mid, fe, known, hold2, ab2, kept2)
+        known = [[tile.get(forces_rim, 3 * s + d) for d in range(3)] for s in range(3)]
+        rho, u = [[tile.get(rims, EARLY + at + d) for d in range(3)] for at in (0, 3)]
+        psi = [tile.get(rims, EARLY_PSI + s) for s in range(3)]
+        rim_collision(
+            grid,
+            tile,
+            lambda s, i, dz: tile.get(rim_level, s * 9 + i, dz),
+            lambda s, j, dz: tile.get(rim_far, s * 5 + j, dz),
+            load,
+            rho,
+            u,
+            psi,
+            known,
+            hold_rim2,
+            None,
+            None,
+        )
 
     grid.over(collide)
-    low = grid.sub < rows // 2
-
-    def collide_rim(tile):
-        t = tile.index
-
-        def streamed_of(s):
-            streamed = []
-            for q in range(19):
-                c = VELOCITY[q]
-                if c[0] == 0:
-                    v = tile.get(rim_level, s * 9 + LEVEL.index(q), c[2])
-                elif c[0] > 0:
-                    v = tile.get(rim_far, s * 5 + AHEAD.index(q), c[2])
-                else:
-                    j = BEHIND.index(q)
-                    v = jnp.where(
-                        low,
-                        tile.get(mid, s * 19 + AHEAD[j], c[2]),
-                        tile.get(mid, s * 19 + BEHIND[j], c[2]),
-                    )
-                if c[1] != 0:
-                    v = grid.roll_cols(v, c[1])
-                streamed.append(v)
-            return streamed
-
-        known = [[forces_rim[3 * s + d, t] for d in range(3)] for s in range(3)]
-        rho, u, psi = [[rims[RIM_EARLY + at + d, t] for d in range(3)] for at in (0, 3, 9)]
-        u[0] = u[0] * outward
-        held, unused, unused = collision_adjoint(streamed_of, rho, u, psi, known)
-        for k in range(9):
-            hold_rim[k, t] = held[k] * outward if k % 3 == 0 else held[k]
-
-    grid.over(collide_rim)
 
     def finish(tile):
-        back = spread_inside(grid, tile, hold, fe)
-        dipole = [tile.get(fe, 6 + d) for d in range(3)]
-        part = spread_plane(
-            grid,
-            lambda k, dz: tile.get(hold_rim, k, dz),
-            lambda k, dz: tile.get(rims, RIM_EARLY + 6 + k, dz),
-            rim_sign(grid),
-            CROSS,
-        )
-        for s, x in enumerate(met(part, dipole)):
-            x = back[s] + jnp.where(at_rim, x, 0.0)
-            total[s, tile.index] = tile.get(ab, s) + (1.0 - tile.get(fe, 9 + s)) * x
+        back = spread_inside(grid, tile, hold2, fe)
+        dip = [tile.get(fe, 6 + d) for d in range(3)]
+        inward = hand_over(grid, tile, hold_rim2, (rims, EARLY + 6), dip, sign)
+        for s in range(3):
+            x = back[s] + jnp.where(at_rim, inward[s], 0.0)
+            total[s, tile.index] = tile.get(ab2, s) + (1.0 - tile.get(fe, 9 + s)) * x
 
     grid.over(finish)
     is_low, is_high = grid.lane < HALO, grid.lane >= cols - HALO
@@ -753,13 +892,13 @@
             return jnp.where(is_low, low, jnp.where(is_high, high, main))
 
         alpha = [patched(total[s, p], total[s, planes]) for s in range(3)]
-        beta = [patched(ab[3 + d, p], ab[3 + d, planes]) for d in range(3)]
+        beta = [patched(ab2[3 + d, p], ab2[3 + d, planes]) for d in range(3)]
         for q in range(19):
             along = mixed(VELOCITY[q], beta) if q != 16 else None
             for s in range(3):
                 v = alpha[s] if along is None else alpha[s] + along
                 if s == 2:
-                    v = v + rest * patched(kept[q, p], kept[q, planes])
+                    v = v + rest * patched(kept2[q, p], kept2[q, planes])
                 staged[s * 19 + q, p] = v
         to_out(p).start()
         return carry
@@ -793,62 +932,63 @@
 
 def shards(adjoint_in, populations_early, populations_late, dipoles_early, dipoles_late):
     pops, planes, rows, cols = adjoint_in.shape
-    tiles = planes + 1
     tile = (rows, cols)
     pack = cols // planes // (2 * HALO)
     groups = -(-(pops + 18) // pack)
     groups += groups % 2
 
     def lines(n):
-        return (-(-n * tiles // 8) * 8, cols)
-
-    def both(n):
-        return (2,) + lines(n)
-
-    send_c, send_d, own_left, own_right, fl_main, fe_main, adj = call(
+        return (-(-n // 8) * 8, cols)
+
+    def main(*counts):
+        return [(n, planes) + tile for n in counts]
+
+    def edges(*counts):
+        return [(n,) + tile for n in counts]
+
+    def tiled(*counts):
+        return [(n, planes + 1) + tile for n in counts]
+
+    static = lines(STATIC * planes)
+    second = lines(STATIC + DYNAMIC * (planes + 1))
+    send_c, send_d, own_left, own_right, fl_m, fe_m, adj = call(
         pack_columns_kernel,
-        [(groups // 2,) + tile] * 2
-        + [(groups,) + tile] * 2
-        + [(9, planes) + tile] * 2
-        + [(pops, planes) + tile],
-        [pltpu.VMEM(x.shape, x.dtype) for x in (populations_late, populations_early)]
-        + [pltpu.VMEM(x.shape, x.dtype) for x in (dipoles_late, dipoles_early)]
-        + [pltpu.SemaphoreType.DMA((5,))],
+        edges(groups // 2, groups // 2, groups, groups) + main(12, 12, pops),
+        [
+            pltpu.VMEM(x.shape, x.dtype)
+            for x in (populations_late, populations_early, dipoles_late, dipoles_early)
+        ]
+        + [pltpu.SemaphoreType.DMA((4 + CHUNKS,))],
         [adjoint_in, populations_late, populations_early, dipoles_late, dipoles_early],
         in_hbm=True,
     )
     recv_c, recv_d = swap(send_c, "gy", 0), swap(send_d, "gy", 1)
-    send_a, send_b, edge, fl, fe = call(
-        pack_rows_kernel,
-        [lines(FIRST_LINES)] * 2 + [(pops,) + tile] + [(12, tiles) + tile] * 2,
-        [both(FIRST_LINES)],
-        [adj, own_left, own_right, recv_c, recv_d, fl_main, fe_main],
-    )
-    first_a, first_b = swap(send_a, "gx", 0), swap(send_b, "gx", 1)
-
-    def tiled(*counts):
-        return [(n, tiles) + tile for n in counts]
-
-    send_a, send_b, ab1, kept1, given1 = call(
-        late_kernel,
-        [lines(SECOND_LINES)] * 2 + tiled(6, 19, 3),
-        [both(FIRST_LINES), both(SECOND_LINES)] + tiled(21, 9),
-        [adj, edge, fl, first_a, first_b],
+    send_a, send_b = call(static_kernel, [static] * 2, [(2,) + static], [adj, fl_m, fe_m])
+    static_a, static_b = swap(send_a, "gx", 0), swap(send_b, "gx", 1)
+    pre = list(call(inside_kernel, main(9, 6, 19), [], [adj, fl_m]))
+    send_a, send_b, edge, fl_e, fe_e = call(
+        edge_kernel,
+        [second] * 2 + edges(pops, 12, 12),
+        [(2,) + second] + edges(9, 6, 19) + tiled(DYNAMIC),
+        [own_left, own_right, recv_c, recv_d, fl_m] + pre,
     )
     recv_a, recv_b = swap(send_a, "gx", 0), swap(send_b, "gx", 1)
-    forces, forces_rim, rims = call(
-        forces_kernel,
-        tiled(9, 9, len(KEPT_LINES)),
-        [both(FIRST_LINES)],
-        [fe, first_a, first_b, given1],
+    step = (RIMS, 9, 6, 19, 9, 6, 14, 9, 9)
+    mains = call(
+        main_kernel,
+        main(*step),
+        [(2,) + static],
+        [adj, fl_m, fe_m, static_a, static_b, fl_e],
     )
     (out,) = call(
-        early_kernel,
+        last_kernel,
         [(pops, planes) + tile],
-        [both(SECOND_LINES)]
-        + tiled(SECOND_LINES, pops, 15, 27, 15, 9, 9, 6, 19, 3)
-        + [(pops, planes) + tile, pltpu.SemaphoreType.DMA((planes,))],
-        [fl, fe, ab1, kept1, given1, forces, forces_rim, rims, recv_a, recv_b],
+        edges(*step)
+        + [(2,) + second]
+        + tiled(DYNAMIC, pops, 15, 27, 15, 9, 9, 6, 19, 3)
+        + main(pops)
+        + [pltpu.SemaphoreType.DMA((planes,))],
+        [fl_m, fe_m, edge, fl_e, fe_e, *mains] + [recv_a, recv_b],
         out_hbm=True,
     )
     return out

time: 29.3 us -> 26.9 us (0.918)
  waiting for transfers between devices: 8.62 us -> 5.27 us
  Pallas kernels: 8.55 us -> 11.2 us
  starting transfers between devices: 12 us -> 10.2 us
    ppermute x6, waiting for transfers between devices: 8.62 us -> 5.27 us  [swap(): return lax.ppermute(block, axis, route)]
    pallas_call x5 -> x6, Pallas kernels: 8.55 us -> 11.2 us  [call(): pl.pallas_call(kernel, out_shape=[jax.ShapeDtypeStruct(s, F32) for s in o...]
    ppermute x6, starting transfers between devices: 12 us -> 10.2 us  [swap(): return lax.ppermute(block, axis, route)]
  transfers between devices with their start and end apart: 6 -> 6, of which waited for: 4 -> 3; matrix products, arithmetic and copies ran while one was open for 0% -> 0% of each run, Pallas kernels for 3% -> 14%
where the time goes in v5:
time: 26.9 us; the launch traced here: 26.7 us
  Pallas kernels  11.2 us (42%)
  starting transfers between devices  10.2 us (38%)
  waiting for transfers between devices  5.27 us (20%)
    pallas_call x6, Pallas kernels, call(): pl.pallas_call(kernel, out_shape=[jax.ShapeDtypeStruct(s, F32) for s in o...  11.2 us
    ppermute x6, starting transfers between devices, swap(): return lax.ppermute(block, axis, route)  10.2 us
    ppermute x6, waiting for transfers between devices, swap(): return lax.ppermute(block, axis, route)  5.27 us
  transfers between devices with their start and end apart: 6, of which 3 were waited for; matrix products, arithmetic and copies ran while one was open for 0% of the time, Pallas kernels for 14%

profile of v5, /device:TPU:0, one launch (start us, length us, event | category | flops | bytes accessed | tf_op | source)
XLA Modules:
  0.0 26.7 jit_solution(1983152631662843179)
XLA Ops:
  0.0 2.0 %shard_map.55 = (f32[10,8,128]{2,1,0:T(8,128)S(1)}, f32[10,8,128]{2,1,0:T(8,128)S(1)}, f32[20,8,128]{2,1,0:T(8,128)S(1)}, f32[20,8,128]{2,1,0:T(8,128)S(1)}, f32...) custom-call(f32[57,4,8,128]{3,2,1,0:T(8,128)} %adj_in.1, ...), custom_call_target="tpu_custom_call" | custom-call | tf_op jit(solution)/shard_map/pallas_call | solution.py:914
  2.0 0.3 %shard_map.58 = (f32[352,128]{1,0:T(8,128)S(1)}, f32[352,128]{1,0:T(8,128)S(1)}) custom-call(f32[57,4,8,128]{3,2,1,0:T(8,128)S(1)} %get-tuple-element.37.adj, f32[12,4,8,128]{3,2,1,0:T(8,128)S(1)} %get-tuple-element.31.fl.fl_main.fl_m, f32[12,4,8,128]{3,2,1,0:T(8,128)S(1)} %get-tuple-element.32.fe.fe_m), custom_call_target="tpu_custom_call" | custom-call | tf_op jit(solution)/shard_map/pallas_call | solution.py:914
  2.3 3.0 %collective-permute-start.2 = (f32[352,128]{1,0:T(8,128)S(1)}, f32[352,128]{1,0:T(8,128)S(1)}, u32[]{:S(2)}, u32[]{:S(2)}) collective-permute-start(f32[352,128]{1,0:T(8,128)S(1)} %get-tuple-element.44), channel_id=1, source_target_pairs={{0,4},{4,0},{8,12},{12,8},{16,20},{20,16},{24,28},{28,24},{1,5},{5... | collective-permute-start | bytes 540680 | tf_op jit(solution)/shard_map/ppermute | solution.py:930
  5.4 3.5 %collective-permute-start.3 = (f32[352,128]{1,0:T(8,128)S(1)}, f32[352,128]{1,0:T(8,128)S(1)}, u32[]{:S(2)}, u32[]{:S(2)}) collective-permute-start(f32[352,128]{1,0:T(8,128)S(1)} %get-tuple-element.45), channel_id=1, source_target_pairs={{4,8},{8,4},{12,16},{16,12},{20,24},{24,20},{28,0},{0,28},{5,9},{9... | collective-permute-start | bytes 540680 | tf_op jit(solution)/shard_map/ppermute | solution.py:930
  8.9 0.0 collective-permute-start
  8.9 1.6 %collective-permute-start.1 = (f32[10,8,128]{2,1,0:T(8,128)S(1)}, f32[10,8,128]{2,1,0:T(8,128)S(1)}, u32[]{:S(2)}, u32[]{:S(2)}) collective-permute-start(f32[10,8,128]{2,1,0:T(8,128)S(1)} %get-tuple-element.36), channel_id=1, source_target_pairs={{1,2},{2,1},{3,0},{0,3},{5,6},{6,5},{7,4},{4,7},{9,10},{10,9},{11,... | collective-permute-start | bytes 122888 | tf_op jit(solution)/shard_map/ppermute | solution.py:930
  10.5 0.7 %shard_map.56 = (f32[9,4,8,128]{3,2,1,0:T(8,128)S(1)}, f32[6,4,8,128]{3,2,1,0:T(8,128)S(1)}, f32[19,4,8,128]{3,2,1,0:T(8,128)S(1)}) custom-call(f32[57,4,8,128]{3,2,1,0:T(8,128)S(1)} %get-tuple-element.37.adj, f32[12,4,8,128]{3,2,1,0:T(8,128)S(1)} %get-tuple-element.31.fl.fl_main.fl_m), custom_call_target="tpu_custom_call" | custom-call | tf_op jit(solution)/shard_map/pallas_call | solution.py:914
  11.2 0.0 collective-permute-done.recv_c
  11.3 1.1 %collective-permute-done.1.recv_d = f32[10,8,128]{2,1,0:T(8,128)S(1)} collective-permute-done((f32[10,8,128]{2,1,0:T(8,128)S(1)}, f32[10,8,128]{2,1,0:T(8,128)S(1)}, u32[]{:S(2)}, u32[]{:S(2)}) %collective-permute-start.1) | collective-permute-done | bytes 40992 | tf_op jit(solution)/shard_map/ppermute | solution.py:930
  12.3 1.4 %shard_map.57 = (f32[152,128]{1,0:T(8,128)S(1)}, f32[152,128]{1,0:T(8,128)S(1)}, f32[57,8,128]{2,1,0:T(8,128)S(1)}, f32[12,8,128]{2,1,0:T(8,128)S(1)}, f32[12,8,128]{2,1,0:T(8,128)S(1)}) custom-call(f32[20,8,128]{2,1,0:T(8,128)S(1)} %get-tuple-element.33.own_left, f32[20,8,128]{2,1,0:T(8,128)S(1)} %get-tuple-element.34.own_right, ...), custom_call_target="tpu_custom_call" | custom-call | tf_op jit(solution)/shard_map/pallas_call | solution.py:914
  13.7 0.1 collective-permute-start.4
  13.8 1.9 %collective-permute-start.5 = (f32[152,128]{1,0:T(8,128)S(1)}, f32[152,128]{1,0:T(8,128)S(1)}, u32[]{:S(2)}, u32[]{:S(2)}) collective-permute-start(f32[152,128]{1,0:T(8,128)S(1)} %get-tuple-element.56), channel_id=1, source_target_pairs={{4,8},{8,4},{12,16},{16,12},{20,24},{24,20},{28,0},{0,28},{5,9},{9... | collective-permute-start | bytes 233480 | tf_op jit(solution)/shard_map/ppermute | solution.py:930
  15.7 0.0 collective-permute-done.2.recv_a
  15.7 0.0 collective-permute-done.3.recv_b
  15.7 1.7 %shard_map.59 = (f32[93,4,8,128]{3,2,1,0:T(8,128)S(1)}, f32[9,4,8,128]{3,2,1,0:T(8,128)S(1)}, f32[6,4,8,128]{3,2,1,0:T(8,128)S(1)}, f32[19,4,8,128]{3,2,1,0:T(8,...) custom-call(f32[57,4,8,128]{3,2,1,0:T(8,128)S(1)} %get-tuple-element, ...), custom_call_target="tpu_custom_call" | custom-call | tf_op jit(solution)/shard_map/pallas_call | solution.py:914
  17.4 1.4 %collective-permute-done.4.recv_a = f32[152,128]{1,0:T(8,128)S(1)} collective-permute-done((f32[152,128]{1,0:T(8,128)S(1)}, f32[152,128]{1,0:T(8,128)S(1)}, u32[]{:S(2)}, u32[]{:S(2)}) %collective-permute-start.4) | collective-permute-done | bytes 77856 | tf_op jit(solution)/shard_map/ppermute | solution.py:930
  18.8 2.8 %collective-permute-done.5.recv_b = f32[152,128]{1,0:T(8,128)S(1)} collective-permute-done((f32[152,128]{1,0:T(8,128)S(1)}, f32[152,128]{1,0:T(8,128)S(1)}, u32[]{:S(2)}, u32[]{:S(2)}) %collective-permute-start.5) | collective-permute-done | bytes 77856 | tf_op jit(solution)/shard_map/ppermute | solution.py:930
  21.6 5.1 %shard_map.60 = f32[57,4,8,128]{3,2,1,0:T(8,128)} custom-call(f32[12,4,8,128]{3,2,1,0:T(8,128)S(1)} %get-tuple-element.31.fl.fl_main.fl_m, f32[12,4,8,128]{3,2,1,0:T(8,128)S(1)} %get-tuple-element.32.fe.fe_m, f32[57,8,128]{2,1,0:T(8,128)S(1)} %get-tuple-element.41.edge, f32[12,8,128]{2,1,0:T(8,128)S(1)} %get-tuple-element.42.after.fl_e, ...), custom_call_target="tpu_custom_call" | custom-call | tf_op jit(solution)/shard_map/pallas_call | solution.py:914
Async XLA Ops:
  2.3 13.4 %collective-permute-start.2 = (f32[352,128]{1,0:T(8,128)S(1)}, f32[352,128]{1,0:T(8,128)S(1)}, u32[]{:S(2)}, u32[]{:S(2)}) collective-permute-start(f32[352,128]{1,0:T(8,128)S(1)} %get-tuple-element.44), channel_id=1, source_target_pairs={{0,4},{4,0},{8,12},{12,8},{16,20},{20,16},{24,28},{28,24},{1,5},{5... | collective-permute-start | bytes 540680 | tf_op jit(solution)/shard_map/ppermute | solution.py:930
  5.4 10.3 %collective-permute-start.3 = (f32[352,128]{1,0:T(8,128)S(1)}, f32[352,128]{1,0:T(8,128)S(1)}, u32[]{:S(2)}, u32[]{:S(2)}) collective-permute-start(f32[352,128]{1,0:T(8,128)S(1)} %get-tuple-element.45), channel_id=1, source_target_pairs={{4,8},{8,4},{12,16},{16,12},{20,24},{24,20},{28,0},{0,28},{5,9},{9... | collective-permute-start | bytes 540680 | tf_op jit(solution)/shard_map/ppermute | solution.py:930
  8.9 2.3 %collective-permute-start = (f32[10,8,128]{2,1,0:T(8,128)S(1)}, f32[10,8,128]{2,1,0:T(8,128)S(1)}, u32[]{:S(2)}, u32[]{:S(2)}) collective-permute-start(f32[10,8,128]{2,1,0:T(8,128)S(1)} %get-tuple-element.35), channel_id=1, source_target_pairs={{0,1},{1,0},{2,3},{3,2},{4,5},{5,4},{6,7},{7,6},{8,9},{9,8},{10,11... | collective-permute-start | bytes 122888 | tf_op jit(solution)/shard_map/ppermute | solution.py:930
  8.9 3.4 %collective-permute-start.1 = (f32[10,8,128]{2,1,0:T(8,128)S(1)}, f32[10,8,128]{2,1,0:T(8,128)S(1)}, u32[]{:S(2)}, u32[]{:S(2)}) collective-permute-start(f32[10,8,128]{2,1,0:T(8,128)S(1)} %get-tuple-element.36), channel_id=1, source_target_pairs={{1,2},{2,1},{3,0},{0,3},{5,6},{6,5},{7,4},{4,7},{9,10},{10,9},{11,... | collective-permute-start | bytes 122888 | tf_op jit(solution)/shard_map/ppermute | solution.py:930
  13.7 5.1 %collective-permute-start.4 = (f32[152,128]{1,0:T(8,128)S(1)}, f32[152,128]{1,0:T(8,128)S(1)}, u32[]{:S(2)}, u32[]{:S(2)}) collective-permute-start(f32[152,128]{1,0:T(8,128)S(1)} %get-tuple-element.55), channel_id=1, source_target_pairs={{0,4},{4,0},{8,12},{12,8},{16,20},{20,16},{24,28},{28,24},{1,5},{5... | collective-permute-start | bytes 233480 | tf_op jit(solution)/shard_map/ppermute | solution.py:930
  13.8 7.8 %collective-permute-start.5 = (f32[152,128]{1,0:T(8,128)S(1)}, f32[152,128]{1,0:T(8,128)S(1)}, u32[]{:S(2)}, u32[]{:S(2)}) collective-permute-start(f32[152,128]{1,0:T(8,128)S(1)} %get-tuple-element.56), channel_id=1, source_target_pairs={{4,8},{8,4},{12,16},{16,12},{20,24},{24,20},{28,0},{0,28},{5,9},{9... | collective-permute-start | bytes 233480 | tf_op jit(solution)/shard_map/ppermute | solution.py:930

commit v6 on v5

--- a/solution.py
+++ b/solution.py
@@ -43,6 +43,7 @@
 DYNAMIC = 12
 F32 = jnp.float32
 CHUNKS = 4
+INSIDE_COST, EDGE_COST, MAIN_COST = 10**7, 10**8, 10**8
 VMEM_BYTES = 40 * 1024 * 1024
 HALO = 4
 
@@ -465,7 +466,7 @@
 
 
 def parity_of(axis):
-    return lax.rem(lax.axis_index(axis), 2)
+    return lax.rem(lax.axis_index(axis) + 1, 2)
 
 
 def lines_from(first, second, parity, lines):
@@ -596,13 +597,6 @@
         send_d[h] = jnp.where(even, left, right)
 
 
-def static_kernel(adj, fl, fe, send_a, send_b, lines):
-    planes, rows, cols = adj.shape[1:]
-    kinds = (adj, fl, fe)
-    pack_static(lambda kind, c, t: kinds[kind][c, t], range(planes), rows, lines, parity_of("gx"))
-    lines_to(send_a, send_b, lines)
-
-
 def inside_collision(grid, tile, load, fields, hold, ab, kept):
     forces = brick_forces(grid, tile, fields, None, 0, 0)
     brick_collision(grid, tile, load, None, fields, forces, hold, ab, kept)
@@ -611,20 +605,44 @@
         tile.put(hold, k, jnp.where(at_rim, 0.0, tile.get(hold, k)))
 
 
-def inside_kernel(adj, fl, hold, ab, kept):
-    grid = Grid(*adj.shape[1:])
-    grid.over_main(
-        lambda tile: inside_collision(
-            grid, tile, lambda c, dz: tile.get(adj, c, dz), fl, hold, ab, kept
-        )
-    )
+def second_row(grid, tile, fields, hold, ab, kept, sides):
+    low = grid.low()
+    rest = 1.0 - 1.0 / RELAXATION[2]
+    back = spread_inside(grid, tile, hold, fields)
+    alpha = [tile.get(ab, s) + (1.0 - tile.get(fields, 9 + s)) * back[s] for s in range(3)]
+    beta = [tile.get(ab, 3 + d) for d in range(3)]
+    ahead = -grid.outward() * beta[0]
+    for s in range(3):
+        tile.put(sides, s, back[s])
+    for s in range(2):
+        tile.put(sides, 3 + s, alpha[s] + ahead)
+        tile.put(sides, 5 + s, beta[1 + s])
+    for j, yz in enumerate(CROSS):
+        v = rest * jnp.where(low, tile.get(kept, AHEAD[j]), tile.get(kept, BEHIND[j]))
+        v = v + (alpha[2] + ahead)
+        tile.put(sides, 7 + j, v + mixed(yz, beta[1:]) if j else v)
+
+
+def static_kernel(adj, fl, fe, send_a, send_b, lines):
+    planes, rows, cols = adj.shape[1:]
+    kinds = (adj, fl, fe)
+    pack_static(lambda kind, c, t: kinds[kind][c, t], range(planes), rows, lines, parity_of("gx"))
+    lines_to(send_a, send_b, lines)
+
+
+def inside_kernel(adj, fl, sides, hold, ab, kept):
+    planes, rows, cols = adj.shape[1:]
+    grid = Grid(planes, rows, cols)
+    load = lambda tile: lambda c, dz: tile.get(adj, c, dz)
+    grid.over_main(lambda tile: inside_collision(grid, tile, load(tile), fl, hold, ab, kept))
+    grid.over_main(lambda tile: second_row(grid, tile, fl, hold, ab, kept, sides))
 
 
 def edge_kernel(
-    own_left, own_right, recv_c, recv_d, fl_main, hold_main, ab_main, kept_main,
+    own_left, own_right, recv_c, recv_d, sides_main,
     send_a, send_b, edge, fl, fe, lines, hold, ab, kept, sides,
 ):
-    planes, rows, cols = fl_main.shape[1:]
+    planes, rows, cols = sides_main.shape[1:]
     pops = edge.shape[0]
     grid = Grid(planes, rows, cols)
     even = parity_of("gy") == 0
@@ -657,42 +675,24 @@
                 field[k] = v
                 if k < 3:
                     field[9 + k] = psi_of(v)
-    fields = Pair(fl_main, fl)
-    hold, ab, kept = Pair(hold_main, hold), Pair(ab_main, ab), Pair(kept_main, kept)
-    adj = Pair(None, edge)
-    grid.over_edge(
-        lambda tile: inside_collision(
-            grid, tile, lambda c, dz: tile.get(adj, c, dz), fields, hold, ab, kept
-        )
-    )
-    low = grid.low()
-    inward = -grid.outward()
-    rest = 1.0 - 1.0 / RELAXATION[2]
-
-    def second_row(tile):
-        back = spread_inside(grid, tile, hold, fields)
-        alpha = [tile.get(ab, s) + (1.0 - tile.get(fields, 9 + s)) * back[s] for s in range(3)]
-        beta = [tile.get(ab, 3 + d) for d in range(3)]
-        ahead = inward * beta[0]
-        for s in range(3):
-            tile.put(sides, s, back[s])
-        for s in range(2):
-            tile.put(sides, 3 + s, alpha[s] + ahead)
-            tile.put(sides, 5 + s, beta[1 + s])
-        for j, yz in enumerate(CROSS):
-            v = rest * jnp.where(low, tile.get(kept, AHEAD[j]), tile.get(kept, BEHIND[j]))
-            v = v + (alpha[2] + ahead)
-            tile.put(sides, 7 + j, v + mixed(yz, beta[1:]) if j else v)
-
-    grid.over(second_row)
+    adj, fields, both = Pair(None, edge), Pair(None, fl), Pair(sides_main, sides)
+    hold, ab, kept = Pair(None, hold), Pair(None, ab), Pair(None, kept)
+
+    def inside(tile):
+        load = lambda c, dz: tile.get(adj, c, dz)
+        inside_collision(grid, tile, load, fields, hold, ab, kept)
+        second_row(grid, tile, fields, hold, ab, kept, both)
+
+    grid.over_edge(inside)
     parity = parity_of("gx")
     kinds = (edge, fl, fe)
     fill = pack_static(lambda kind, c, t: kinds[kind][c], (0,), rows, lines, parity)
     for c in range(DYNAMIC):
         depth = 0 if c < 3 else 1
         for t in range(grid.tiles):
-            lines[parity, fill : fill + 1, :] = sides[c, t, rows - 1 - depth : rows - depth, :]
-            lines[1 - parity, fill : fill + 1, :] = sides[c, t, depth : depth + 1, :]
+            v = both.at(c, t)
+            lines[parity, fill : fill + 1, :] = v[rows - 1 - depth : rows - depth, :]
+            lines[1 - parity, fill : fill + 1, :] = v[depth : depth + 1, :]
             fill += 1
     lines_to(send_a, send_b, lines)
 
@@ -735,9 +735,41 @@
         tile.put(rims, EARLY_PSI + s, psi_of(tile.get(rims, EARLY + s)))
 
 
+def finish_first(grid, tile, fl, rims, hold, ab, kept, hold_rim, ab_rim, mid, part):
+    rest = 1.0 - 1.0 / RELAXATION[2]
+    sign, at_rim = rim_sign(grid), grid.at_rim()
+    own_dip, rim_dip = (fl, 6), (rims, LATE + 6)
+    dip = [tile.get(fl, 6 + d) for d in range(3)]
+    dip_rim = [tile.get(rims, LATE + 6 + d) for d in range(3)]
+    dip_far = [tile.get(rims, LATE + FAR + 3 + d) for d in range(3)]
+    back = spread_inside(grid, tile, hold, fl)
+    inward = hand_over(grid, tile, hold_rim, rim_dip, dip, sign)
+    alpha = [
+        tile.get(ab, s)
+        + (1.0 - tile.get(fl, 9 + s)) * (back[s] + jnp.where(at_rim, inward[s], 0.0))
+        for s in range(3)
+    ]
+    beta = [tile.get(ab, 3 + d) for d in range(3)]
+    for q in range(19):
+        along = mixed(VELOCITY[q], beta) if q != 16 else None
+        for s in range(3):
+            v = alpha[s] if along is None else alpha[s] + along
+            if s == 2:
+                v = v + rest * tile.get(kept, q)
+            tile.put(mid, s * 19 + q, v)
+    given = hand_over(grid, tile, hold, own_dip, dip_rim, -sign)
+    level = spread_level(grid, tile, hold_rim, *rim_dip)
+    after = hand_over(grid, tile, hold_rim, rim_dip, dip_far, -sign)
+    for s in range(3):
+        open_share = 1.0 - tile.get(rims, LATE_PSI + s)
+        tile.put(part, s, tile.get(ab_rim, s) + open_share * (given[s] + level[s]))
+        tile.put(part, 3 + s, tile.get(ab_rim, 3 + s))
+        tile.put(part, 6 + s, (1.0 - tile.get(rims, LATE + FAR + s)) * after[s])
+
+
 def main_kernel(
     adj, fl, fe, recv_a, recv_b, after,
-    rims, hold, ab, kept, hold_rim, ab_rim, kept_rim, forces, forces_rim, lines,
+    rims, mid, part, kept_rim, forces, forces_rim, lines, hold, ab, kept, hold_rim, ab_rim,
 ):
     planes, rows, cols = adj.shape[1:]
     grid = Grid(planes, rows, cols)
@@ -753,16 +785,21 @@
         early_forces(grid, tile, fe, rims, forces, forces_rim)
 
     grid.over_main(step)
+    grid.over_main(
+        lambda tile: finish_first(
+            grid, tile, fl, rims, hold, ab, kept, hold_rim, ab_rim, mid, part
+        )
+    )
 
 
 def last_kernel(
-    fl_m, fe_m, edge, fl_e, fe_e, rims_m, hold_m, ab_m, kept_m, hold_rim_m, ab_rim_m, kept_rim_m,
-    forces_m, forces_rim_m, recv_a, recv_b, out,
-    rims_e, hold_e, ab_e, kept_e, hold_rim_e, ab_rim_e, kept_rim_e, forces_e, forces_rim_e,
-    lines, near, mid, rim_mid, rim_level, rim_far, hold2, hold_rim2, ab2, kept2, total, staged,
-    sems,
+    fe_m, rims_m, mid_m, part_m, kept_rim_m, forces_m, forces_rim_m, edge, fl_e, fe_e,
+    recv_a, recv_b, out,
+    rims_e, mid_e, part_e, kept_rim_e, forces_e, forces_rim_e, hold_e, ab_e, kept_e, hold_rim_e,
+    ab_rim_e, patches, lines, near, rim_mid, rim_level, rim_far, hold2, hold_rim2, ab2, kept2,
+    total, staged, sems,
 ):
-    planes, rows, cols = fl_m.shape[1:]
+    planes, rows, cols = fe_m.shape[1:]
     grid = Grid(planes, rows, cols)
     lines_from(recv_a, recv_b, parity_of("gx"), lines)
     for c in range(STATIC):
@@ -771,10 +808,8 @@
         for t in range(grid.tiles):
             k = STATIC + c * grid.tiles + t
             near[c, t] = grid.sides(lines[0, k : k + 1, :], lines[1, k : k + 1, :])
-    fl, fe, rims = Pair(fl_m, fl_e), Pair(fe_m, fe_e), Pair(rims_m, rims_e)
-    hold, ab, kept = Pair(hold_m, hold_e), Pair(ab_m, ab_e), Pair(kept_m, kept_e)
-    hold_rim, ab_rim = Pair(hold_rim_m, hold_rim_e), Pair(ab_rim_m, ab_rim_e)
-    kept_rim = Pair(kept_rim_m, kept_rim_e)
+    fe, rims, mid = Pair(fe_m, fe_e), Pair(rims_m, rims_e), Pair(mid_m, mid_e)
+    part, kept_rim = Pair(part_m, part_e), Pair(kept_rim_m, kept_rim_e)
     forces, forces_rim = Pair(forces_m, forces_e), Pair(forces_rim_m, forces_rim_e)
     rest = 1.0 - 1.0 / RELAXATION[2]
     at_rim = grid.at_rim()
@@ -782,46 +817,24 @@
     outward = grid.outward()
 
     def edge_steps(tile):
+        adj, fl = Pair(None, edge), Pair(None, fl_e)
+        hold, ab, kept = Pair(None, hold_e), Pair(None, ab_e), Pair(None, kept_e)
+        hold_rim, ab_rim = Pair(None, hold_rim_e), Pair(None, ab_rim_e)
         rim_psis(grid, tile, rims)
-        first_step(
-            grid, tile, Pair(None, edge), fl, rims, hold, ab, kept, hold_rim, ab_rim, kept_rim
-        )
+        first_step(grid, tile, adj, fl, rims, hold, ab, kept, hold_rim, ab_rim, kept_rim)
         early_forces(grid, tile, fe, rims, forces, forces_rim)
+        finish_first(grid, tile, fl, rims, hold, ab, kept, hold_rim, ab_rim, mid, part)
 
     grid.over_edge(edge_steps)
 
     def complete(tile):
         t = tile.index
-        own_dip, rim_dip = (fl, 6), (rims, LATE + 6)
-        dip = [tile.get(fl, 6 + d) for d in range(3)]
-        dip_rim = [tile.get(rims, LATE + 6 + d) for d in range(3)]
-        dip_far = [tile.get(rims, LATE + FAR + 3 + d) for d in range(3)]
-        back = spread_inside(grid, tile, hold, fl)
-        inward = hand_over(grid, tile, hold_rim, rim_dip, dip, sign)
         alpha = [
-            tile.get(ab, s)
-            + (1.0 - tile.get(fl, 9 + s)) * (back[s] + jnp.where(at_rim, inward[s], 0.0))
+            tile.get(part, s) + (1.0 - tile.get(rims, LATE_PSI + s)) * near[s, t]
             for s in range(3)
         ]
-        beta = [tile.get(ab, 3 + d) for d in range(3)]
-        for q in range(19):
-            along = mixed(VELOCITY[q], beta) if q != 16 else None
-            for s in range(3):
-                v = alpha[s] if along is None else alpha[s] + along
-                if s == 2:
-                    v = v + rest * tile.get(kept, q)
-                mid[s * 19 + q, t] = v
-        given = hand_over(grid, tile, hold, own_dip, dip_rim, -sign)
-        level = spread_level(grid, tile, hold_rim, *rim_dip)
-        alpha = [
-            tile.get(ab_rim, s)
-            + (1.0 - tile.get(rims, LATE_PSI + s)) * (given[s] + level[s] + near[s, t])
-            for s in range(3)
-        ]
-        beta = [tile.get(ab_rim, 3 + d) for d in range(3)]
-        given = hand_over(grid, tile, hold_rim, rim_dip, dip_far, -sign)
-        fixes = [(1.0 - tile.get(rims, LATE + FAR + s)) * given[s] for s in range(3)]
-        far = [near[3 + s, t] + fixes[s] for s in range(2)]
+        beta = [tile.get(part, 3 + d) for d in range(3)]
+        far = [near[3 + s, t] + tile.get(part, 6 + s) for s in range(2)]
         far_beta = [near[5 + d, t] for d in range(2)]
         ahead = outward * beta[0]
         for j, yz in enumerate(CROSS):
@@ -831,7 +844,7 @@
                 v = plus(side, alpha[s] + ahead)
                 if s == 2:
                     v = v + rest * tile.get(kept_rim, 9 + j)
-                    rim_far[10 + j, t] = near[7 + j, t] + fixes[2]
+                    rim_far[10 + j, t] = near[7 + j, t] + tile.get(part, 8)
                 else:
                     rim_far[s * 5 + j, t] = plus(side_far, far[s])
                 rim_mid[s * 5 + j, t] = v
@@ -878,37 +891,36 @@
             total[s, tile.index] = tile.get(ab2, s) + (1.0 - tile.get(fe, 9 + s)) * x
 
     grid.over(finish)
-    is_low, is_high = grid.lane < HALO, grid.lane >= cols - HALO
-
-    def to_out(p):
-        return pltpu.make_async_copy(staged.at[:, p], out.at[:, p], sems.at[p])
-
-    def emit(p, carry):
-        base = p * grid.width
-
-        def patched(main, edge):
-            low = pltpu.roll(edge, lax.rem(2 * cols - base - grid.group, cols), 1)
-            high = pltpu.roll(edge, lax.rem(2 * cols - base - 3 * grid.group, cols), 1)
-            return jnp.where(is_low, low, jnp.where(is_high, high, main))
-
-        alpha = [patched(total[s, p], total[s, planes]) for s in range(3)]
-        beta = [patched(ab2[3 + d, p], ab2[3 + d, planes]) for d in range(3)]
+    at_side = (grid.lane < HALO) | (grid.lane >= cols - HALO)
+    first_group = lax.rem(grid.lane, grid.width) < grid.group
+    sources = [total.at[s] for s in range(3)] + [ab2.at[3 + d] for d in range(3)]
+    sources += [kept2.at[q] for q in range(19)]
+    for i, ref in enumerate(sources):
+        v = ref[planes]
+        patches[i] = jnp.where(first_group, pltpu.roll(v, cols - 2 * grid.group, 1), v)
+    copies = []
+    for p in range(planes):
+        turn = (cols - p * grid.width - grid.group) % cols
+
+        def patched(i):
+            return jnp.where(at_side, pltpu.roll(patches[i], turn, 1), sources[i][p])
+
+        alpha = [patched(s) for s in range(3)]
+        beta = [patched(3 + d) for d in range(3)]
         for q in range(19):
             along = mixed(VELOCITY[q], beta) if q != 16 else None
             for s in range(3):
                 v = alpha[s] if along is None else alpha[s] + along
                 if s == 2:
-                    v = v + rest * patched(kept2[q, p], kept2[q, planes])
+                    v = v + rest * patched(6 + q)
                 staged[s * 19 + q, p] = v
-        to_out(p).start()
-        return carry
-
-    lax.fori_loop(0, planes, emit, 0)
-    for p in range(planes):
-        to_out(p).wait()
-
-
-def call(kernel, outs, scratch, args, in_hbm=False, out_hbm=False):
+        copies.append(pltpu.make_async_copy(staged.at[:, p], out.at[:, p], sems.at[p]))
+        copies[p].start()
+    for copy in copies:
+        copy.wait()
+
+
+def call(kernel, outs, scratch, args, in_hbm=False, out_hbm=False, cost=0):
     vmem = pl.BlockSpec(memory_space=pltpu.VMEM)
     hbm = pl.BlockSpec(memory_space=pltpu.HBM)
     return pl.pallas_call(
@@ -918,6 +930,7 @@
         out_specs=[hbm if out_hbm else vmem] * len(outs),
         scratch_shapes=[pltpu.VMEM(s, F32) if isinstance(s, tuple) else s for s in scratch],
         compiler_params=pltpu.CompilerParams(vmem_limit_bytes=VMEM_BYTES),
+        cost_estimate=pl.CostEstimate(flops=cost, bytes_accessed=cost, transcendentals=0),
     )(*[pltpu.with_memory_space_constraint(x, pltpu.HBM) if in_hbm else x for x in args])
 
 
@@ -962,33 +975,39 @@
         [adjoint_in, populations_late, populations_early, dipoles_late, dipoles_early],
         in_hbm=True,
     )
-    recv_c, recv_d = swap(send_c, "gy", 0), swap(send_d, "gy", 1)
-    send_a, send_b = call(static_kernel, [static] * 2, [(2,) + static], [adj, fl_m, fe_m])
-    static_a, static_b = swap(send_a, "gx", 0), swap(send_b, "gx", 1)
-    pre = list(call(inside_kernel, main(9, 6, 19), [], [adj, fl_m]))
+    recv_c, recv_d = swap(send_c, "gy", 1), swap(send_d, "gy", 0)
+    send_a, send_b = call(
+        static_kernel, [static] * 2, [(2,) + static], [adj, fl_m, fe_m]
+    )
+    (sides,) = call(
+        inside_kernel, main(DYNAMIC), main(9, 6, 19), [adj, fl_m], cost=INSIDE_COST
+    )
+    static_a, static_b = swap(send_a, "gx", 1), swap(send_b, "gx", 0)
     send_a, send_b, edge, fl_e, fe_e = call(
         edge_kernel,
         [second] * 2 + edges(pops, 12, 12),
-        [(2,) + second] + edges(9, 6, 19) + tiled(DYNAMIC),
-        [own_left, own_right, recv_c, recv_d, fl_m] + pre,
+        [(2,) + second] + edges(9, 6, 19, DYNAMIC),
+        [own_left, own_right, recv_c, recv_d, sides],
+        cost=EDGE_COST,
     )
-    recv_a, recv_b = swap(send_a, "gx", 0), swap(send_b, "gx", 1)
-    step = (RIMS, 9, 6, 19, 9, 6, 14, 9, 9)
+    recv_a, recv_b = swap(send_a, "gx", 1), swap(send_b, "gx", 0)
+    known = (RIMS, pops, 9, 14, 9, 9)
     mains = call(
         main_kernel,
-        main(*step),
-        [(2,) + static],
+        main(*known),
+        [(2,) + static] + main(9, 6, 19, 9, 6),
         [adj, fl_m, fe_m, static_a, static_b, fl_e],
+        cost=MAIN_COST,
     )
     (out,) = call(
         last_kernel,
         [(pops, planes) + tile],
-        edges(*step)
+        edges(*known, 9, 6, 19, 9, 6, 25)
         + [(2,) + second]
-        + tiled(DYNAMIC, pops, 15, 27, 15, 9, 9, 6, 19, 3)
+        + tiled(DYNAMIC, 15, 27, 15, 9, 9, 6, 19, 3)
         + main(pops)
         + [pltpu.SemaphoreType.DMA((planes,))],
-        [fl_m, fe_m, edge, fl_e, fe_e, *mains] + [recv_a, recv_b],
+        [fe_m, *mains, edge, fl_e, fe_e, recv_a, recv_b],
         out_hbm=True,
     )
     return out

time: 26.9 us -> 25.6 us (0.952)
  waiting for transfers between devices: 5.27 us -> 4.36 us
  starting transfers between devices: 10.2 us -> 9.84 us
    ppermute x6, waiting for transfers between devices: 5.27 us -> 4.36 us  [swap(): return lax.ppermute(block, axis, route)]
    ppermute x6, starting transfers between devices: 10.2 us -> 9.84 us  [swap(): return lax.ppermute(block, axis, route)]
  transfers between devices with their start and end apart: 6 -> 6, of which waited for: 3 -> 4; matrix products, arithmetic and copies ran while one was open for 0% -> 0% of each run, Pallas kernels for 14% -> 18%
where the time goes in v6:
time: 25.6 us; the launch traced here: 25.5 us
  Pallas kernels  11.2 us (44%)
  starting transfers between devices  9.84 us (38%)
  waiting for transfers between devices  4.36 us (17%)
    pallas_call x6, Pallas kernels, call(): pl.pallas_call(kernel, out_shape=[jax.ShapeDtypeStruct(s, F32) for s in o...  11.2 us
    ppermute x6, starting transfers between devices, swap(): return lax.ppermute(block, axis, route)  9.84 us
    ppermute x6, waiting for transfers between devices, swap(): return lax.ppermute(block, axis, route)  4.36 us
  transfers between devices with their start and end apart: 6, of which 4 were waited for; matrix products, arithmetic and copies ran while one was open for 0% of the time, Pallas kernels for 18%

profile of v6, /device:TPU:0, one launch (start us, length us, event | category | flops | bytes accessed | tf_op | source)
XLA Modules:
  0.0 25.5 jit_solution(10512798391109435177)
XLA Ops:
  0.0 2.0 %shard_map.55 = (f32[10,8,128]{2,1,0:T(8,128)S(1)}, f32[10,8,128]{2,1,0:T(8,128)S(1)}, f32[20,8,128]{2,1,0:T(8,128)S(1)}, f32[20,8,128]{2,1,0:T(8,128)S(1)}, f32...) custom-call(f32[57,4,8,128]{3,2,1,0:T(8,128)} %adj_in.1, ...), custom_call_target="tpu_custom_call" | custom-call | tf_op jit(solution)/shard_map/pallas_call | solution.py:926
  2.0 0.3 %shard_map.56 = (f32[352,128]{1,0:T(8,128)S(1)}, f32[352,128]{1,0:T(8,128)S(1)}) custom-call(f32[57,4,8,128]{3,2,1,0:T(8,128)S(1)} %get-tuple-element.26.adj, f32[12,4,8,128]{3,2,1,0:T(8,128)S(1)} %get-tuple-element.27.fl, f32[12,4,8,128]{3,2,1,0:T(8,128)S(1)} %get-tuple-element.25.fe.fe_m), custom_call_target="tpu_custom_call" | custom-call | tf_op jit(solution)/shard_map/pallas_call | solution.py:926
  2.3 6.1 %collective-permute-start = (f32[352,128]{1,0:T(8,128)S(1)}, f32[352,128]{1,0:T(8,128)S(1)}, u32[]{:S(2)}, u32[]{:S(2)}) collective-permute-start(f32[352,128]{1,0:T(8,128)S(1)} %get-tuple-element.28), channel_id=1, source_target_pairs={{4,8},{8,4},{12,16},{16,12},{20,24},{24,20},{28,0},{0,28},{5,9},{9... | collective-permute-start | bytes 540680 | tf_op jit(solution)/shard_map/ppermute | solution.py:943
  8.4 0.0 collective-permute-start.1
  8.4 0.7 %collective-permute-start.2 = (f32[10,8,128]{2,1,0:T(8,128)S(1)}, f32[10,8,128]{2,1,0:T(8,128)S(1)}, u32[]{:S(2)}, u32[]{:S(2)}) collective-permute-start(f32[10,8,128]{2,1,0:T(8,128)S(1)} %get-tuple-element.32), channel_id=1, source_target_pairs={{1,2},{2,1},{3,0},{0,3},{5,6},{6,5},{7,4},{4,7},{9,10},{10,9},{11,... | collective-permute-start | bytes 122888 | tf_op jit(solution)/shard_map/ppermute | solution.py:943
  9.1 1.0 %collective-permute-start.3 = (f32[10,8,128]{2,1,0:T(8,128)S(1)}, f32[10,8,128]{2,1,0:T(8,128)S(1)}, u32[]{:S(2)}, u32[]{:S(2)}) collective-permute-start(f32[10,8,128]{2,1,0:T(8,128)S(1)} %get-tuple-element.33), channel_id=1, source_target_pairs={{0,1},{1,0},{2,3},{3,2},{4,5},{5,4},{6,7},{7,6},{8,9},{9,8},{10,11... | collective-permute-start | bytes 122888 | tf_op jit(solution)/shard_map/ppermute | solution.py:943
  10.0 1.2 %shard_map.57.sides_main = f32[12,4,8,128]{3,2,1,0:T(8,128)S(1)} custom-call(f32[57,4,8,128]{3,2,1,0:T(8,128)S(1)} %get-tuple-element.26.adj, f32[12,4,8,128]{3,2,1,0:T(8,128)S(1)} %get-tuple-element.27.fl), custom_call_target="tpu_custom_call" | custom-call | flops 10000000 | bytes 10000000 | tf_op jit(solution)/shard_map/pallas_call | solution.py:926
  11.2 1.0 %collective-permute-done.2.recv_c = f32[10,8,128]{2,1,0:T(8,128)S(1)} collective-permute-done((f32[10,8,128]{2,1,0:T(8,128)S(1)}, f32[10,8,128]{2,1,0:T(8,128)S(1)}, u32[]{:S(2)}, u32[]{:S(2)}) %collective-permute-start.2) | collective-permute-done | bytes 40992 | tf_op jit(solution)/shard_map/ppermute | solution.py:943
  12.2 0.0 collective-permute-done.3.recv_d
  12.2 0.8 %shard_map.58 = (f32[152,128]{1,0:T(8,128)S(1)}, f32[152,128]{1,0:T(8,128)S(1)}, f32[57,8,128]{2,1,0:T(8,128)S(1)}, f32[12,8,128]{2,1,0:T(8,128)S(1)}, f32[12,8,128]{2,1,0:T(8,128)S(1)}) custom-call(f32[20,8,128]{2,1,0:T(8,128)S(1)} %get-tuple-element.30.own_left, f32[20,8,128]{2,1,0:T(8,128)S(1)} %get-tuple-element.31.own_right, ...), custom_call_target="tpu_custom_call" | custom-call | flops 100000000 | bytes 100000000 | tf_op jit(solution)/shard_map/pallas_call | solution.py:926
  13.0 2.0 %collective-permute-start.4 = (f32[152,128]{1,0:T(8,128)S(1)}, f32[152,128]{1,0:T(8,128)S(1)}, u32[]{:S(2)}, u32[]{:S(2)}) collective-permute-start(f32[152,128]{1,0:T(8,128)S(1)} %get-tuple-element.43), channel_id=1, source_target_pairs={{4,8},{8,4},{12,16},{16,12},{20,24},{24,20},{28,0},{0,28},{5,9},{9... | collective-permute-start | bytes 233480 | tf_op jit(solution)/shard_map/ppermute | solution.py:943
  15.0 0.2 collective-permute-start.5
  15.2 0.0 collective-permute-done.recv_a
  15.2 1.6 %collective-permute-done.1.recv_b = f32[352,128]{1,0:T(8,128)S(1)} collective-permute-done((f32[352,128]{1,0:T(8,128)S(1)}, f32[352,128]{1,0:T(8,128)S(1)}, u32[]{:S(2)}, u32[]{:S(2)}) %collective-permute-start.1) | collective-permute-done | bytes 180256 | tf_op jit(solution)/shard_map/ppermute | solution.py:943
  16.8 2.5 %shard_map.59 = (f32[93,4,8,128]{3,2,1,0:T(8,128)S(1)}, f32[57,4,8,128]{3,2,1,0:T(8,128)S(1)}, f32[9,4,8,128]{3,2,1,0:T(8,128)S(1)}, f32[14,4,8,128]{3,2,1,0:T(8...) custom-call(f32[57,4,8,128]{3,2,1,0:T(8,128)S(1)} %get-tuple-element.26.adj, ...), custom_call_target="tpu_custom_call" | custom-call | flops 100000000 | bytes 100000000 | tf_op jit(solution)/shard_map/pallas_call | solution.py:926
  19.3 1.0 %collective-permute-done.4.recv_a = f32[152,128]{1,0:T(8,128)S(1)} collective-permute-done((f32[152,128]{1,0:T(8,128)S(1)}, f32[152,128]{1,0:T(8,128)S(1)}, u32[]{:S(2)}, u32[]{:S(2)}) %collective-permute-start.4) | collective-permute-done | bytes 77856 | tf_op jit(solution)/shard_map/ppermute | solution.py:943
  20.3 0.7 %collective-permute-done.5.recv_b = f32[152,128]{1,0:T(8,128)S(1)} collective-permute-done((f32[152,128]{1,0:T(8,128)S(1)}, f32[152,128]{1,0:T(8,128)S(1)}, u32[]{:S(2)}, u32[]{:S(2)}) %collective-permute-start.5) | collective-permute-done | bytes 77856 | tf_op jit(solution)/shard_map/ppermute | solution.py:943
  21.0 4.4 %shard_map.60 = f32[57,4,8,128]{3,2,1,0:T(8,128)} custom-call(f32[12,4,8,128]{3,2,1,0:T(8,128)S(1)} %get-tuple-element.25.fe.fe_m, f32[93,4,8,128]{3,2,1,0:T(8,128)S(1)} %get-tuple-element.35.rims_m, f32[57,4,8,128]{3,2,1,0:T(8,128)S(1)} %get-tuple-element.36.mid_m, f32[9,4,8,128]{3,2,1,0:T(8,128)S(1)} %get-tuple-element.37.part_m, ...), custom_call_target="tpu_custom_call" | custom-call | tf_op jit(solution)/shard_map/pallas_call | solution.py:926
Async XLA Ops:
  2.3 12.9 %collective-permute-start = (f32[352,128]{1,0:T(8,128)S(1)}, f32[352,128]{1,0:T(8,128)S(1)}, u32[]{:S(2)}, u32[]{:S(2)}) collective-permute-start(f32[352,128]{1,0:T(8,128)S(1)} %get-tuple-element.28), channel_id=1, source_target_pairs={{4,8},{8,4},{12,16},{16,12},{20,24},{24,20},{28,0},{0,28},{5,9},{9... | collective-permute-start | bytes 540680 | tf_op jit(solution)/shard_map/ppermute | solution.py:943
  8.4 8.4 %collective-permute-start.1 = (f32[352,128]{1,0:T(8,128)S(1)}, f32[352,128]{1,0:T(8,128)S(1)}, u32[]{:S(2)}, u32[]{:S(2)}) collective-permute-start(f32[352,128]{1,0:T(8,128)S(1)} %get-tuple-element.29), channel_id=1, source_target_pairs={{0,4},{4,0},{8,12},{12,8},{16,20},{20,16},{24,28},{28,24},{1,5},{5... | collective-permute-start | bytes 540680 | tf_op jit(solution)/shard_map/ppermute | solution.py:943
  8.4 3.8 %collective-permute-start.2 = (f32[10,8,128]{2,1,0:T(8,128)S(1)}, f32[10,8,128]{2,1,0:T(8,128)S(1)}, u32[]{:S(2)}, u32[]{:S(2)}) collective-permute-start(f32[10,8,128]{2,1,0:T(8,128)S(1)} %get-tuple-element.32), channel_id=1, source_target_pairs={{1,2},{2,1},{3,0},{0,3},{5,6},{6,5},{7,4},{4,7},{9,10},{10,9},{11,... | collective-permute-start | bytes 122888 | tf_op jit(solution)/shard_map/ppermute | solution.py:943
  9.1 3.2 %collective-permute-start.3 = (f32[10,8,128]{2,1,0:T(8,128)S(1)}, f32[10,8,128]{2,1,0:T(8,128)S(1)}, u32[]{:S(2)}, u32[]{:S(2)}) collective-permute-start(f32[10,8,128]{2,1,0:T(8,128)S(1)} %get-tuple-element.33), channel_id=1, source_target_pairs={{0,1},{1,0},{2,3},{3,2},{4,5},{5,4},{6,7},{7,6},{8,9},{9,8},{10,11... | collective-permute-start | bytes 122888 | tf_op jit(solution)/shard_map/ppermute | solution.py:943
  13.0 7.3 %collective-permute-start.4 = (f32[152,128]{1,0:T(8,128)S(1)}, f32[152,128]{1,0:T(8,128)S(1)}, u32[]{:S(2)}, u32[]{:S(2)}) collective-permute-start(f32[152,128]{1,0:T(8,128)S(1)} %get-tuple-element.43), channel_id=1, source_target_pairs={{4,8},{8,4},{12,16},{16,12},{20,24},{24,20},{28,0},{0,28},{5,9},{9... | collective-permute-start | bytes 233480 | tf_op jit(solution)/shard_map/ppermute | solution.py:943
  15.0 6.0 %collective-permute-start.5 = (f32[152,128]{1,0:T(8,128)S(1)}, f32[152,128]{1,0:T(8,128)S(1)}, u32[]{:S(2)}, u32[]{:S(2)}) collective-permute-start(f32[152,128]{1,0:T(8,128)S(1)} %get-tuple-element.44), channel_id=1, source_target_pairs={{0,4},{4,0},{8,12},{12,8},{16,20},{20,16},{24,28},{28,24},{1,5},{5... | collective-permute-start | bytes 233480 | tf_op jit(solution)/shard_map/ppermute | solution.py:943

commit v7 on v6

--- a/solution.py
+++ b/solution.py
@@ -76,11 +76,8 @@
         return jnp.where(self.sub == 0, low, high)
 
     def over_main(self, body):
-        def step(p, carry):
+        for p in range(self.planes):
             body(Tile(self, p, False))
-            return carry
-
-        lax.fori_loop(0, self.planes, step, 0)
 
     def over_edge(self, body):
         body(Tile(self, self.planes, True))
@@ -106,7 +103,7 @@
     def of(self, dz):
         if dz == 0 or self.edge:
             return self.index
-        return lax.rem(self.index + (dz + self.grid.planes), self.grid.planes)
+        return (self.index + dz) % self.grid.planes
 
     def get(self, ref, c, dz=0):
         if isinstance(ref, Pair):
@@ -541,7 +538,7 @@
         copies[2 * which].wait()
         copies[2 * which + 1].wait()
 
-        def step(p, carry):
+        for p in range(planes):
             flows = [None] * 19
             rho = []
             for s in range(3):
@@ -561,9 +558,6 @@
                         momentum = plus(momentum, flows[q] if VELOCITY[q][d] > 0 else -flows[q])
                 out[3 + d, p] = momentum * inverse
                 out[6 + d, p] = dip[d, p].astype(F32)
-            return carry
-
-        lax.fori_loop(0, planes, step, 0)
     pops = adj.shape[0]
     components = pops + 18
     slot = grid.lane // grid.group

time: 25.6 us -> 25 us (0.977)
  Pallas kernels: 11.2 us -> 9.87 us
  waiting for transfers between devices: 4.36 us -> 5.12 us
    pallas_call x6, Pallas kernels: 11.2 us -> 9.87 us  [call(): pl.pallas_call(kernel, out_shape=[jax.ShapeDtypeStruct(s, F32) for s in o...]
    ppermute x6, waiting for transfers between devices: 4.36 us -> 5.12 us  [swap(): return lax.ppermute(block, axis, route)]
  transfers between devices with their start and end apart: 6 -> 6, of which waited for: 4 -> 4; matrix products, arithmetic and copies ran while one was open for 0% -> 0% of each run, Pallas kernels for 18% -> 15%
where the time goes in v7:
time: 25 us; the launch traced here: 24.9 us
  Pallas kernels  9.87 us (39%)
  starting transfers between devices  9.84 us (39%)
  waiting for transfers between devices  5.12 us (20%)
    pallas_call x6, Pallas kernels, call(): pl.pallas_call(kernel, out_shape=[jax.ShapeDtypeStruct(s, F32) for s in o...  9.87 us
    ppermute x6, starting transfers between devices, swap(): return lax.ppermute(block, axis, route)  9.84 us
    ppermute x6, waiting for transfers between devices, swap(): return lax.ppermute(block, axis, route)  5.12 us
  transfers between devices with their start and end apart: 6, of which 4 were waited for; matrix products, arithmetic and copies ran while one was open for 0% of the time, Pallas kernels for 15%

profile of v7, /device:TPU:0, one launch (start us, length us, event | category | flops | bytes accessed | tf_op | source)
XLA Modules:
  0.0 24.9 jit_solution(15470820104092890589)
XLA Ops:
  0.0 2.0 %shard_map.55 = (f32[10,8,128]{2,1,0:T(8,128)S(1)}, f32[10,8,128]{2,1,0:T(8,128)S(1)}, f32[20,8,128]{2,1,0:T(8,128)S(1)}, f32[20,8,128]{2,1,0:T(8,128)S(1)}, f32...) custom-call(f32[57,4,8,128]{3,2,1,0:T(8,128)} %adj_in.1, ...), custom_call_target="tpu_custom_call" | custom-call | tf_op jit(solution)/shard_map/pallas_call | solution.py:920
  2.0 0.3 %shard_map.56 = (f32[352,128]{1,0:T(8,128)S(1)}, f32[352,128]{1,0:T(8,128)S(1)}) custom-call(f32[57,4,8,128]{3,2,1,0:T(8,128)S(1)} %get-tuple-element.26.adj, f32[12,4,8,128]{3,2,1,0:T(8,128)S(1)} %get-tuple-element.27.fl, f32[12,4,8,128]{3,2,1,0:T(8,128)S(1)} %get-tuple-element.25.fe.fe_m), custom_call_target="tpu_custom_call" | custom-call | tf_op jit(solution)/shard_map/pallas_call | solution.py:920
  2.3 6.1 %collective-permute-start = (f32[352,128]{1,0:T(8,128)S(1)}, f32[352,128]{1,0:T(8,128)S(1)}, u32[]{:S(2)}, u32[]{:S(2)}) collective-permute-start(f32[352,128]{1,0:T(8,128)S(1)} %get-tuple-element.28), channel_id=1, source_target_pairs={{4,8},{8,4},{12,16},{16,12},{20,24},{24,20},{28,0},{0,28},{5,9},{9... | collective-permute-start | bytes 540680 | tf_op jit(solution)/shard_map/ppermute | solution.py:937
  8.4 0.0 collective-permute-start.1
  8.4 0.7 %collective-permute-start.2 = (f32[10,8,128]{2,1,0:T(8,128)S(1)}, f32[10,8,128]{2,1,0:T(8,128)S(1)}, u32[]{:S(2)}, u32[]{:S(2)}) collective-permute-start(f32[10,8,128]{2,1,0:T(8,128)S(1)} %get-tuple-element.32), channel_id=1, source_target_pairs={{1,2},{2,1},{3,0},{0,3},{5,6},{6,5},{7,4},{4,7},{9,10},{10,9},{11,... | collective-permute-start | bytes 122888 | tf_op jit(solution)/shard_map/ppermute | solution.py:937
  9.0 1.0 %collective-permute-start.3 = (f32[10,8,128]{2,1,0:T(8,128)S(1)}, f32[10,8,128]{2,1,0:T(8,128)S(1)}, u32[]{:S(2)}, u32[]{:S(2)}) collective-permute-start(f32[10,8,128]{2,1,0:T(8,128)S(1)} %get-tuple-element.33), channel_id=1, source_target_pairs={{0,1},{1,0},{2,3},{3,2},{4,5},{5,4},{6,7},{7,6},{8,9},{9,8},{10,11... | collective-permute-start | bytes 122888 | tf_op jit(solution)/shard_map/ppermute | solution.py:937
  10.0 0.8 %shard_map.57.sides_main = f32[12,4,8,128]{3,2,1,0:T(8,128)S(1)} custom-call(f32[57,4,8,128]{3,2,1,0:T(8,128)S(1)} %get-tuple-element.26.adj, f32[12,4,8,128]{3,2,1,0:T(8,128)S(1)} %get-tuple-element.27.fl), custom_call_target="tpu_custom_call" | custom-call | flops 10000000 | bytes 10000000 | tf_op jit(solution)/shard_map/pallas_call | solution.py:920
  10.8 1.4 %collective-permute-done.2.recv_c = f32[10,8,128]{2,1,0:T(8,128)S(1)} collective-permute-done((f32[10,8,128]{2,1,0:T(8,128)S(1)}, f32[10,8,128]{2,1,0:T(8,128)S(1)}, u32[]{:S(2)}, u32[]{:S(2)}) %collective-permute-start.2) | collective-permute-done | bytes 40992 | tf_op jit(solution)/shard_map/ppermute | solution.py:937
  12.2 0.0 collective-permute-done.3.recv_d
  12.2 0.8 %shard_map.58 = (f32[152,128]{1,0:T(8,128)S(1)}, f32[152,128]{1,0:T(8,128)S(1)}, f32[57,8,128]{2,1,0:T(8,128)S(1)}, f32[12,8,128]{2,1,0:T(8,128)S(1)}, f32[12,8,128]{2,1,0:T(8,128)S(1)}) custom-call(f32[20,8,128]{2,1,0:T(8,128)S(1)} %get-tuple-element.30.own_left, f32[20,8,128]{2,1,0:T(8,128)S(1)} %get-tuple-element.31.own_right, ...), custom_call_target="tpu_custom_call" | custom-call | flops 100000000 | bytes 100000000 | tf_op jit(solution)/shard_map/pallas_call | solution.py:920
  13.0 2.0 %collective-permute-start.4 = (f32[152,128]{1,0:T(8,128)S(1)}, f32[152,128]{1,0:T(8,128)S(1)}, u32[]{:S(2)}, u32[]{:S(2)}) collective-permute-start(f32[152,128]{1,0:T(8,128)S(1)} %get-tuple-element.43), channel_id=1, source_target_pairs={{4,8},{8,4},{12,16},{16,12},{20,24},{24,20},{28,0},{0,28},{5,9},{9... | collective-permute-start | bytes 233480 | tf_op jit(solution)/shard_map/ppermute | solution.py:937
  15.0 0.2 collective-permute-start.5
  15.2 0.0 collective-permute-done.recv_a
  15.2 1.6 %collective-permute-done.1.recv_b = f32[352,128]{1,0:T(8,128)S(1)} collective-permute-done((f32[352,128]{1,0:T(8,128)S(1)}, f32[352,128]{1,0:T(8,128)S(1)}, u32[]{:S(2)}, u32[]{:S(2)}) %collective-permute-start.1) | collective-permute-done | bytes 180256 | tf_op jit(solution)/shard_map/ppermute | solution.py:937
  16.8 2.1 %shard_map.59 = (f32[93,4,8,128]{3,2,1,0:T(8,128)S(1)}, f32[57,4,8,128]{3,2,1,0:T(8,128)S(1)}, f32[9,4,8,128]{3,2,1,0:T(8,128)S(1)}, f32[14,4,8,128]{3,2,1,0:T(8...) custom-call(f32[57,4,8,128]{3,2,1,0:T(8,128)S(1)} %get-tuple-element.26.adj, ...), custom_call_target="tpu_custom_call" | custom-call | flops 100000000 | bytes 100000000 | tf_op jit(solution)/shard_map/pallas_call | solution.py:920
  18.9 1.4 %collective-permute-done.4.recv_a = f32[152,128]{1,0:T(8,128)S(1)} collective-permute-done((f32[152,128]{1,0:T(8,128)S(1)}, f32[152,128]{1,0:T(8,128)S(1)}, u32[]{:S(2)}, u32[]{:S(2)}) %collective-permute-start.4) | collective-permute-done | bytes 77856 | tf_op jit(solution)/shard_map/ppermute | solution.py:937
  20.3 0.7 %collective-permute-done.5.recv_b = f32[152,128]{1,0:T(8,128)S(1)} collective-permute-done((f32[152,128]{1,0:T(8,128)S(1)}, f32[152,128]{1,0:T(8,128)S(1)}, u32[]{:S(2)}, u32[]{:S(2)}) %collective-permute-start.5) | collective-permute-done | bytes 77856 | tf_op jit(solution)/shard_map/ppermute | solution.py:937
  21.0 3.9 %shard_map.60 = f32[57,4,8,128]{3,2,1,0:T(8,128)} custom-call(f32[12,4,8,128]{3,2,1,0:T(8,128)S(1)} %get-tuple-element.25.fe.fe_m, f32[93,4,8,128]{3,2,1,0:T(8,128)S(1)} %get-tuple-element.35.rims_m, f32[57,4,8,128]{3,2,1,0:T(8,128)S(1)} %get-tuple-element.36.mid_m, f32[9,4,8,128]{3,2,1,0:T(8,128)S(1)} %get-tuple-element.37.part_m, ...), custom_call_target="tpu_custom_call" | custom-call | tf_op jit(solution)/shard_map/pallas_call | solution.py:920
Async XLA Ops:
  2.3 12.9 %collective-permute-start = (f32[352,128]{1,0:T(8,128)S(1)}, f32[352,128]{1,0:T(8,128)S(1)}, u32[]{:S(2)}, u32[]{:S(2)}) collective-permute-start(f32[352,128]{1,0:T(8,128)S(1)} %get-tuple-element.28), channel_id=1, source_target_pairs={{4,8},{8,4},{12,16},{16,12},{20,24},{24,20},{28,0},{0,28},{5,9},{9... | collective-permute-start | bytes 540680 | tf_op jit(solution)/shard_map/ppermute | solution.py:937
  8.4 8.4 %collective-permute-start.1 = (f32[352,128]{1,0:T(8,128)S(1)}, f32[352,128]{1,0:T(8,128)S(1)}, u32[]{:S(2)}, u32[]{:S(2)}) collective-permute-start(f32[352,128]{1,0:T(8,128)S(1)} %get-tuple-element.29), channel_id=1, source_target_pairs={{0,4},{4,0},{8,12},{12,8},{16,20},{20,16},{24,28},{28,24},{1,5},{5... | collective-permute-start | bytes 540680 | tf_op jit(solution)/shard_map/ppermute | solution.py:937
  8.4 3.8 %collective-permute-start.2 = (f32[10,8,128]{2,1,0:T(8,128)S(1)}, f32[10,8,128]{2,1,0:T(8,128)S(1)}, u32[]{:S(2)}, u32[]{:S(2)}) collective-permute-start(f32[10,8,128]{2,1,0:T(8,128)S(1)} %get-tuple-element.32), channel_id=1, source_target_pairs={{1,2},{2,1},{3,0},{0,3},{5,6},{6,5},{7,4},{4,7},{9,10},{10,9},{11,... | collective-permute-start | bytes 122888 | tf_op jit(solution)/shard_map/ppermute | solution.py:937
  9.0 3.2 %collective-permute-start.3 = (f32[10,8,128]{2,1,0:T(8,128)S(1)}, f32[10,8,128]{2,1,0:T(8,128)S(1)}, u32[]{:S(2)}, u32[]{:S(2)}) collective-permute-start(f32[10,8,128]{2,1,0:T(8,128)S(1)} %get-tuple-element.33), channel_id=1, source_target_pairs={{0,1},{1,0},{2,3},{3,2},{4,5},{5,4},{6,7},{7,6},{8,9},{9,8},{10,11... | collective-permute-start | bytes 122888 | tf_op jit(solution)/shard_map/ppermute | solution.py:937
  13.0 7.3 %collective-permute-start.4 = (f32[152,128]{1,0:T(8,128)S(1)}, f32[152,128]{1,0:T(8,128)S(1)}, u32[]{:S(2)}, u32[]{:S(2)}) collective-permute-start(f32[152,128]{1,0:T(8,128)S(1)} %get-tuple-element.43), channel_id=1, source_target_pairs={{4,8},{8,4},{12,16},{16,12},{20,24},{24,20},{28,0},{0,28},{5,9},{9... | collective-permute-start | bytes 233480 | tf_op jit(solution)/shard_map/ppermute | solution.py:937
  15.0 6.0 %collective-permute-start.5 = (f32[152,128]{1,0:T(8,128)S(1)}, f32[152,128]{1,0:T(8,128)S(1)}, u32[]{:S(2)}, u32[]{:S(2)}) collective-permute-start(f32[152,128]{1,0:T(8,128)S(1)} %get-tuple-element.44), channel_id=1, source_target_pairs={{0,4},{4,0},{8,12},{12,8},{16,20},{20,16},{24,28},{28,24},{1,5},{5... | collective-permute-start | bytes 233480 | tf_op jit(solution)/shard_map/ppermute | solution.py:937

commit v8 on v7

--- a/solution.py
+++ b/solution.py
@@ -92,6 +92,14 @@
     def low(self):
         return self.sub < self.rows // 2
 
+    def corners(self, j):
+        at = lax.rem(self.lane + (self.cols - j * self.group), self.width)
+        high = 3 * self.group
+        return ((at >= HALO) & (at < 2 * HALO)) | ((at >= high) & (at < high + HALO))
+
+    def turn(self, v, lanes):
+        return pltpu.roll(v, lanes % self.cols, 1) if lanes % self.cols else v
+
     def outward(self):
         return jnp.where(self.low(), -1.0, 1.0).astype(F32)
 
@@ -480,40 +488,46 @@
     return 1.0 - jnp.exp(-rho)
 
 
-def pack_static(get, tiles, rows, lines, parity):
+def static_rows():
+    for s in range(3):
+        for j in range(5):
+            yield 0, s * 19 + BEHIND[j], s * 19 + AHEAD[j], 0
+    for s in range(3):
+        for q in LEVEL:
+            yield 0, s * 19 + q, s * 19 + q, 0
+    for s in range(3):
+        for j in range(5):
+            yield 0, s * 19 + BEHIND[j], s * 19 + AHEAD[j], 1
+    for kind in (1, 2):
+        for c in range(9):
+            yield kind, c, c, 0
+        for c in (9, 10, 11, 6, 7, 8):
+            yield kind, c, c, 1
+
+
+def corner_groups(pack):
+    for depth in range(2):
+        found = [c for c, row in enumerate(static_rows()) if row[3] == depth]
+        for at in range(0, len(found), pack):
+            yield depth, found[at : at + pack]
+
+
+def pack_static(kinds, planes, rows, lines, parity):
     up, down = parity, 1 - parity
     fill = 0
-
-    def put(kind, above, below, depth):
-        nonlocal fill
-        for t in tiles:
-            v = get(kind, above, t)
+    for kind, above, below, depth in static_rows():
+        for p in range(planes):
+            v = kinds[kind][above, p]
             lines[up, fill : fill + 1, :] = v[rows - 1 - depth : rows - depth, :]
-            v = get(kind, below, t)
+            v = kinds[kind][below, p]
             lines[down, fill : fill + 1, :] = v[depth : depth + 1, :]
             fill += 1
 
-    for s in range(3):
-        for j in range(5):
-            put(0, s * 19 + BEHIND[j], s * 19 + AHEAD[j], 0)
-    for s in range(3):
-        for q in LEVEL:
-            put(0, s * 19 + q, s * 19 + q, 0)
-    for s in range(3):
-        for j in range(5):
-            put(0, s * 19 + BEHIND[j], s * 19 + AHEAD[j], 1)
-    for kind in (1, 2):
-        for c in range(9):
-            put(kind, c, c, 0)
-        for c in (9, 10, 11, 6, 7, 8):
-            put(kind, c, c, 1)
-    return fill
-
 
 def pack_columns_kernel(
     adj_in, late_in, early_in, dip_late_in, dip_early_in,
-    send_c, send_d, own_left, own_right, fl, fe, adj,
-    late, early, dip_late, dip_early, sems,
+    send_c, send_d, own_left, own_right, fl, fe, adj, send_a, send_b,
+    late, early, dip_late, dip_early, lines, sems,
 ):
     planes, rows, cols = adj.shape[1:]
     grid = Grid(planes, rows, cols)
@@ -589,6 +603,8 @@
         right = jnp.where(low, pltpu.roll(own_right[2 * h + 1], cols - HALO, 1), own_right[2 * h])
         send_c[h] = jnp.where(even, right, left)
         send_d[h] = jnp.where(even, left, right)
+    pack_static((adj, fl, fe), planes, rows, lines, parity_of("gx"))
+    lines_to(send_a, send_b, lines)
 
 
 def inside_collision(grid, tile, load, fields, hold, ab, kept):
@@ -615,13 +631,6 @@
         v = rest * jnp.where(low, tile.get(kept, AHEAD[j]), tile.get(kept, BEHIND[j]))
         v = v + (alpha[2] + ahead)
         tile.put(sides, 7 + j, v + mixed(yz, beta[1:]) if j else v)
-
-
-def static_kernel(adj, fl, fe, send_a, send_b, lines):
-    planes, rows, cols = adj.shape[1:]
-    kinds = (adj, fl, fe)
-    pack_static(lambda kind, c, t: kinds[kind][c, t], range(planes), rows, lines, parity_of("gx"))
-    lines_to(send_a, send_b, lines)
 
 
 def inside_kernel(adj, fl, sides, hold, ab, kept):
@@ -680,7 +689,21 @@
     grid.over_edge(inside)
     parity = parity_of("gx")
     kinds = (edge, fl, fe)
-    fill = pack_static(lambda kind, c, t: kinds[kind][c], (0,), rows, lines, parity)
+    rows_of = list(static_rows())
+    low = grid.low()
+    fill = 0
+    for depth, members in corner_groups(grid.pack):
+        v = None
+        for j, c in enumerate(members):
+            kind, above, below, unused = rows_of[c]
+            one = kinds[kind][above]
+            if above != below:
+                one = jnp.where(low, kinds[kind][below], one)
+            one = grid.turn(one, j * grid.group)
+            v = one if j == 0 else jnp.where(grid.corners(j), one, v)
+        lines[parity, fill : fill + 1, :] = v[rows - 1 - depth : rows - depth, :]
+        lines[1 - parity, fill : fill + 1, :] = v[depth : depth + 1, :]
+        fill += 1
     for c in range(DYNAMIC):
         depth = 0 if c < 3 else 1
         for t in range(grid.tiles):
@@ -763,7 +786,7 @@
 
 def main_kernel(
     adj, fl, fe, recv_a, recv_b, after,
-    rims, mid, part, kept_rim, forces, forces_rim, lines, hold, ab, kept, hold_rim, ab_rim,
+    rims, mid, part, kept_rim, forces, forces_rim, known, lines, hold, ab, kept, hold_rim, ab_rim,
 ):
     planes, rows, cols = adj.shape[1:]
     grid = Grid(planes, rows, cols)
@@ -773,6 +796,13 @@
             k = c * planes + p
             rims[c, p] = grid.sides(lines[0, k : k + 1, :], lines[1, k : k + 1, :])
     grid.over_main(lambda tile: rim_psis(grid, tile, rims))
+    left_half = lax.rem(grid.lane, grid.width) < grid.width // 2
+    for c in range(STATIC):
+        v = None
+        for p in range(planes):
+            one = grid.turn(rims[c, p], p * grid.width + 2 * grid.group)
+            v = one if p == 0 else jnp.where(grid.lane // grid.width == p, one, v)
+        known[c] = jnp.where(left_half, grid.turn(v, -grid.group), grid.turn(v, grid.group))
 
     def step(tile):
         first_step(grid, tile, adj, fl, rims, hold, ab, kept, hold_rim, ab_rim, kept_rim)
@@ -787,7 +817,7 @@
 
 
 def last_kernel(
-    fe_m, rims_m, mid_m, part_m, kept_rim_m, forces_m, forces_rim_m, edge, fl_e, fe_e,
+    fe_m, rims_m, mid_m, part_m, kept_rim_m, forces_m, forces_rim_m, known, edge, fl_e, fe_e,
     recv_a, recv_b, out,
     rims_e, mid_e, part_e, kept_rim_e, forces_e, forces_rim_e, hold_e, ab_e, kept_e, hold_rim_e,
     ab_rim_e, patches, lines, near, rim_mid, rim_level, rim_far, hold2, hold_rim2, ab2, kept2,
@@ -796,11 +826,16 @@
     planes, rows, cols = fe_m.shape[1:]
     grid = Grid(planes, rows, cols)
     lines_from(recv_a, recv_b, parity_of("gx"), lines)
-    for c in range(STATIC):
-        rims_e[c] = grid.sides(lines[0, c : c + 1, :], lines[1, c : c + 1, :])
+    is_corner = grid.corners(0)
+    corner_lines = 0
+    for k, (unused, members) in enumerate(corner_groups(grid.pack)):
+        v = grid.sides(lines[0, k : k + 1, :], lines[1, k : k + 1, :])
+        for j, c in enumerate(members):
+            rims_e[c] = jnp.where(is_corner, grid.turn(v, -j * grid.group), known[c])
+        corner_lines += 1
     for c in range(DYNAMIC):
         for t in range(grid.tiles):
-            k = STATIC + c * grid.tiles + t
+            k = corner_lines + c * grid.tiles + t
             near[c, t] = grid.sides(lines[0, k : k + 1, :], lines[1, k : k + 1, :])
     fe, rims, mid = Pair(fe_m, fe_e), Pair(rims_m, rims_e), Pair(mid_m, mid_e)
     part, kept_rim = Pair(part_m, part_e), Pair(kept_rim_m, kept_rim_e)
@@ -957,26 +992,23 @@
         return [(n, planes + 1) + tile for n in counts]
 
     static = lines(STATIC * planes)
-    second = lines(STATIC + DYNAMIC * (planes + 1))
-    send_c, send_d, own_left, own_right, fl_m, fe_m, adj = call(
+    second = lines(len(list(corner_groups(pack))) + DYNAMIC * (planes + 1))
+    send_c, send_d, own_left, own_right, fl_m, fe_m, adj, send_a, send_b = call(
         pack_columns_kernel,
-        edges(groups // 2, groups // 2, groups, groups) + main(12, 12, pops),
+        edges(groups // 2, groups // 2, groups, groups) + main(12, 12, pops) + [static] * 2,
         [
             pltpu.VMEM(x.shape, x.dtype)
             for x in (populations_late, populations_early, dipoles_late, dipoles_early)
         ]
-        + [pltpu.SemaphoreType.DMA((4 + CHUNKS,))],
+        + [(2,) + static, pltpu.SemaphoreType.DMA((4 + CHUNKS,))],
         [adjoint_in, populations_late, populations_early, dipoles_late, dipoles_early],
         in_hbm=True,
     )
+    static_a, static_b = swap(send_a, "gx", 1), swap(send_b, "gx", 0)
     recv_c, recv_d = swap(send_c, "gy", 1), swap(send_d, "gy", 0)
-    send_a, send_b = call(
-        static_kernel, [static] * 2, [(2,) + static], [adj, fl_m, fe_m]
-    )
     (sides,) = call(
         inside_kernel, main(DYNAMIC), main(9, 6, 19), [adj, fl_m], cost=INSIDE_COST
     )
-    static_a, static_b = swap(send_a, "gx", 1), swap(send_b, "gx", 0)
     send_a, send_b, edge, fl_e, fe_e = call(
         edge_kernel,
         [second] * 2 + edges(pops, 12, 12),
@@ -988,7 +1020,7 @@
     known = (RIMS, pops, 9, 14, 9, 9)
     mains = call(
         main_kernel,
-        main(*known),
+        main(*known) + edges(STATIC),
         [(2,) + static] + main(9, 6, 19, 9, 6),
         [adj, fl_m, fe_m, static_a, static_b, fl_e],
         cost=MAIN_COST,

time: 25 us -> 28.4 us (1.14)
  Pallas kernels: 9.87 us -> 15.6 us
  waiting for transfers between devices: 5.12 us -> 2.81 us
    pallas_call x6 -> x5, Pallas kernels: 9.87 us -> 15.6 us  [call(): pl.pallas_call(kernel, out_shape=[jax.ShapeDtypeStruct(s, F32) for s in o...]
    ppermute x6, waiting for transfers between devices: 5.12 us -> 2.81 us  [swap(): return lax.ppermute(block, axis, route)]
  transfers between devices with their start and end apart: 6 -> 6, of which waited for: 4 -> 2; matrix products, arithmetic and copies ran while one was open for 0% -> 0% of each run, Pallas kernels for 15% -> 33%
where the time goes in v8:
time: 28.4 us; the launch traced here: 28.3 us
  Pallas kernels  15.6 us (55%)
  starting transfers between devices  9.84 us (35%)
  waiting for transfers between devices  2.81 us (10%)
    pallas_call x5, Pallas kernels, call(): pl.pallas_call(kernel, out_shape=[jax.ShapeDtypeStruct(s, F32) for s in o...  15.6 us
    ppermute x6, starting transfers between devices, swap(): return lax.ppermute(block, axis, route)  9.84 us
    ppermute x6, waiting for transfers between devices, swap(): return lax.ppermute(block, axis, route)  2.81 us
  transfers between devices with their start and end apart: 6, of which 2 were waited for; matrix products, arithmetic and copies ran while one was open for 0% of the time, Pallas kernels for 33%

profile of v8, /device:TPU:0, one launch (start us, length us, event | category | flops | bytes accessed | tf_op | source)
XLA Modules:
  0.0 28.3 jit_solution(13960026481055384642)
XLA Ops:
  0.0 2.2 %shard_map.55 = (f32[10,8,128]{2,1,0:T(8,128)S(1)}, f32[10,8,128]{2,1,0:T(8,128)S(1)}, f32[20,8,128]{2,1,0:T(8,128)S(1)}, f32[20,8,128]{2,1,0:T(8,128)S(1)}, f32...) custom-call(f32[57,4,8,128]{3,2,1,0:T(8,128)} %adj_in.1, ...), custom_call_target="tpu_custom_call" | custom-call | tf_op jit(solution)/shard_map/pallas_call | solution.py:955
  2.2 6.1 %collective-permute-start = (f32[352,128]{1,0:T(8,128)S(1)}, f32[352,128]{1,0:T(8,128)S(1)}, u32[]{:S(2)}, u32[]{:S(2)}) collective-permute-start(f32[352,128]{1,0:T(8,128)S(1)} %get-tuple-element.29), channel_id=1, source_target_pairs={{4,8},{8,4},{12,16},{16,12},{20,24},{24,20},{28,0},{0,28},{5,9},{9... | collective-permute-start | bytes 540680 | tf_op jit(solution)/shard_map/ppermute | solution.py:972
  8.3 0.0 collective-permute-start.1
  8.3 0.7 %collective-permute-start.2 = (f32[10,8,128]{2,1,0:T(8,128)S(1)}, f32[10,8,128]{2,1,0:T(8,128)S(1)}, u32[]{:S(2)}, u32[]{:S(2)}) collective-permute-start(f32[10,8,128]{2,1,0:T(8,128)S(1)} %get-tuple-element.33), channel_id=1, source_target_pairs={{1,2},{2,1},{3,0},{0,3},{5,6},{6,5},{7,4},{4,7},{9,10},{10,9},{11,... | collective-permute-start | bytes 122888 | tf_op jit(solution)/shard_map/ppermute | solution.py:972
  8.9 1.0 %collective-permute-start.3 = (f32[10,8,128]{2,1,0:T(8,128)S(1)}, f32[10,8,128]{2,1,0:T(8,128)S(1)}, u32[]{:S(2)}, u32[]{:S(2)}) collective-permute-start(f32[10,8,128]{2,1,0:T(8,128)S(1)} %get-tuple-element.34), channel_id=1, source_target_pairs={{0,1},{1,0},{2,3},{3,2},{4,5},{5,4},{6,7},{7,6},{8,9},{9,8},{10,11... | collective-permute-start | bytes 122888 | tf_op jit(solution)/shard_map/ppermute | solution.py:972
  9.9 0.8 %shard_map.56.sides_main = f32[12,4,8,128]{3,2,1,0:T(8,128)S(1)} custom-call(f32[57,4,8,128]{3,2,1,0:T(8,128)S(1)} %get-tuple-element.27.adj, f32[12,4,8,128]{3,2,1,0:T(8,128)S(1)} %get-tuple-element.28.fl), custom_call_target="tpu_custom_call" | custom-call | flops 10000000 | bytes 10000000 | tf_op jit(solution)/shard_map/pallas_call | solution.py:955
  10.7 1.4 %collective-permute-done.2.recv_c = f32[10,8,128]{2,1,0:T(8,128)S(1)} collective-permute-done((f32[10,8,128]{2,1,0:T(8,128)S(1)}, f32[10,8,128]{2,1,0:T(8,128)S(1)}, u32[]{:S(2)}, u32[]{:S(2)}) %collective-permute-start.2) | collective-permute-done | bytes 40992 | tf_op jit(solution)/shard_map/ppermute | solution.py:972
  12.1 0.0 collective-permute-done.3.recv_d
  12.1 1.0 %shard_map.57 = (f32[88,128]{1,0:T(8,128)S(1)}, f32[88,128]{1,0:T(8,128)S(1)}, f32[57,8,128]{2,1,0:T(8,128)S(1)}, f32[12,8,128]{2,1,0:T(8,128)S(1)}, f32[12,8,128]{2,1,0:T(8,128)S(1)}) custom-call(f32[20,8,128]{2,1,0:T(8,128)S(1)} %get-tuple-element.31.own_left, f32[20,8,128]{2,1,0:T(8,128)S(1)} %get-tuple-element.32.own_right, ...), custom_call_target="tpu_custom_call" | custom-call | flops 100000000 | bytes 100000000 | tf_op jit(solution)/shard_map/pallas_call | solution.py:955
  13.1 2.0 %collective-permute-start.4 = (f32[88,128]{1,0:T(8,128)S(1)}, f32[88,128]{1,0:T(8,128)S(1)}, u32[]{:S(2)}, u32[]{:S(2)}) collective-permute-start(f32[88,128]{1,0:T(8,128)S(1)} %get-tuple-element.45), channel_id=1, source_target_pairs={{4,8},{8,4},{12,16},{16,12},{20,24},{24,20},{28,0},{0,28},{5,9},{9... | collective-permute-start | bytes 135176 | tf_op jit(solution)/shard_map/ppermute | solution.py:972
  15.1 0.2 collective-permute-start.5
  15.3 0.0 collective-permute-done.recv_a
  15.3 1.4 %collective-permute-done.1.recv_b = f32[352,128]{1,0:T(8,128)S(1)} collective-permute-done((f32[352,128]{1,0:T(8,128)S(1)}, f32[352,128]{1,0:T(8,128)S(1)}, u32[]{:S(2)}, u32[]{:S(2)}) %collective-permute-start.1) | collective-permute-done | bytes 180256 | tf_op jit(solution)/shard_map/ppermute | solution.py:972
  16.7 7.4 %shard_map.58 = (f32[93,4,8,128]{3,2,1,0:T(8,128)S(1)}, f32[57,4,8,128]{3,2,1,0:T(8,128)S(1)}, f32[9,4,8,128]{3,2,1,0:T(8,128)S(1)}, f32[14,4,8,128]{3,2,1,0:T(8...) custom-call(f32[57,4,8,128]{3,2,1,0:T(8,128)S(1)} %get-tuple-element.27.adj, ...), custom_call_target="tpu_custom_call" | custom-call | flops 100000000 | bytes 100000000 | tf_op jit(solution)/shard_map/pallas_call | solution.py:955
  24.1 0.0 collective-permute-done.4.recv_a
  24.1 0.0 collective-permute-done.5.recv_b
  24.1 4.2 %shard_map.59 = f32[57,4,8,128]{3,2,1,0:T(8,128)} custom-call(f32[12,4,8,128]{3,2,1,0:T(8,128)S(1)} %get-tuple-element.26.fe.fe_m, f32[93,4,8,128]{3,2,1,0:T(8,128)S(1)} %get-tuple-element.36.rims_m, f32[57,4,8,128]{3,2,1,0:T(8,128)S(1)} %get-tuple-element.37.mid_m, f32[9,4,8,128]{3,2,1,0:T(8,128)S(1)} %get-tuple-element.38.part_m, ...), custom_call_target="tpu_custom_call" | custom-call | tf_op jit(solution)/shard_map/pallas_call | solution.py:955
Async XLA Ops:
  2.2 13.1 %collective-permute-start = (f32[352,128]{1,0:T(8,128)S(1)}, f32[352,128]{1,0:T(8,128)S(1)}, u32[]{:S(2)}, u32[]{:S(2)}) collective-permute-start(f32[352,128]{1,0:T(8,128)S(1)} %get-tuple-element.29), channel_id=1, source_target_pairs={{4,8},{8,4},{12,16},{16,12},{20,24},{24,20},{28,0},{0,28},{5,9},{9... | collective-permute-start | bytes 540680 | tf_op jit(solution)/shard_map/ppermute | solution.py:972
  8.3 8.4 %collective-permute-start.1 = (f32[352,128]{1,0:T(8,128)S(1)}, f32[352,128]{1,0:T(8,128)S(1)}, u32[]{:S(2)}, u32[]{:S(2)}) collective-permute-start(f32[352,128]{1,0:T(8,128)S(1)} %get-tuple-element.30), channel_id=1, source_target_pairs={{0,4},{4,0},{8,12},{12,8},{16,20},{20,16},{24,28},{28,24},{1,5},{5... | collective-permute-start | bytes 540680 | tf_op jit(solution)/shard_map/ppermute | solution.py:972
  8.3 3.8 %collective-permute-start.2 = (f32[10,8,128]{2,1,0:T(8,128)S(1)}, f32[10,8,128]{2,1,0:T(8,128)S(1)}, u32[]{:S(2)}, u32[]{:S(2)}) collective-permute-start(f32[10,8,128]{2,1,0:T(8,128)S(1)} %get-tuple-element.33), channel_id=1, source_target_pairs={{1,2},{2,1},{3,0},{0,3},{5,6},{6,5},{7,4},{4,7},{9,10},{10,9},{11,... | collective-permute-start | bytes 122888 | tf_op jit(solution)/shard_map/ppermute | solution.py:972
  8.9 3.2 %collective-permute-start.3 = (f32[10,8,128]{2,1,0:T(8,128)S(1)}, f32[10,8,128]{2,1,0:T(8,128)S(1)}, u32[]{:S(2)}, u32[]{:S(2)}) collective-permute-start(f32[10,8,128]{2,1,0:T(8,128)S(1)} %get-tuple-element.34), channel_id=1, source_target_pairs={{0,1},{1,0},{2,3},{3,2},{4,5},{5,4},{6,7},{7,6},{8,9},{9,8},{10,11... | collective-permute-start | bytes 122888 | tf_op jit(solution)/shard_map/ppermute | solution.py:972
  13.1 11.0 %collective-permute-start.4 = (f32[88,128]{1,0:T(8,128)S(1)}, f32[88,128]{1,0:T(8,128)S(1)}, u32[]{:S(2)}, u32[]{:S(2)}) collective-permute-start(f32[88,128]{1,0:T(8,128)S(1)} %get-tuple-element.45), channel_id=1, source_target_pairs={{4,8},{8,4},{12,16},{16,12},{20,24},{24,20},{28,0},{0,28},{5,9},{9... | collective-permute-start | bytes 135176 | tf_op jit(solution)/shard_map/ppermute | solution.py:972
  15.1 9.0 %collective-permute-start.5 = (f32[88,128]{1,0:T(8,128)S(1)}, f32[88,128]{1,0:T(8,128)S(1)}, u32[]{:S(2)}, u32[]{:S(2)}) collective-permute-start(f32[88,128]{1,0:T(8,128)S(1)} %get-tuple-element.46), channel_id=1, source_target_pairs={{0,4},{4,0},{8,12},{12,8},{16,20},{20,16},{24,28},{28,24},{1,5},{5... | collective-permute-start | bytes 135176 | tf_op jit(solution)/shard_map/ppermute | solution.py:972

commit v9 on v8

--- a/solution.py
+++ b/solution.py
@@ -57,6 +57,22 @@
         self.pack = self.width // self.group
         self.sub = lax.broadcasted_iota(jnp.int32, (rows, cols), 0)
         self.lane = lax.broadcasted_iota(jnp.int32, (rows, cols), 1)
+        self.masks = {}
+
+    def once(self, name, make):
+        if name not in self.masks:
+            self.masks[name] = make()
+        return self.masks[name]
+
+    def in_width(self):
+        return self.once("width", lambda: lax.rem(self.lane, self.width))
+
+    def plane_lanes(self, p):
+        low, high = p * self.width, (p + 1) * self.width
+        return self.once(("plane", p), lambda: (self.lane >= low) & (self.lane < high))
+
+    def left_half(self):
+        return self.once("left", lambda: self.in_width() < self.width // 2)
 
     def roll_rows(self, v, dx):
         return pltpu.roll(v, (-dx) % self.rows, 0)
@@ -87,21 +103,27 @@
         self.over_edge(body)
 
     def at_rim(self):
-        return (self.sub == 0) | (self.sub == self.rows - 1)
+        return self.once("rim", lambda: (self.sub == 0) | (self.sub == self.rows - 1))
 
     def low(self):
-        return self.sub < self.rows // 2
+        return self.once("low", lambda: self.sub < self.rows // 2)
 
     def corners(self, j):
-        at = lax.rem(self.lane + (self.cols - j * self.group), self.width)
-        high = 3 * self.group
-        return ((at >= HALO) & (at < 2 * HALO)) | ((at >= high) & (at < high + HALO))
+        return self.once(("corner", j), lambda: self.make_corners(j))
+
+    def make_corners(self, j):
+        at, inside = self.in_width(), None
+        for low in (HALO, 3 * self.group):
+            low = (low + j * self.group) % self.width
+            window = (at >= low) & (at < low + HALO)
+            inside = window if inside is None else inside | window
+        return inside
 
     def turn(self, v, lanes):
         return pltpu.roll(v, lanes % self.cols, 1) if lanes % self.cols else v
 
     def outward(self):
-        return jnp.where(self.low(), -1.0, 1.0).astype(F32)
+        return self.once("out", lambda: jnp.where(self.low(), -1.0, 1.0).astype(F32))
 
 
 class Tile:
@@ -442,9 +464,7 @@
 
 
 def rim_sign(grid):
-    return jnp.where(
-        grid.sub == 0, -1.0, jnp.where(grid.sub == grid.rows - 1, 1.0, 0.0)
-    ).astype(F32)
+    return grid.once("sign", lambda: jnp.where(grid.at_rim(), grid.outward(), 0.0))
 
 
 def hand_over(grid, tile, hold, hold_dip, target, sign):
@@ -592,8 +612,12 @@
                     v = fe[c - pops - 9, p]
                 at = p * grid.pack + j
                 rolled = pltpu.roll(v, at * grid.group, 1) if at else v
-                left = jnp.where(slot == at, rolled, left)
-                right = jnp.where(slot == (at - 1) % (cols // grid.group), rolled, right)
+                here, prior = [
+                    grid.once(("slot", k), lambda: slot == k)
+                    for k in (at, (at - 1) % (cols // grid.group))
+                ]
+                left = jnp.where(here, rolled, left)
+                right = jnp.where(prior, rolled, right)
         own_left[g] = left
         own_right[g] = right
     low = lax.rem(grid.lane, grid.group) < HALO
@@ -650,7 +674,7 @@
     grid = Grid(planes, rows, cols)
     even = parity_of("gy") == 0
     slot = lax.rem(grid.lane // grid.group, grid.pack)
-    left_half = lax.rem(grid.lane, grid.width) < grid.width // 2
+    left_half = grid.left_half()
     components = pops + 18
     for g in range(own_left.shape[0]):
         first, second = recv_c[g // 2], recv_d[g // 2]
@@ -663,7 +687,7 @@
             c = g * grid.pack + j
             if c >= components:
                 continue
-            before = slot == (j - 1) % grid.pack
+            before = grid.once(("slot", j), lambda: slot == (j - 1) % grid.pack)
             low = jnp.where(before, from_prior, own_left[g])
             high = jnp.where(before, own_right[g], from_next)
             v = jnp.where(
@@ -796,13 +820,12 @@
             k = c * planes + p
             rims[c, p] = grid.sides(lines[0, k : k + 1, :], lines[1, k : k + 1, :])
     grid.over_main(lambda tile: rim_psis(grid, tile, rims))
-    left_half = lax.rem(grid.lane, grid.width) < grid.width // 2
     for c in range(STATIC):
         v = None
         for p in range(planes):
             one = grid.turn(rims[c, p], p * grid.width + 2 * grid.group)
-            v = one if p == 0 else jnp.where(grid.lane // grid.width == p, one, v)
-        known[c] = jnp.where(left_half, grid.turn(v, -grid.group), grid.turn(v, grid.group))
+            v = one if p == 0 else jnp.where(grid.plane_lanes(p), one, v)
+        known[c] = jnp.where(grid.left_half(), grid.turn(v, -grid.group), grid.turn(v, grid.group))
 
     def step(tile):
         first_step(grid, tile, adj, fl, rims, hold, ab, kept, hold_rim, ab_rim, kept_rim)

time: 28.4 us -> 28.5 us (level)
  no operation moved by 1% of the time
where the time goes in v9:
time: 28.5 us; the launch traced here: 28.3 us
  Pallas kernels  15.6 us (55%)
  starting transfers between devices  9.84 us (35%)
  waiting for transfers between devices  2.81 us (10%)
    pallas_call x5, Pallas kernels, call(): pl.pallas_call(kernel, out_shape=[jax.ShapeDtypeStruct(s, F32) for s in o...  15.6 us
    ppermute x6, starting transfers between devices, swap(): return lax.ppermute(block, axis, route)  9.84 us
    ppermute x6, waiting for transfers between devices, swap(): return lax.ppermute(block, axis, route)  2.81 us
  transfers between devices with their start and end apart: 6, of which 2 were waited for; matrix products, arithmetic and copies ran while one was open for 0% of the time, Pallas kernels for 33%

profile of v9, /device:TPU:0, one launch (start us, length us, event | category | flops | bytes accessed | tf_op | source)
XLA Modules:
  0.0 28.3 jit_solution(11060650402750043847)
XLA Ops:
  0.0 2.2 %shard_map.55 = (f32[10,8,128]{2,1,0:T(8,128)S(1)}, f32[10,8,128]{2,1,0:T(8,128)S(1)}, f32[20,8,128]{2,1,0:T(8,128)S(1)}, f32[20,8,128]{2,1,0:T(8,128)S(1)}, f32...) custom-call(f32[57,4,8,128]{3,2,1,0:T(8,128)} %adj_in.1, ...), custom_call_target="tpu_custom_call" | custom-call | tf_op jit(solution)/shard_map/pallas_call | solution.py:978
  2.2 6.1 %collective-permute-start = (f32[352,128]{1,0:T(8,128)S(1)}, f32[352,128]{1,0:T(8,128)S(1)}, u32[]{:S(2)}, u32[]{:S(2)}) collective-permute-start(f32[352,128]{1,0:T(8,128)S(1)} %get-tuple-element.29), channel_id=1, source_target_pairs={{4,8},{8,4},{12,16},{16,12},{20,24},{24,20},{28,0},{0,28},{5,9},{9... | collective-permute-start | bytes 540680 | tf_op jit(solution)/shard_map/ppermute | solution.py:995
  8.3 0.0 collective-permute-start.1
  8.3 0.7 %collective-permute-start.2 = (f32[10,8,128]{2,1,0:T(8,128)S(1)}, f32[10,8,128]{2,1,0:T(8,128)S(1)}, u32[]{:S(2)}, u32[]{:S(2)}) collective-permute-start(f32[10,8,128]{2,1,0:T(8,128)S(1)} %get-tuple-element.33), channel_id=1, source_target_pairs={{1,2},{2,1},{3,0},{0,3},{5,6},{6,5},{7,4},{4,7},{9,10},{10,9},{11,... | collective-permute-start | bytes 122888 | tf_op jit(solution)/shard_map/ppermute | solution.py:995
  8.9 1.0 %collective-permute-start.3 = (f32[10,8,128]{2,1,0:T(8,128)S(1)}, f32[10,8,128]{2,1,0:T(8,128)S(1)}, u32[]{:S(2)}, u32[]{:S(2)}) collective-permute-start(f32[10,8,128]{2,1,0:T(8,128)S(1)} %get-tuple-element.34), channel_id=1, source_target_pairs={{0,1},{1,0},{2,3},{3,2},{4,5},{5,4},{6,7},{7,6},{8,9},{9,8},{10,11... | collective-permute-start | bytes 122888 | tf_op jit(solution)/shard_map/ppermute | solution.py:995
  9.9 0.8 %shard_map.56.sides_main = f32[12,4,8,128]{3,2,1,0:T(8,128)S(1)} custom-call(f32[57,4,8,128]{3,2,1,0:T(8,128)S(1)} %get-tuple-element.27.adj, f32[12,4,8,128]{3,2,1,0:T(8,128)S(1)} %get-tuple-element.28.fl), custom_call_target="tpu_custom_call" | custom-call | flops 10000000 | bytes 10000000 | tf_op jit(solution)/shard_map/pallas_call | solution.py:978
  10.7 1.4 %collective-permute-done.2.recv_c = f32[10,8,128]{2,1,0:T(8,128)S(1)} collective-permute-done((f32[10,8,128]{2,1,0:T(8,128)S(1)}, f32[10,8,128]{2,1,0:T(8,128)S(1)}, u32[]{:S(2)}, u32[]{:S(2)}) %collective-permute-start.2) | collective-permute-done | bytes 40992 | tf_op jit(solution)/shard_map/ppermute | solution.py:995
  12.1 0.0 collective-permute-done.3.recv_d
  12.1 1.0 %shard_map.57 = (f32[88,128]{1,0:T(8,128)S(1)}, f32[88,128]{1,0:T(8,128)S(1)}, f32[57,8,128]{2,1,0:T(8,128)S(1)}, f32[12,8,128]{2,1,0:T(8,128)S(1)}, f32[12,8,128]{2,1,0:T(8,128)S(1)}) custom-call(f32[20,8,128]{2,1,0:T(8,128)S(1)} %get-tuple-element.31.own_left, f32[20,8,128]{2,1,0:T(8,128)S(1)} %get-tuple-element.32.own_right, ...), custom_call_target="tpu_custom_call" | custom-call | flops 100000000 | bytes 100000000 | tf_op jit(solution)/shard_map/pallas_call | solution.py:978
  13.1 2.0 %collective-permute-start.4 = (f32[88,128]{1,0:T(8,128)S(1)}, f32[88,128]{1,0:T(8,128)S(1)}, u32[]{:S(2)}, u32[]{:S(2)}) collective-permute-start(f32[88,128]{1,0:T(8,128)S(1)} %get-tuple-element.45), channel_id=1, source_target_pairs={{4,8},{8,4},{12,16},{16,12},{20,24},{24,20},{28,0},{0,28},{5,9},{9... | collective-permute-start | bytes 135176 | tf_op jit(solution)/shard_map/ppermute | solution.py:995
  15.1 0.2 collective-permute-start.5
  15.3 0.0 collective-permute-done.recv_a
  15.3 1.4 %collective-permute-done.1.recv_b = f32[352,128]{1,0:T(8,128)S(1)} collective-permute-done((f32[352,128]{1,0:T(8,128)S(1)}, f32[352,128]{1,0:T(8,128)S(1)}, u32[]{:S(2)}, u32[]{:S(2)}) %collective-permute-start.1) | collective-permute-done | bytes 180256 | tf_op jit(solution)/shard_map/ppermute | solution.py:995
  16.7 7.4 %shard_map.58 = (f32[93,4,8,128]{3,2,1,0:T(8,128)S(1)}, f32[57,4,8,128]{3,2,1,0:T(8,128)S(1)}, f32[9,4,8,128]{3,2,1,0:T(8,128)S(1)}, f32[14,4,8,128]{3,2,1,0:T(8...) custom-call(f32[57,4,8,128]{3,2,1,0:T(8,128)S(1)} %get-tuple-element.27.adj, ...), custom_call_target="tpu_custom_call" | custom-call | flops 100000000 | bytes 100000000 | tf_op jit(solution)/shard_map/pallas_call | solution.py:978
  24.1 0.0 collective-permute-done.4.recv_a
  24.1 0.0 collective-permute-done.5.recv_b
  24.1 4.2 %shard_map.59 = f32[57,4,8,128]{3,2,1,0:T(8,128)} custom-call(f32[12,4,8,128]{3,2,1,0:T(8,128)S(1)} %get-tuple-element.26.fe.fe_m, f32[93,4,8,128]{3,2,1,0:T(8,128)S(1)} %get-tuple-element.36.rims_m, f32[57,4,8,128]{3,2,1,0:T(8,128)S(1)} %get-tuple-element.37.mid_m, f32[9,4,8,128]{3,2,1,0:T(8,128)S(1)} %get-tuple-element.38.part_m, ...), custom_call_target="tpu_custom_call" | custom-call | tf_op jit(solution)/shard_map/pallas_call | solution.py:978
Async XLA Ops:
  2.2 13.1 %collective-permute-start = (f32[352,128]{1,0:T(8,128)S(1)}, f32[352,128]{1,0:T(8,128)S(1)}, u32[]{:S(2)}, u32[]{:S(2)}) collective-permute-start(f32[352,128]{1,0:T(8,128)S(1)} %get-tuple-element.29), channel_id=1, source_target_pairs={{4,8},{8,4},{12,16},{16,12},{20,24},{24,20},{28,0},{0,28},{5,9},{9... | collective-permute-start | bytes 540680 | tf_op jit(solution)/shard_map/ppermute | solution.py:995
  8.3 8.4 %collective-permute-start.1 = (f32[352,128]{1,0:T(8,128)S(1)}, f32[352,128]{1,0:T(8,128)S(1)}, u32[]{:S(2)}, u32[]{:S(2)}) collective-permute-start(f32[352,128]{1,0:T(8,128)S(1)} %get-tuple-element.30), channel_id=1, source_target_pairs={{0,4},{4,0},{8,12},{12,8},{16,20},{20,16},{24,28},{28,24},{1,5},{5... | collective-permute-start | bytes 540680 | tf_op jit(solution)/shard_map/ppermute | solution.py:995
  8.3 3.8 %collective-permute-start.2 = (f32[10,8,128]{2,1,0:T(8,128)S(1)}, f32[10,8,128]{2,1,0:T(8,128)S(1)}, u32[]{:S(2)}, u32[]{:S(2)}) collective-permute-start(f32[10,8,128]{2,1,0:T(8,128)S(1)} %get-tuple-element.33), channel_id=1, source_target_pairs={{1,2},{2,1},{3,0},{0,3},{5,6},{6,5},{7,4},{4,7},{9,10},{10,9},{11,... | collective-permute-start | bytes 122888 | tf_op jit(solution)/shard_map/ppermute | solution.py:995
  8.9 3.2 %collective-permute-start.3 = (f32[10,8,128]{2,1,0:T(8,128)S(1)}, f32[10,8,128]{2,1,0:T(8,128)S(1)}, u32[]{:S(2)}, u32[]{:S(2)}) collective-permute-start(f32[10,8,128]{2,1,0:T(8,128)S(1)} %get-tuple-element.34), channel_id=1, source_target_pairs={{0,1},{1,0},{2,3},{3,2},{4,5},{5,4},{6,7},{7,6},{8,9},{9,8},{10,11... | collective-permute-start | bytes 122888 | tf_op jit(solution)/shard_map/ppermute | solution.py:995
  13.1 11.0 %collective-permute-start.4 = (f32[88,128]{1,0:T(8,128)S(1)}, f32[88,128]{1,0:T(8,128)S(1)}, u32[]{:S(2)}, u32[]{:S(2)}) collective-permute-start(f32[88,128]{1,0:T(8,128)S(1)} %get-tuple-element.45), channel_id=1, source_target_pairs={{4,8},{8,4},{12,16},{16,12},{20,24},{24,20},{28,0},{0,28},{5,9},{9... | collective-permute-start | bytes 135176 | tf_op jit(solution)/shard_map/ppermute | solution.py:995
  15.1 9.0 %collective-permute-start.5 = (f32[88,128]{1,0:T(8,128)S(1)}, f32[88,128]{1,0:T(8,128)S(1)}, u32[]{:S(2)}, u32[]{:S(2)}) collective-permute-start(f32[88,128]{1,0:T(8,128)S(1)} %get-tuple-element.46), channel_id=1, source_target_pairs={{0,4},{4,0},{8,12},{12,8},{16,20},{20,16},{24,28},{28,24},{1,5},{5... | collective-permute-start | bytes 135176 | tf_op jit(solution)/shard_map/ppermute | solution.py:995

commit v10 on v9

--- a/solution.py
+++ b/solution.py
@@ -67,10 +67,6 @@
     def in_width(self):
         return self.once("width", lambda: lax.rem(self.lane, self.width))
 
-    def plane_lanes(self, p):
-        low, high = p * self.width, (p + 1) * self.width
-        return self.once(("plane", p), lambda: (self.lane >= low) & (self.lane < high))
-
     def left_half(self):
         return self.once("left", lambda: self.in_width() < self.width // 2)
 
@@ -107,20 +103,6 @@
 
     def low(self):
         return self.once("low", lambda: self.sub < self.rows // 2)
-
-    def corners(self, j):
-        return self.once(("corner", j), lambda: self.make_corners(j))
-
-    def make_corners(self, j):
-        at, inside = self.in_width(), None
-        for low in (HALO, 3 * self.group):
-            low = (low + j * self.group) % self.width
-            window = (at >= low) & (at < low + HALO)
-            inside = window if inside is None else inside | window
-        return inside
-
-    def turn(self, v, lanes):
-        return pltpu.roll(v, lanes % self.cols, 1) if lanes % self.cols else v
 
     def outward(self):
         return self.once("out", lambda: jnp.where(self.low(), -1.0, 1.0).astype(F32))
@@ -188,13 +170,37 @@
         for d in range(3):
             if c[d] == 0:
                 continue
-            if diff is not None:
+            if diff is not None and diff[c] is not None:
                 first[d] = plus(first[d], (w * c[d]) * diff[c])
-            if total is not None:
+            if total is not None and total[c] is not None:
                 for e in range(d, 3):
                     if c[e] != 0:
                         second[d, e] = plus(second.get((d, e)), (w * c[d] * c[e]) * total[c])
     return first, second
+
+
+PAIRS = tuple((d, e) for d in range(3) for e in range(d, 3))
+
+
+def moments_of(streamed):
+    diff, total = {}, {}
+    for c, w in axis_pairs():
+        a, b = streamed[INDEX[c]], streamed[INDEX[tuple(-i for i in c)]]
+        if a is None or b is None:
+            diff[c] = a if b is None else -b
+            total[c] = b if a is None else a
+        else:
+            diff[c], total[c] = a - b, a + b
+    first, second = first_and_second(diff, total)
+    zeroth = None if streamed[16] is None else W0 * streamed[16]
+    for c, w in axis_pairs():
+        if total[c] is not None:
+            zeroth = plus(zeroth, w * total[c])
+    return [zeroth] + first + [second.get(k) for k in PAIRS]
+
+
+def summed(known, change):
+    return [k if x is None else k + x for k, x in zip(known, change)]
 
 
 def turned(second, v):
@@ -304,20 +310,13 @@
     return field_forces(grid, loads, lambda get, cx, dz: get(cx, dz), dipole)
 
 
-def collision_adjoint(streamed_of, rho, u, psi, forces):
+def collision_adjoint(moments, rho, u, psi, forces):
     inverse_sum = 1.0 / (rho[0] + rho[1] + rho[2])
     grad_u = [None] * 3
     alphas, held = [], []
     for s in range(3):
-        streamed = streamed_of(s)
-        diff, total = {}, {}
-        for c, w in axis_pairs():
-            a, b = streamed[INDEX[c]], streamed[INDEX[tuple(-i for i in c)]]
-            diff[c], total[c] = a - b, a + b
-        m1, m2 = first_and_second(diff, total)
-        m0 = W0 * streamed[16]
-        for c, w in axis_pairs():
-            m0 = m0 + w * total[c]
+        m0, m1 = moments[s][0], moments[s][1:4]
+        m2 = dict(zip(PAIRS, moments[s][4:]))
         inverse = 1.0 / rho[s]
         ratio = psi[s] * inverse
         tau = RELAXATION[s]
@@ -336,7 +335,7 @@
     return held, [a - along for a in alphas], beta
 
 
-def brick_collision(grid, tile, load, rim, fields, forces, hold, ab, kept):
+def brick_moments(grid, tile, load, rim, kept):
     def streamed_of(s):
         streamed = []
         for q in range(19):
@@ -355,8 +354,31 @@
                 tile.put(kept, q, v)
         return streamed
 
+    return [moments_of(streamed_of(s)) for s in range(3)]
+
+
+def crossing_moments(grid, tile, rim, kept):
+    first, last = grid.sub == 0, grid.sub == grid.rows - 1
+
+    def streamed_of(s):
+        streamed = [None] * 19
+        for j, (cy, cz) in enumerate(CROSS):
+            v = tile.get(rim, s * 5 + j, cz)
+            if cy != 0:
+                v = grid.roll_cols(v, cy)
+            streamed[AHEAD[j]] = jnp.where(last, v, 0.0)
+            streamed[BEHIND[j]] = jnp.where(first, v, 0.0)
+        if s == 2:
+            for q in AHEAD + BEHIND:
+                tile.put(kept, q, tile.get(kept, q) + streamed[q])
+        return streamed
+
+    return [moments_of(streamed_of(s)) for s in range(3)]
+
+
+def brick_adjoint(tile, moments, fields, forces, hold, ab):
     rho, u, psi = [[tile.get(fields, at + d) for d in range(3)] for at in (0, 3, 9)]
-    held, alpha, beta = collision_adjoint(streamed_of, rho, u, psi, forces)
+    held, alpha, beta = collision_adjoint(moments, rho, u, psi, forces)
     for k in range(9):
         tile.put(hold, k, held[k])
     for s in range(3):
@@ -364,35 +386,57 @@
         tile.put(ab, 3 + s, beta[s])
 
 
-def rim_collision(grid, tile, level, after, inner, rho, u, psi, forces, hold, ab, kept):
-    outward, low = grid.outward(), grid.low()
+def brick_collision(grid, tile, load, rim, fields, forces, hold, ab, kept):
+    moments = brick_moments(grid, tile, load, rim, kept)
+    brick_adjoint(tile, moments, fields, forces, hold, ab)
+
+
+def rim_moments(grid, tile, level, after, inner, kept):
+    low = grid.low()
 
     def streamed_of(s):
         streamed = []
         for q in range(19):
             c = VELOCITY[q]
-            if c[0] == 0:
+            v = None
+            if c[0] == 0 and level is not None:
                 v = level(s, LEVEL.index(q), c[2])
-            elif c[0] > 0:
+            elif c[0] > 0 and after is not None:
                 v = after(s, AHEAD.index(q), c[2])
-            else:
+            elif c[0] < 0 and inner is not None:
                 j = BEHIND.index(q)
                 v = jnp.where(low, inner(s * 19 + AHEAD[j], c[2]), inner(s * 19 + BEHIND[j], c[2]))
-            if c[1] != 0:
+            if c[1] != 0 and v is not None:
                 v = grid.roll_cols(v, c[1])
             streamed.append(v)
             if s == 2 and kept is not None and c[0] >= 0:
                 tile.put(kept, LEVEL.index(q) if c[0] == 0 else 9 + AHEAD.index(q), v)
         return streamed
 
+    return [moments_of(streamed_of(s)) for s in range(3)]
+
+
+def rim_adjoint(grid, tile, moments, rho, u, psi, forces, hold, ab):
+    outward = grid.outward()
     u = [u[0] * outward, u[1], u[2]]
-    held, alpha, beta = collision_adjoint(streamed_of, rho, u, psi, forces)
+    held, alpha, beta = collision_adjoint(moments, rho, u, psi, forces)
     for k in range(9):
         tile.put(hold, k, held[k] * outward if k % 3 == 0 else held[k])
     if ab is not None:
         for s in range(3):
             tile.put(ab, s, alpha[s])
             tile.put(ab, 3 + s, beta[s] * outward if s == 0 else beta[s])
+
+
+def put_moments(tile, ref, moments):
+    for s in range(3):
+        for k in range(10):
+            v = moments[s][k]
+            tile.put(ref, s * 10 + k, jnp.zeros(ref.shape[-2:], F32) if v is None else v)
+
+
+def get_moments(tile, ref):
+    return [[tile.get(ref, s * 10 + k) for k in range(10)] for s in range(3)]
 
 
 def spread_plane(grid, get_h, get_d, sign, pairs):
@@ -525,23 +569,17 @@
             yield kind, c, c, 1
 
 
-def corner_groups(pack):
-    for depth in range(2):
-        found = [c for c, row in enumerate(static_rows()) if row[3] == depth]
-        for at in range(0, len(found), pack):
-            yield depth, found[at : at + pack]
-
-
-def pack_static(kinds, planes, rows, lines, parity):
+def pack_static(get, tiles, rows, lines, parity):
     up, down = parity, 1 - parity
     fill = 0
     for kind, above, below, depth in static_rows():
-        for p in range(planes):
-            v = kinds[kind][above, p]
+        for t in tiles:
+            v = get(kind, above, t)
             lines[up, fill : fill + 1, :] = v[rows - 1 - depth : rows - depth, :]
-            v = kinds[kind][below, p]
+            v = get(kind, below, t)
             lines[down, fill : fill + 1, :] = v[depth : depth + 1, :]
             fill += 1
+    return fill
 
 
 def pack_columns_kernel(
@@ -627,7 +665,8 @@
         right = jnp.where(low, pltpu.roll(own_right[2 * h + 1], cols - HALO, 1), own_right[2 * h])
         send_c[h] = jnp.where(even, right, left)
         send_d[h] = jnp.where(even, left, right)
-    pack_static((adj, fl, fe), planes, rows, lines, parity_of("gx"))
+    kinds = (adj, fl, fe)
+    pack_static(lambda kind, c, t: kinds[kind][c, t], range(planes), rows, lines, parity_of("gx"))
     lines_to(send_a, send_b, lines)
 
 
@@ -711,23 +750,9 @@
         second_row(grid, tile, fields, hold, ab, kept, both)
 
     grid.over_edge(inside)
+    kinds = (edge, fl, fe)
     parity = parity_of("gx")
-    kinds = (edge, fl, fe)
-    rows_of = list(static_rows())
-    low = grid.low()
-    fill = 0
-    for depth, members in corner_groups(grid.pack):
-        v = None
-        for j, c in enumerate(members):
-            kind, above, below, unused = rows_of[c]
-            one = kinds[kind][above]
-            if above != below:
-                one = jnp.where(low, kinds[kind][below], one)
-            one = grid.turn(one, j * grid.group)
-            v = one if j == 0 else jnp.where(grid.corners(j), one, v)
-        lines[parity, fill : fill + 1, :] = v[rows - 1 - depth : rows - depth, :]
-        lines[1 - parity, fill : fill + 1, :] = v[depth : depth + 1, :]
-        fill += 1
+    fill = pack_static(lambda kind, c, t: kinds[kind][c], (0,), rows, lines, parity)
     for c in range(DYNAMIC):
         depth = 0 if c < 3 else 1
         for t in range(grid.tiles):
@@ -745,20 +770,15 @@
     forces = rim_forces(grid, tile, fl, rims, LATE_PSI, LATE)
     rho, u = [[tile.get(rims, LATE + at + d) for d in range(3)] for at in (0, 3)]
     psi = [tile.get(rims, LATE_PSI + s) for s in range(3)]
-    rim_collision(
+    moments = rim_moments(
         grid,
         tile,
         lambda s, i, dz: tile.get(rims, ALONG + s * 9 + i, dz),
         lambda s, j, dz: tile.get(rims, AFTER + s * 5 + j, dz),
         load,
-        rho,
-        u,
-        psi,
-        forces,
-        hold_rim,
-        ab_rim,
         kept_rim,
     )
+    rim_adjoint(grid, tile, moments, rho, u, psi, forces, hold_rim, ab_rim)
 
 
 def early_forces(grid, tile, fe, rims, forces, forces_rim):
@@ -808,9 +828,22 @@
         tile.put(part, 6 + s, (1.0 - tile.get(rims, LATE + FAR + s)) * after[s])
 
 
+def level_row(tile, alpha, part, kept_rim, level):
+    rest = 1.0 - 1.0 / RELAXATION[2]
+    beta = [tile.get(part, 3 + d) for d in range(3)]
+    for i, q in enumerate(LEVEL):
+        side = mixed(VELOCITY[q][1:], beta[1:]) if q != 16 else None
+        for s in range(3):
+            v = plus(side, alpha[s])
+            if s == 2:
+                v = v + rest * tile.get(kept_rim, i)
+            tile.put(level, s * 9 + i, v)
+
+
 def main_kernel(
     adj, fl, fe, recv_a, recv_b, after,
-    rims, mid, part, kept_rim, forces, forces_rim, known, lines, hold, ab, kept, hold_rim, ab_rim,
+    rims, mid, part, kept_rim, forces, forces_rim, brick2, rim2, kept2,
+    lines, hold, ab, kept, hold_rim, ab_rim, level,
 ):
     planes, rows, cols = adj.shape[1:]
     grid = Grid(planes, rows, cols)
@@ -820,12 +853,6 @@
             k = c * planes + p
             rims[c, p] = grid.sides(lines[0, k : k + 1, :], lines[1, k : k + 1, :])
     grid.over_main(lambda tile: rim_psis(grid, tile, rims))
-    for c in range(STATIC):
-        v = None
-        for p in range(planes):
-            one = grid.turn(rims[c, p], p * grid.width + 2 * grid.group)
-            v = one if p == 0 else jnp.where(grid.plane_lanes(p), one, v)
-        known[c] = jnp.where(grid.left_half(), grid.turn(v, -grid.group), grid.turn(v, grid.group))
 
     def step(tile):
         first_step(grid, tile, adj, fl, rims, hold, ab, kept, hold_rim, ab_rim, kept_rim)
@@ -837,28 +864,33 @@
             grid, tile, fl, rims, hold, ab, kept, hold_rim, ab_rim, mid, part
         )
     )
+    grid.over_main(lambda tile: level_row(tile, [tile.get(part, s) for s in range(3)], part, kept_rim, level))
+
+    def known_moments(tile):
+        load = lambda c, dz: tile.get(mid, c, dz)
+        put_moments(tile, brick2, brick_moments(grid, tile, load, None, kept2))
+        along = lambda s, i, dz: tile.get(level, s * 9 + i, dz)
+        put_moments(tile, rim2, rim_moments(grid, tile, along, None, load, None))
+
+    grid.over_main(known_moments)
 
 
 def last_kernel(
-    fe_m, rims_m, mid_m, part_m, kept_rim_m, forces_m, forces_rim_m, known, edge, fl_e, fe_e,
+    fe_m, rims_m, mid_m, part_m, kept_rim_m, forces_m, forces_rim_m, brick2_m, rim2_m, kept2_m,
+    edge, fl_e, fe_e,
     recv_a, recv_b, out,
     rims_e, mid_e, part_e, kept_rim_e, forces_e, forces_rim_e, hold_e, ab_e, kept_e, hold_rim_e,
-    ab_rim_e, patches, lines, near, rim_mid, rim_level, rim_far, hold2, hold_rim2, ab2, kept2,
+    ab_rim_e, patches, lines, near, change, rim_mid, rim_level, rim_far, hold2, hold_rim2, ab2, kept2,
     total, staged, sems,
 ):
     planes, rows, cols = fe_m.shape[1:]
     grid = Grid(planes, rows, cols)
     lines_from(recv_a, recv_b, parity_of("gx"), lines)
-    is_corner = grid.corners(0)
-    corner_lines = 0
-    for k, (unused, members) in enumerate(corner_groups(grid.pack)):
-        v = grid.sides(lines[0, k : k + 1, :], lines[1, k : k + 1, :])
-        for j, c in enumerate(members):
-            rims_e[c] = jnp.where(is_corner, grid.turn(v, -j * grid.group), known[c])
-        corner_lines += 1
+    for c in range(STATIC):
+        rims_e[c] = grid.sides(lines[0, c : c + 1, :], lines[1, c : c + 1, :])
     for c in range(DYNAMIC):
         for t in range(grid.tiles):
-            k = corner_lines + c * grid.tiles + t
+            k = STATIC + c * grid.tiles + t
             near[c, t] = grid.sides(lines[0, k : k + 1, :], lines[1, k : k + 1, :])
     fe, rims, mid = Pair(fe_m, fe_e), Pair(rims_m, rims_e), Pair(mid_m, mid_e)
     part, kept_rim = Pair(part_m, part_e), Pair(kept_rim_m, kept_rim_e)
@@ -881,14 +913,14 @@
 
     def complete(tile):
         t = tile.index
-        alpha = [
-            tile.get(part, s) + (1.0 - tile.get(rims, LATE_PSI + s)) * near[s, t]
-            for s in range(3)
-        ]
+        added = [(1.0 - tile.get(rims, LATE_PSI + s)) * near[s, t] for s in range(3)]
+        alpha = [tile.get(part, s) + added[s] for s in range(3)]
         beta = [tile.get(part, 3 + d) for d in range(3)]
         far = [near[3 + s, t] + tile.get(part, 6 + s) for s in range(2)]
         far_beta = [near[5 + d, t] for d in range(2)]
         ahead = outward * beta[0]
+        for s in range(3):
+            change[s, t] = added[s]
         for j, yz in enumerate(CROSS):
             side = mixed(yz, beta[1:]) if j else None
             side_far = mixed(yz, far_beta) if j else None
@@ -900,37 +932,34 @@
                 else:
                     rim_far[s * 5 + j, t] = plus(side_far, far[s])
                 rim_mid[s * 5 + j, t] = v
-        for i, q in enumerate(LEVEL):
-            side = mixed(VELOCITY[q][1:], beta[1:]) if q != 16 else None
-            for s in range(3):
-                v = plus(side, alpha[s])
-                if s == 2:
-                    v = v + rest * tile.get(kept_rim, i)
-                rim_level[s * 9 + i, t] = v
+        if tile.edge:
+            level_row(tile, alpha, part, kept_rim, rim_level)
 
     grid.over(complete)
 
     def collide(tile):
         load = lambda c, dz: tile.get(mid, c, dz)
+        after = lambda s, j, dz: tile.get(rim_far, s * 5 + j, dz)
+        if tile.edge:
+            moments = brick_moments(grid, tile, load, rim_mid, kept2)
+            along = lambda s, i, dz: tile.get(rim_level, s * 9 + i, dz)
+            moments_rim = rim_moments(grid, tile, along, after, load, None)
+        else:
+            for q in range(19):
+                kept2[q, tile.index] = kept2_m[q, tile.index]
+            moments, moments_rim = get_moments(tile, brick2_m), get_moments(tile, rim2_m)
+            along = lambda s, i, dz: tile.get(change, s, dz)
+            more = crossing_moments(grid, tile, rim_mid, kept2)
+            more_rim = rim_moments(grid, tile, along, after, None, None)
+            for s in range(3):
+                moments[s] = summed(moments[s], more[s])
+                moments_rim[s] = summed(moments_rim[s], more_rim[s])
         known = [[tile.get(forces, 3 * s + d) for d in range(3)] for s in range(3)]
-        brick_collision(grid, tile, load, rim_mid, fe, known, hold2, ab2, kept2)
+        brick_adjoint(tile, moments, fe, known, hold2, ab2)
         known = [[tile.get(forces_rim, 3 * s + d) for d in range(3)] for s in range(3)]
         rho, u = [[tile.get(rims, EARLY + at + d) for d in range(3)] for at in (0, 3)]
         psi = [tile.get(rims, EARLY_PSI + s) for s in range(3)]
-        rim_collision(
-            grid,
-            tile,
-            lambda s, i, dz: tile.get(rim_level, s * 9 + i, dz),
-            lambda s, j, dz: tile.get(rim_far, s * 5 + j, dz),
-            load,
-            rho,
-            u,
-            psi,
-            known,
-            hold_rim2,
-            None,
-            None,
-        )
+        rim_adjoint(grid, tile, moments_rim, rho, u, psi, known, hold_rim2, None)
 
     grid.over(collide)
 
@@ -1015,7 +1044,7 @@
         return [(n, planes + 1) + tile for n in counts]
 
     static = lines(STATIC * planes)
-    second = lines(len(list(corner_groups(pack))) + DYNAMIC * (planes + 1))
+    second = lines(STATIC + DYNAMIC * (planes + 1))
     send_c, send_d, own_left, own_right, fl_m, fe_m, adj, send_a, send_b = call(
         pack_columns_kernel,
         edges(groups // 2, groups // 2, groups, groups) + main(12, 12, pops) + [static] * 2,
@@ -1043,8 +1072,8 @@
     known = (RIMS, pops, 9, 14, 9, 9)
     mains = call(
         main_kernel,
-        main(*known) + edges(STATIC),
-        [(2,) + static] + main(9, 6, 19, 9, 6),
+        main(*known, 30, 30, 19),
+        [(2,) + static] + main(9, 6, 19, 9, 6, 27),
         [adj, fl_m, fe_m, static_a, static_b, fl_e],
         cost=MAIN_COST,
     )
@@ -1053,7 +1082,7 @@
         [(pops, planes) + tile],
         edges(*known, 9, 6, 19, 9, 6, 25)
         + [(2,) + second]
-        + tiled(DYNAMIC, 15, 27, 15, 9, 9, 6, 19, 3)
+        + tiled(DYNAMIC, 3, 15, 27, 15, 9, 9, 6, 19, 3)
         + main(pops)
         + [pltpu.SemaphoreType.DMA((planes,))],
         [fe_m, *mains, edge, fl_e, fe_e, recv_a, recv_b],

time: 28.5 us -> 24.8 us (0.87)
  Pallas kernels: 15.6 us -> 9.93 us
  waiting for transfers between devices: 2.81 us -> 4.87 us
    pallas_call x5, Pallas kernels: 15.6 us -> 9.93 us  [call(): pl.pallas_call(kernel, out_shape=[jax.ShapeDtypeStruct(s, F32) for s in o...]
    ppermute x6, waiting for transfers between devices: 2.81 us -> 4.87 us  [swap(): return lax.ppermute(block, axis, route)]
  transfers between devices with their start and end apart: 6 -> 6, of which waited for: 2 -> 4; matrix products, arithmetic and copies ran while one was open for 0% -> 0% of each run, Pallas kernels for 33% -> 16%
where the time goes in v10:
time: 24.8 us; the launch traced here: 24.7 us
  Pallas kernels  9.93 us (40%)
  starting transfers between devices  9.84 us (40%)
  waiting for transfers between devices  4.87 us (20%)
    pallas_call x5, Pallas kernels, call(): pl.pallas_call(kernel, out_shape=[jax.ShapeDtypeStruct(s, F32) for s in o...  9.93 us
    ppermute x6, starting transfers between devices, swap(): return lax.ppermute(block, axis, route)  9.84 us
    ppermute x6, waiting for transfers between devices, swap(): return lax.ppermute(block, axis, route)  4.87 us
  transfers between devices with their start and end apart: 6, of which 4 were waited for; matrix products, arithmetic and copies ran while one was open for 0% of the time, Pallas kernels for 16%

profile of v10, /device:TPU:0, one launch (start us, length us, event | category | flops | bytes accessed | tf_op | source)
XLA Modules:
  0.0 24.7 jit_solution(11233174774887250034)
XLA Ops:
  0.0 2.2 %shard_map.55 = (f32[10,8,128]{2,1,0:T(8,128)S(1)}, f32[10,8,128]{2,1,0:T(8,128)S(1)}, f32[20,8,128]{2,1,0:T(8,128)S(1)}, f32[20,8,128]{2,1,0:T(8,128)S(1)}, f32...) custom-call(f32[57,4,8,128]{3,2,1,0:T(8,128)} %adj_in.1, ...), custom_call_target="tpu_custom_call" | custom-call | tf_op jit(solution)/shard_map/pallas_call | solution.py:1007
  2.2 6.1 %collective-permute-start = (f32[352,128]{1,0:T(8,128)S(1)}, f32[352,128]{1,0:T(8,128)S(1)}, u32[]{:S(2)}, u32[]{:S(2)}) collective-permute-start(f32[352,128]{1,0:T(8,128)S(1)} %get-tuple-element.31), channel_id=1, source_target_pairs={{4,8},{8,4},{12,16},{16,12},{20,24},{24,20},{28,0},{0,28},{5,9},{9... | collective-permute-start | bytes 540680 | tf_op jit(solution)/shard_map/ppermute | solution.py:1024
  8.3 0.0 collective-permute-start.1
  8.3 0.7 %collective-permute-start.2 = (f32[10,8,128]{2,1,0:T(8,128)S(1)}, f32[10,8,128]{2,1,0:T(8,128)S(1)}, u32[]{:S(2)}, u32[]{:S(2)}) collective-permute-start(f32[10,8,128]{2,1,0:T(8,128)S(1)} %get-tuple-element.35), channel_id=1, source_target_pairs={{1,2},{2,1},{3,0},{0,3},{5,6},{6,5},{7,4},{4,7},{9,10},{10,9},{11,... | collective-permute-start | bytes 122888 | tf_op jit(solution)/shard_map/ppermute | solution.py:1024
  8.9 1.0 %collective-permute-start.3 = (f32[10,8,128]{2,1,0:T(8,128)S(1)}, f32[10,8,128]{2,1,0:T(8,128)S(1)}, u32[]{:S(2)}, u32[]{:S(2)}) collective-permute-start(f32[10,8,128]{2,1,0:T(8,128)S(1)} %get-tuple-element.36), channel_id=1, source_target_pairs={{0,1},{1,0},{2,3},{3,2},{4,5},{5,4},{6,7},{7,6},{8,9},{9,8},{10,11... | collective-permute-start | bytes 122888 | tf_op jit(solution)/shard_map/ppermute | solution.py:1024
  9.9 0.8 %shard_map.56.sides_main = f32[12,4,8,128]{3,2,1,0:T(8,128)S(1)} custom-call(f32[57,4,8,128]{3,2,1,0:T(8,128)S(1)} %get-tuple-element.29.adj, f32[12,4,8,128]{3,2,1,0:T(8,128)S(1)} %get-tuple-element.30.fl), custom_call_target="tpu_custom_call" | custom-call | flops 10000000 | bytes 10000000 | tf_op jit(solution)/shard_map/pallas_call | solution.py:1007
  10.7 1.4 %collective-permute-done.2.recv_c = f32[10,8,128]{2,1,0:T(8,128)S(1)} collective-permute-done((f32[10,8,128]{2,1,0:T(8,128)S(1)}, f32[10,8,128]{2,1,0:T(8,128)S(1)}, u32[]{:S(2)}, u32[]{:S(2)}) %collective-permute-start.2) | collective-permute-done | bytes 40992 | tf_op jit(solution)/shard_map/ppermute | solution.py:1024
  12.1 0.0 collective-permute-done.3.recv_d
  12.1 0.8 %shard_map.57 = (f32[152,128]{1,0:T(8,128)S(1)}, f32[152,128]{1,0:T(8,128)S(1)}, f32[57,8,128]{2,1,0:T(8,128)S(1)}, f32[12,8,128]{2,1,0:T(8,128)S(1)}, f32[12,8,128]{2,1,0:T(8,128)S(1)}) custom-call(f32[20,8,128]{2,1,0:T(8,128)S(1)} %get-tuple-element.33.own_left, f32[20,8,128]{2,1,0:T(8,128)S(1)} %get-tuple-element.34.own_right, ...), custom_call_target="tpu_custom_call" | custom-call | flops 100000000 | bytes 100000000 | tf_op jit(solution)/shard_map/pallas_call | solution.py:1007
  12.9 2.0 %collective-permute-start.4 = (f32[152,128]{1,0:T(8,128)S(1)}, f32[152,128]{1,0:T(8,128)S(1)}, u32[]{:S(2)}, u32[]{:S(2)}) collective-permute-start(f32[152,128]{1,0:T(8,128)S(1)} %get-tuple-element.49), channel_id=1, source_target_pairs={{4,8},{8,4},{12,16},{16,12},{20,24},{24,20},{28,0},{0,28},{5,9},{9... | collective-permute-start | bytes 233480 | tf_op jit(solution)/shard_map/ppermute | solution.py:1024
  14.9 0.2 collective-permute-start.5
  15.1 0.0 collective-permute-done.recv_a
  15.1 1.6 %collective-permute-done.1.recv_b = f32[352,128]{1,0:T(8,128)S(1)} collective-permute-done((f32[352,128]{1,0:T(8,128)S(1)}, f32[352,128]{1,0:T(8,128)S(1)}, u32[]{:S(2)}, u32[]{:S(2)}) %collective-permute-start.1) | collective-permute-done | bytes 180256 | tf_op jit(solution)/shard_map/ppermute | solution.py:1024
  16.7 2.4 %shard_map.58 = (f32[93,4,8,128]{3,2,1,0:T(8,128)S(1)}, f32[57,4,8,128]{3,2,1,0:T(8,128)S(1)}, f32[9,4,8,128]{3,2,1,0:T(8,128)S(1)}, f32[14,4,8,128]{3,2,1,0:T(8...) custom-call(f32[57,4,8,128]{3,2,1,0:T(8,128)S(1)} %get-tuple-element, ...), custom_call_target="tpu_custom_call" | custom-call | flops 100000000 | bytes 100000000 | tf_op jit(solution)/shard_map/pallas_call | solution.py:1007
  19.1 1.1 %collective-permute-done.4.recv_a = f32[152,128]{1,0:T(8,128)S(1)} collective-permute-done((f32[152,128]{1,0:T(8,128)S(1)}, f32[152,128]{1,0:T(8,128)S(1)}, u32[]{:S(2)}, u32[]{:S(2)}) %collective-permute-start.4) | collective-permute-done | bytes 77856 | tf_op jit(solution)/shard_map/ppermute | solution.py:1024
  20.2 0.7 %collective-permute-done.5.recv_b = f32[152,128]{1,0:T(8,128)S(1)} collective-permute-done((f32[152,128]{1,0:T(8,128)S(1)}, f32[152,128]{1,0:T(8,128)S(1)}, u32[]{:S(2)}, u32[]{:S(2)}) %collective-permute-start.5) | collective-permute-done | bytes 77856 | tf_op jit(solution)/shard_map/ppermute | solution.py:1024
  20.9 3.8 %shard_map.59 = f32[57,4,8,128]{3,2,1,0:T(8,128)} custom-call(f32[12,4,8,128]{3,2,1,0:T(8,128)S(1)} %get-tuple-element.28.fe.fe_m, f32[93,4,8,128]{3,2,1,0:T(8,128)S(1)} %get-tuple-element.38.rims_m, f32[57,4,8,128]{3,2,1,0:T(8,128)S(1)} %get-tuple-element.39.mid_m, f32[9,4,8,128]{3,2,1,0:T(8,128)S(1)} %get-tuple-element.40.part_m, ...), custom_call_target="tpu_custom_call" | custom-call | tf_op jit(solution)/shard_map/pallas_call | solution.py:1007
Async XLA Ops:
  2.2 12.9 %collective-permute-start = (f32[352,128]{1,0:T(8,128)S(1)}, f32[352,128]{1,0:T(8,128)S(1)}, u32[]{:S(2)}, u32[]{:S(2)}) collective-permute-start(f32[352,128]{1,0:T(8,128)S(1)} %get-tuple-element.31), channel_id=1, source_target_pairs={{4,8},{8,4},{12,16},{16,12},{20,24},{24,20},{28,0},{0,28},{5,9},{9... | collective-permute-start | bytes 540680 | tf_op jit(solution)/shard_map/ppermute | solution.py:1024
  8.3 8.4 %collective-permute-start.1 = (f32[352,128]{1,0:T(8,128)S(1)}, f32[352,128]{1,0:T(8,128)S(1)}, u32[]{:S(2)}, u32[]{:S(2)}) collective-permute-start(f32[352,128]{1,0:T(8,128)S(1)} %get-tuple-element.32), channel_id=1, source_target_pairs={{0,4},{4,0},{8,12},{12,8},{16,20},{20,16},{24,28},{28,24},{1,5},{5... | collective-permute-start | bytes 540680 | tf_op jit(solution)/shard_map/ppermute | solution.py:1024
  8.3 3.8 %collective-permute-start.2 = (f32[10,8,128]{2,1,0:T(8,128)S(1)}, f32[10,8,128]{2,1,0:T(8,128)S(1)}, u32[]{:S(2)}, u32[]{:S(2)}) collective-permute-start(f32[10,8,128]{2,1,0:T(8,128)S(1)} %get-tuple-element.35), channel_id=1, source_target_pairs={{1,2},{2,1},{3,0},{0,3},{5,6},{6,5},{7,4},{4,7},{9,10},{10,9},{11,... | collective-permute-start | bytes 122888 | tf_op jit(solution)/shard_map/ppermute | solution.py:1024
  8.9 3.2 %collective-permute-start.3 = (f32[10,8,128]{2,1,0:T(8,128)S(1)}, f32[10,8,128]{2,1,0:T(8,128)S(1)}, u32[]{:S(2)}, u32[]{:S(2)}) collective-permute-start(f32[10,8,128]{2,1,0:T(8,128)S(1)} %get-tuple-element.36), channel_id=1, source_target_pairs={{0,1},{1,0},{2,3},{3,2},{4,5},{5,4},{6,7},{7,6},{8,9},{9,8},{10,11... | collective-permute-start | bytes 122888 | tf_op jit(solution)/shard_map/ppermute | solution.py:1024
  12.9 7.3 %collective-permute-start.4 = (f32[152,128]{1,0:T(8,128)S(1)}, f32[152,128]{1,0:T(8,128)S(1)}, u32[]{:S(2)}, u32[]{:S(2)}) collective-permute-start(f32[152,128]{1,0:T(8,128)S(1)} %get-tuple-element.49), channel_id=1, source_target_pairs={{4,8},{8,4},{12,16},{16,12},{20,24},{24,20},{28,0},{0,28},{5,9},{9... | collective-permute-start | bytes 233480 | tf_op jit(solution)/shard_map/ppermute | solution.py:1024
  14.9 6.0 %collective-permute-start.5 = (f32[152,128]{1,0:T(8,128)S(1)}, f32[152,128]{1,0:T(8,128)S(1)}, u32[]{:S(2)}, u32[]{:S(2)}) collective-permute-start(f32[152,128]{1,0:T(8,128)S(1)} %get-tuple-element.50), channel_id=1, source_target_pairs={{0,4},{4,0},{8,12},{12,8},{16,20},{20,16},{24,28},{28,24},{1,5},{5... | collective-permute-start | bytes 233480 | tf_op jit(solution)/shard_map/ppermute | solution.py:1024

commit v11 on v10

--- a/solution.py
+++ b/solution.py
@@ -569,10 +569,13 @@
             yield kind, c, c, 1
 
 
-def pack_static(get, tiles, rows, lines, parity):
+def pack_static(get, tiles, rows, lines, parity, wanted=None):
     up, down = parity, 1 - parity
     fill = 0
     for kind, above, below, depth in static_rows():
+        if wanted is not None and not wanted(kind, max(above, below)):
+            fill += len(tiles)
+            continue
         for t in tiles:
             v = get(kind, above, t)
             lines[up, fill : fill + 1, :] = v[rows - 1 - depth : rows - depth, :]
@@ -630,12 +633,22 @@
                         momentum = plus(momentum, flows[q] if VELOCITY[q][d] > 0 else -flows[q])
                 out[3 + d, p] = momentum * inverse
                 out[6 + d, p] = dip[d, p].astype(F32)
+    kinds = (adj, fl, fe)
+    parity = parity_of("gx")
+
+    def pack_rows(wanted):
+        get = lambda kind, c, t: kinds[kind][c, t]
+        pack_static(get, range(planes), rows, lines, parity, wanted)
+
+    pack_rows(lambda kind, c: kind > 0)
     pops = adj.shape[0]
     components = pops + 18
     slot = grid.lane // grid.group
     for g in range(own_left.shape[0]):
         if g * grid.pack % per_chunk == 0 and g * grid.pack < pops:
-            copies[4 + g * grid.pack // per_chunk].wait()
+            chunk = g * grid.pack // per_chunk
+            copies[4 + chunk].wait()
+            pack_rows(lambda kind, c: kind == 0 and c // per_chunk == chunk)
         left = right = jnp.zeros((rows, cols), F32)
         for j in range(grid.pack):
             c = g * grid.pack + j
@@ -665,8 +678,6 @@
         right = jnp.where(low, pltpu.roll(own_right[2 * h + 1], cols - HALO, 1), own_right[2 * h])
         send_c[h] = jnp.where(even, right, left)
         send_d[h] = jnp.where(even, left, right)
-    kinds = (adj, fl, fe)
-    pack_static(lambda kind, c, t: kinds[kind][c, t], range(planes), rows, lines, parity_of("gx"))
     lines_to(send_a, send_b, lines)
 
 

time: 24.8 us -> 24.7 us (level)
  no operation moved by 1% of the time
where the time goes in v11:
time: 24.7 us; the launch traced here: 24.6 us
  Pallas kernels  9.84 us (40%)
  starting transfers between devices  9.84 us (40%)
  waiting for transfers between devices  4.87 us (20%)
    ppermute x6, starting transfers between devices, swap(): return lax.ppermute(block, axis, route)  9.84 us
    pallas_call x5, Pallas kernels, call(): pl.pallas_call(kernel, out_shape=[jax.ShapeDtypeStruct(s, F32) for s in o...  9.84 us
    ppermute x6, waiting for transfers between devices, swap(): return lax.ppermute(block, axis, route)  4.87 us
  transfers between devices with their start and end apart: 6, of which 4 were waited for; matrix products, arithmetic and copies ran while one was open for 0% of the time, Pallas kernels for 16%

profile of v11, /device:TPU:0, one launch (start us, length us, event | category | flops | bytes accessed | tf_op | source)
XLA Modules:
  0.0 24.6 jit_solution(12301290757534772153)
XLA Ops:
  0.0 2.1 %shard_map.55 = (f32[10,8,128]{2,1,0:T(8,128)S(1)}, f32[10,8,128]{2,1,0:T(8,128)S(1)}, f32[20,8,128]{2,1,0:T(8,128)S(1)}, f32[20,8,128]{2,1,0:T(8,128)S(1)}, f32...) custom-call(f32[57,4,8,128]{3,2,1,0:T(8,128)} %adj_in.1, ...), custom_call_target="tpu_custom_call" | custom-call | tf_op jit(solution)/shard_map/pallas_call | solution.py:1018
  2.1 6.1 %collective-permute-start = (f32[352,128]{1,0:T(8,128)S(1)}, f32[352,128]{1,0:T(8,128)S(1)}, u32[]{:S(2)}, u32[]{:S(2)}) collective-permute-start(f32[352,128]{1,0:T(8,128)S(1)} %get-tuple-element.31), channel_id=1, source_target_pairs={{4,8},{8,4},{12,16},{16,12},{20,24},{24,20},{28,0},{0,28},{5,9},{9... | collective-permute-start | bytes 540680 | tf_op jit(solution)/shard_map/ppermute | solution.py:1035
  8.2 0.0 collective-permute-start.1
  8.2 0.7 %collective-permute-start.2 = (f32[10,8,128]{2,1,0:T(8,128)S(1)}, f32[10,8,128]{2,1,0:T(8,128)S(1)}, u32[]{:S(2)}, u32[]{:S(2)}) collective-permute-start(f32[10,8,128]{2,1,0:T(8,128)S(1)} %get-tuple-element.35), channel_id=1, source_target_pairs={{1,2},{2,1},{3,0},{0,3},{5,6},{6,5},{7,4},{4,7},{9,10},{10,9},{11,... | collective-permute-start | bytes 122888 | tf_op jit(solution)/shard_map/ppermute | solution.py:1035
  8.8 1.0 %collective-permute-start.3 = (f32[10,8,128]{2,1,0:T(8,128)S(1)}, f32[10,8,128]{2,1,0:T(8,128)S(1)}, u32[]{:S(2)}, u32[]{:S(2)}) collective-permute-start(f32[10,8,128]{2,1,0:T(8,128)S(1)} %get-tuple-element.36), channel_id=1, source_target_pairs={{0,1},{1,0},{2,3},{3,2},{4,5},{5,4},{6,7},{7,6},{8,9},{9,8},{10,11... | collective-permute-start | bytes 122888 | tf_op jit(solution)/shard_map/ppermute | solution.py:1035
  9.8 0.8 %shard_map.56.sides_main = f32[12,4,8,128]{3,2,1,0:T(8,128)S(1)} custom-call(f32[57,4,8,128]{3,2,1,0:T(8,128)S(1)} %get-tuple-element.29.adj, f32[12,4,8,128]{3,2,1,0:T(8,128)S(1)} %get-tuple-element.30.fl), custom_call_target="tpu_custom_call" | custom-call | flops 10000000 | bytes 10000000 | tf_op jit(solution)/shard_map/pallas_call | solution.py:1018
  10.6 1.4 %collective-permute-done.2.recv_c = f32[10,8,128]{2,1,0:T(8,128)S(1)} collective-permute-done((f32[10,8,128]{2,1,0:T(8,128)S(1)}, f32[10,8,128]{2,1,0:T(8,128)S(1)}, u32[]{:S(2)}, u32[]{:S(2)}) %collective-permute-start.2) | collective-permute-done | bytes 40992 | tf_op jit(solution)/shard_map/ppermute | solution.py:1035
  12.0 0.0 collective-permute-done.3.recv_d
  12.0 0.8 %shard_map.57 = (f32[152,128]{1,0:T(8,128)S(1)}, f32[152,128]{1,0:T(8,128)S(1)}, f32[57,8,128]{2,1,0:T(8,128)S(1)}, f32[12,8,128]{2,1,0:T(8,128)S(1)}, f32[12,8,128]{2,1,0:T(8,128)S(1)}) custom-call(f32[20,8,128]{2,1,0:T(8,128)S(1)} %get-tuple-element.33.own_left, f32[20,8,128]{2,1,0:T(8,128)S(1)} %get-tuple-element.34.own_right, ...), custom_call_target="tpu_custom_call" | custom-call | flops 100000000 | bytes 100000000 | tf_op jit(solution)/shard_map/pallas_call | solution.py:1018
  12.8 2.0 %collective-permute-start.4 = (f32[152,128]{1,0:T(8,128)S(1)}, f32[152,128]{1,0:T(8,128)S(1)}, u32[]{:S(2)}, u32[]{:S(2)}) collective-permute-start(f32[152,128]{1,0:T(8,128)S(1)} %get-tuple-element.49), channel_id=1, source_target_pairs={{4,8},{8,4},{12,16},{16,12},{20,24},{24,20},{28,0},{0,28},{5,9},{9... | collective-permute-start | bytes 233480 | tf_op jit(solution)/shard_map/ppermute | solution.py:1035
  14.8 0.2 collective-permute-start.5
  15.0 0.0 collective-permute-done.recv_a
  15.0 1.6 %collective-permute-done.1.recv_b = f32[352,128]{1,0:T(8,128)S(1)} collective-permute-done((f32[352,128]{1,0:T(8,128)S(1)}, f32[352,128]{1,0:T(8,128)S(1)}, u32[]{:S(2)}, u32[]{:S(2)}) %collective-permute-start.1) | collective-permute-done | bytes 180256 | tf_op jit(solution)/shard_map/ppermute | solution.py:1035
  16.6 2.4 %shard_map.58 = (f32[93,4,8,128]{3,2,1,0:T(8,128)S(1)}, f32[57,4,8,128]{3,2,1,0:T(8,128)S(1)}, f32[9,4,8,128]{3,2,1,0:T(8,128)S(1)}, f32[14,4,8,128]{3,2,1,0:T(8...) custom-call(f32[57,4,8,128]{3,2,1,0:T(8,128)S(1)} %get-tuple-element, ...), custom_call_target="tpu_custom_call" | custom-call | flops 100000000 | bytes 100000000 | tf_op jit(solution)/shard_map/pallas_call | solution.py:1018
  19.0 1.1 %collective-permute-done.4.recv_a = f32[152,128]{1,0:T(8,128)S(1)} collective-permute-done((f32[152,128]{1,0:T(8,128)S(1)}, f32[152,128]{1,0:T(8,128)S(1)}, u32[]{:S(2)}, u32[]{:S(2)}) %collective-permute-start.4) | collective-permute-done | bytes 77856 | tf_op jit(solution)/shard_map/ppermute | solution.py:1035
  20.1 0.7 %collective-permute-done.5.recv_b = f32[152,128]{1,0:T(8,128)S(1)} collective-permute-done((f32[152,128]{1,0:T(8,128)S(1)}, f32[152,128]{1,0:T(8,128)S(1)}, u32[]{:S(2)}, u32[]{:S(2)}) %collective-permute-start.5) | collective-permute-done | bytes 77856 | tf_op jit(solution)/shard_map/ppermute | solution.py:1035
  20.8 3.8 %shard_map.59 = f32[57,4,8,128]{3,2,1,0:T(8,128)} custom-call(f32[12,4,8,128]{3,2,1,0:T(8,128)S(1)} %get-tuple-element.28.fe.fe_m, f32[93,4,8,128]{3,2,1,0:T(8,128)S(1)} %get-tuple-element.38.rims_m, f32[57,4,8,128]{3,2,1,0:T(8,128)S(1)} %get-tuple-element.39.mid_m, f32[9,4,8,128]{3,2,1,0:T(8,128)S(1)} %get-tuple-element.40.part_m, ...), custom_call_target="tpu_custom_call" | custom-call | tf_op jit(solution)/shard_map/pallas_call | solution.py:1018
Async XLA Ops:
  2.1 12.9 %collective-permute-start = (f32[352,128]{1,0:T(8,128)S(1)}, f32[352,128]{1,0:T(8,128)S(1)}, u32[]{:S(2)}, u32[]{:S(2)}) collective-permute-start(f32[352,128]{1,0:T(8,128)S(1)} %get-tuple-element.31), channel_id=1, source_target_pairs={{4,8},{8,4},{12,16},{16,12},{20,24},{24,20},{28,0},{0,28},{5,9},{9... | collective-permute-start | bytes 540680 | tf_op jit(solution)/shard_map/ppermute | solution.py:1035
  8.2 8.4 %collective-permute-start.1 = (f32[352,128]{1,0:T(8,128)S(1)}, f32[352,128]{1,0:T(8,128)S(1)}, u32[]{:S(2)}, u32[]{:S(2)}) collective-permute-start(f32[352,128]{1,0:T(8,128)S(1)} %get-tuple-element.32), channel_id=1, source_target_pairs={{0,4},{4,0},{8,12},{12,8},{16,20},{20,16},{24,28},{28,24},{1,5},{5... | collective-permute-start | bytes 540680 | tf_op jit(solution)/shard_map/ppermute | solution.py:1035
  8.2 3.8 %collective-permute-start.2 = (f32[10,8,128]{2,1,0:T(8,128)S(1)}, f32[10,8,128]{2,1,0:T(8,128)S(1)}, u32[]{:S(2)}, u32[]{:S(2)}) collective-permute-start(f32[10,8,128]{2,1,0:T(8,128)S(1)} %get-tuple-element.35), channel_id=1, source_target_pairs={{1,2},{2,1},{3,0},{0,3},{5,6},{6,5},{7,4},{4,7},{9,10},{10,9},{11,... | collective-permute-start | bytes 122888 | tf_op jit(solution)/shard_map/ppermute | solution.py:1035
  8.8 3.2 %collective-permute-start.3 = (f32[10,8,128]{2,1,0:T(8,128)S(1)}, f32[10,8,128]{2,1,0:T(8,128)S(1)}, u32[]{:S(2)}, u32[]{:S(2)}) collective-permute-start(f32[10,8,128]{2,1,0:T(8,128)S(1)} %get-tuple-element.36), channel_id=1, source_target_pairs={{0,1},{1,0},{2,3},{3,2},{4,5},{5,4},{6,7},{7,6},{8,9},{9,8},{10,11... | collective-permute-start | bytes 122888 | tf_op jit(solution)/shard_map/ppermute | solution.py:1035
  12.8 7.3 %collective-permute-start.4 = (f32[152,128]{1,0:T(8,128)S(1)}, f32[152,128]{1,0:T(8,128)S(1)}, u32[]{:S(2)}, u32[]{:S(2)}) collective-permute-start(f32[152,128]{1,0:T(8,128)S(1)} %get-tuple-element.49), channel_id=1, source_target_pairs={{4,8},{8,4},{12,16},{16,12},{20,24},{24,20},{28,0},{0,28},{5,9},{9... | collective-permute-start | bytes 233480 | tf_op jit(solution)/shard_map/ppermute | solution.py:1035
  14.8 6.0 %collective-permute-start.5 = (f32[152,128]{1,0:T(8,128)S(1)}, f32[152,128]{1,0:T(8,128)S(1)}, u32[]{:S(2)}, u32[]{:S(2)}) collective-permute-start(f32[152,128]{1,0:T(8,128)S(1)} %get-tuple-element.50), channel_id=1, source_target_pairs={{0,4},{4,0},{8,12},{12,8},{16,20},{20,16},{24,28},{28,24},{1,5},{5... | collective-permute-start | bytes 233480 | tf_op jit(solution)/shard_map/ppermute | solution.py:1035
